TPU v7x, 32 devices: a whole 2x2x4 slice. The times are simulated.
32 devices in a mesh: lhs: 8 (over y, x, core), rhs: 4 (over z).
Axes of the slice: x: 2, y: 2, z: 4, core: 2. Of those that a mesh axis runs over, the one named last changes fastest.
Arguments:
- left_table: float32 [8, 4, 384, 400], P('lhs', 'rhs'), may hold values from -6 to 6
- left_state: float32 [8, 4, 384], P('lhs', 'rhs'), may hold values from 1e-06 to 0.0001
- right_table: float32 [8, 4, 384, 400], P('lhs', 'rhs'), may hold values from -6 to 6
- right_state: float32 [8, 4, 384], P('lhs', 'rhs'), may hold values from 1e-06 to 0.0001
- operators: float32 [2, 400, 400], replicated, may hold values from -0.3125 to 0.3125
- operator_state: float32 [2, 400], replicated, may hold values from 0.1 to 10
- sources: int32 [8, 4, 384], P('lhs', 'rhs'), may hold values from 0 to 383
- targets: int32 [8, 4, 384], P('lhs', 'rhs'), may hold values from 0 to 383
- relations: int32 [8, 4, 384], P('lhs', 'rhs'), may hold values from 0 to 1, as said below
- negatives: int32 [8, 4, 384], P('lhs', 'rhs'), may hold values from 0 to 383
- counts: int32 [8, 4], P('lhs', 'rhs'), may hold values from 1 to 384, 960 in all within a row
Outputs:
- new_left: float32 [8, 4, 384, 400], P('lhs', 'rhs')
- new_right: float32 [8, 4, 384, 400], P('lhs', 'rhs')
- new_operators: float32 [2, 400, 400], replicated
Inputs may be any that keep to these rules, and one draw needn't show every extreme that they name: For each index along lhs, the counts over rhs sum to 960, and at least one of them equals 384. `relations`: within each bucket the edge slots are grouped by relation: relation ids never fall from one slot to the next.
All inputs are finite; a program needn't handle non-finite values. No bound on the sum of `counts` on one device may be relied on, other than what follows from the above.
Results may differ from a plain program's by a relative error of at most 0.0003.
Values sent between devices are 32-bit elements; how exact they have to be, the bound alone decides.
No kernel may reach another device: no remote copies, remote signals or barrier semaphores. Data moves between devices by JAX's collectives and lax.ppermute only.
A program may use at most 64 MiB of HBM per device.

v0:
```python
import jax
import jax.numpy as jnp
from jax import lax
from jax.sharding import PartitionSpec as P


def from_behind(value, axis, steps):
    count = lax.axis_size(axis)
    pairs = [(source, (source + steps) % count) for source in range(count)]
    return lax.ppermute(value, axis, pairs)


def map_edges(inputs, operators, relations):
    edge_count, feat_width = inputs.shape
    block_len = min(128, edge_count)
    blocks = edge_count // block_len
    grouped = relations.reshape(blocks, block_len)
    firsts = grouped[:, 0]
    picked = operators[firsts]
    shaped = inputs.reshape(blocks, block_len, feat_width)
    mapped = jnp.einsum("nbw,nwv->nbv", shaped, picked, precision=lax.Precision.HIGHEST)
    split_at = jnp.sum((relations == 0).astype(jnp.int32))
    edge_block = jnp.minimum(split_at // block_len, blocks - 1)
    boundary = lax.dynamic_index_in_dim(shaped, edge_block, 0, keepdims=False)
    patched = jnp.dot(boundary, operators[operators.shape[0] - 1], precision=lax.Precision.HIGHEST)
    block_ids = jnp.arange(blocks, dtype=jnp.int32)
    needs_patch = (block_ids[:, None] == edge_block) & (grouped == 1)
    mapped = jnp.where(needs_patch[:, :, None], patched[None], mapped)
    return mapped.reshape(edge_count, feat_width)


def bucket_loss(
    left_block, right_block, operators, sources, targets, relations, negatives, live_count
):
    inputs = left_block[sources]
    mapped = map_edges(inputs, operators, relations)
    unit_mapped = mapped * lax.rsqrt(jnp.sum(mapped * mapped, -1, keepdims=True) + 1e-06)
    unit_right = right_block * lax.rsqrt(
        jnp.sum(right_block * right_block, -1, keepdims=True) + 1e-06
    )
    positive = jnp.sum(unit_mapped * unit_right[targets], -1)
    sampled = jnp.dot(unit_mapped, unit_right[negatives].T, precision=lax.Precision.HIGHEST)
    log_total = jnp.log(jnp.exp(positive) + jnp.sum(jnp.exp(sampled), -1))
    live_slot = jnp.arange(sources.shape[0], dtype=jnp.int32) < live_count
    return jnp.sum(jnp.where(live_slot, log_total - positive, jnp.zeros_like(log_total)))


def adagrad(weights, sums_in, gradient):
    summed = sums_in + jnp.mean(gradient * gradient, -1)
    return weights - 0.1 * gradient / jnp.sqrt(summed)[..., None]


def body(
    left_table,
    left_state,
    right_table,
    right_state,
    operators,
    operator_state,
    sources,
    targets,
    relations,
    negatives,
    counts,
):
    left_block, left_bstate = from_behind((left_table, left_state), "lhs", 1)
    right_block, right_bstate = from_behind((right_table, right_state), "rhs", 1)

    def local_loss(first, second, third):
        return bucket_loss(
            first,
            second,
            third,
            sources[0, 0],
            targets[0, 0],
            relations[0, 0],
            negatives[0, 0],
            counts[0, 0],
        )

    loss_value, pullback = jax.vjp(local_loss, left_block[0, 0], right_block[0, 0], operators)
    left_grad, right_grad, operator_grad = pullback(jnp.ones_like(loss_value))
    new_left = adagrad(left_block[0, 0], left_bstate[0, 0], left_grad)[None, None]
    new_right = adagrad(right_block[0, 0], right_bstate[0, 0], right_grad)[None, None]
    summed = lax.psum(operator_grad, ("lhs", "rhs"))
    new_operators = adagrad(operators, operator_state, summed)
    return (new_left, new_right, new_operators)


def solution(mesh):
    return jax.shard_map(
        body,
        mesh=mesh,
        in_specs=(
            P("lhs", "rhs", None, None),
            P("lhs", "rhs", None),
            P("lhs", "rhs", None, None),
            P("lhs", "rhs", None),
            P(),
            P(),
            P("lhs", "rhs", None),
            P("lhs", "rhs", None),
            P("lhs", "rhs", None),
            P("lhs", "rhs", None),
            P("lhs", "rhs"),
        ),
        out_specs=(P("lhs", "rhs", None, None), P("lhs", "rhs", None, None), P()),
        check_vma=False,
    )
```

profile of v0, /device:TPU:0, one launch (start us, length us, event | category | flops | bytes accessed | tf_op | source)
XLA Modules:
  0.0 232.7 jit_solution(14902514481122141323)
XLA Ops:
  7.2 0.0 all-reduce.3.cloned.1.call-start
  7.2 0.5 collective-permute-start.2
  7.7 2.6 %collective-permute-start.3 = (f32[1,1,384]{2,1,0:T(1,128)}, f32[1,1,384]{2,1,0:T(1,128)S(1)}, u32[]{:S(2)}, u32[]{:S(2)}) collective-permute-start(f32[1,1,384]{2,1,0:T(1,128)} %param.14), channel_id=1, source_target_pairs={{0,1},{1,2},{2,3},{3,0},{4,5},{5,6},{6,7},{7,4},{8,9},{9,10},{10,1... | collective-permute-start | bytes 4616 | tf_op jit(solution)/shard_map/ppermute | solution.py:10
  10.4 1.3 collective-permute-start
  11.6 1.6 collective-permute-start.1
  13.2 1.3 fusion.45
  15.8 0.7 fusion.43
  16.5 0.7 fusion.44
  18.5 0.1 copy.67
  18.7 0.7 fusion.42
  19.4 0.1 compare_and_fusion
  20.1 2.1 gather_fusion.1
  22.3 0.0 copy-start
  22.3 0.0 collective-permute-done.2
  22.3 0.0 collective-permute-done.3
  22.3 0.0 collective-permute-done
  22.3 1.8 copy.41
  24.1 2.2 gather_fusion
  26.4 3.0 %fusion.3 = f32[128,400]{0,1:T(8,128)S(1)} fusion(f32[2,400,400]{2,1,0:T(8,128)} %param.15, f32[3,128,400]{2,1,0:T(8,128)} %bitcast.117, s32[]{:T(128)S(6)} %select_n.62), kind=kOutput, calls=%fused_computation.20 | convolution fusion | flops 245760000 | bytes 1286148 | tf_op jit(solution)/shard_map/jvp()/dot_general | solution.py:25
  29.4 0.0 copy-done
  29.4 0.0 copy-done.4
  29.4 5.7 %multiply_reduce_fusion.4 = (f32[3,128]{1,0:T(4,128)S(1)}, f32[3,128,400]{1,2,0:T(8,128)}) fusion(f32[3,128,400]{2,1,0:T(8,128)S(1)} %bitcast.119, f32[3,400,400]{2,1,0:T(8,128)S(1)} %gather_fusion.1, f32[128,400]{0,1:T(8,128)S(1)} %fusion.3, pred[3,128]{1,0:T(4,128)(4,1)S(1)} %compare_and_fusion), kind=kOutput, calls=%fused_computation.44 | convolution fusion | flops 737740416 | bytes 3355520 | tf_op jit(solution)/shard_map/jvp(nbw,nwv->nbv)/dot_general | solution.py:21
  35.1 0.0 collective-permute-done.1
  35.1 1.3 copy.45
  36.5 0.1 fusion.5
  36.6 0.1 bitcast_multiply_fusion.2
  36.8 1.6 gather_fusion.3
  38.4 2.2 gather_fusion.2
  40.7 2.3 copy.49
  42.9 2.2 copy.47
  45.2 0.0 copy-done.2
  45.2 1.2 multiply_reduce_fusion.3
  46.3 1.5 fusion.51
  47.8 2.3 fusion.15
  50.1 0.0 copy-done.8
  50.1 1.6 fusion.11
  51.8 0.0 copy-start.1
  51.8 0.2 fusion.18
  51.9 1.5 copy-done.1
  53.5 3.0 %fusion.14 = f32[3,128,400]{1,2,0:T(8,128)} fusion(f32[3,400,400]{2,1,0:T(8,128)S(1)} %copy-done.1, f32[50,3,8,128]{3,2,1,0:T(8,128)S(1)} %get-tuple-element.15, pred[3,128]{1,0:T(4,128)(4,1)S(1)} %compare_and_fusion), kind=kOutput, calls=%fused_computation.46 | convolution fusion | flops 737433600 | bytes 3149184 | tf_op jit(solution)/shard_map/transpose(jvp(nbw,nwv->nbv))/dot_general | solution.py:21
  56.5 0.0 copy-done.5
  56.5 4.1 %fusion.13 = f32[3,400,400]{2,1,0:T(8,128)} fusion(f32[3,128,400]{2,1,0:T(8,128)S(1)} %bitcast.120, f32[50,3,8,128]{3,2,1,0:T(8,128)S(1)} %get-tuple-element.15, pred[3,128]{1,0:T(4,128)(4,1)S(1)} %compare_and_fusion), kind=kOutput, calls=%fused_computation.45 | convolution fusion | flops 737433600 | bytes 3149184 | tf_op jit(solution)/shard_map/transpose(jvp(nbw,nwv->nbv))/dot_general | solution.py:21
  60.7 1.1 copy.55
  61.8 3.8 %scatter_custom_fusion.1 = f32[384,400]{1,0:T(8,128)S(1)} fusion(s32[384]{0:T(512)S(1)} %fusion.44, f32[384,400]{1,0:T(8,128)} %fusion.15, f32[]{:T(128)} %constant.18.clone.1), kind=kCustom, calls=%fused_computation.57 | custom fusion | flops 153600 | bytes 614912 | tf_op jit(solution)/shard_map/transpose(jvp())/scatter-add | solution.py:42
  65.6 3.6 %scatter_custom_fusion.2 = f32[384,400]{1,0:T(8,128)S(1)} fusion(s32[384]{0:T(512)S(1)} %fusion.43, f32[384,400]{1,0:T(8,128)} %copy.55, f32[]{:T(128)} %constant.18.clone.1), kind=kCustom, calls=%fused_computation.55 | custom fusion | flops 153600 | bytes 614912 | tf_op jit(solution)/shard_map/transpose(jvp())/scatter-add | solution.py:41
  69.2 0.2 fusion.6
  69.4 0.3 multiply_reduce_fusion.1
  69.8 1.2 fusion.7
  71.0 2.3 %copy.58 = f32[1,1,384,400]{2,3,1,0:T(8,128)} copy(f32[1,1,384,400]{3,2,1,0:T(8,128)} %fusion.7) | data formatting | bytes 1228800
  73.3 2.8 %convolution_bitcast_fusion = f32[1,400,400]{2,1,0:T(8,128)} fusion(f32[128,400]{0,1:T(8,128)S(1)} %fusion.12, f32[3,128,400]{2,1,0:T(8,128)} %bitcast.118, s32[]{:T(128)S(6)} %select_n.62), kind=kOutput, calls=%fused_computation.10 | convolution fusion | flops 245760000 | bytes 1106948 | tf_op jit(solution)/shard_map/transpose(jvp())/dot_general | solution.py:25
  76.2 0.0 copy-done.3
  76.2 0.8 fusion.1
  77.0 1.1 copy.65
  78.1 3.6 %scatter_custom_fusion = f32[384,400]{1,0:T(8,128)S(1)} fusion(s32[384]{0:T(512)S(1)} %fusion.42, f32[384,400]{1,0:T(8,128)} %bitcast.122, f32[]{:T(128)} %constant.18.clone.1), kind=kCustom, calls=%fused_computation.59 | custom fusion | flops 153600 | bytes 614912 | tf_op jit(solution)/shard_map/transpose(jvp())/scatter-add | solution.py:35
  81.7 2.5 %pad.3 = f32[2,400,400]{2,1,0:T(8,128)} pad(f32[1,400,400]{2,1,0:T(8,128)} %convolution_bitcast_fusion, f32[]{:T(128)} %constant.18.clone.1), padding=1_0x0_0x0_0 | pad | bytes 1920004 | tf_op jit(solution)/shard_map/transpose(jvp())/pad | solution.py:25
  84.3 6.9 %scatter_fusion = f32[2,400,400]{2,1,0:T(8,128)} fusion(f32[2,400,400]{2,1,0:T(8,128)} %pad.3, s32[3]{0:T(128)S(1)} %fusion.48, f32[3,400,400]{2,1,0:T(8,128)} %fusion.13), kind=kCustom, calls=%fused_computation.7 | custom fusion | flops 480000 | bytes 5760012 | tf_op jit(solution)/shard_map/transpose(jvp())/scatter-add | solution.py:19
  91.2 0.0 all-reduce.3.cloned.1.call-update
  91.2 0.1 multiply_reduce_fusion.2
  91.4 1.1 subtract_bitcast_fusion
  92.5 2.2 copy.57
  94.7 127.8 %all-reduce.3.cloned.1.call-done = f32[2,400,400]{2,1,0:T(8,128)} async-done(((f32[2,400,400]{2,1,0:T(8,128)}), f32[2,400,400]{2,1,0:T(8,128)}) %all-reduce.3.cloned.1.call-update) | async-done | bytes 1280016 | tf_op jit(solution)/shard_map/psum | solution.py:85
  222.4 1.8 multiply_reduce_fusion
  224.2 0.1 copy-done.6
  224.3 1.5 divide_subtract_fusion
  (28 shorter events, 0.2 us)
Async XLA Ops:
  7.2 215.2 %all-reduce.3.cloned.1.call-start = ((), (), s32[]{:S(2)}) async-start(), calls=%async_computation | async-start | bytes 3276800 | tf_op jit(solution)/shard_map/psum | solution.py:85
  7.2 15.1 %collective-permute-start.2 = (f32[1,1,384]{2,1,0:T(1,128)}, f32[1,1,384]{2,1,0:T(1,128)S(1)}, u32[]{:S(2)}, u32[]{:S(2)}) collective-permute-start(f32[1,1,384]{2,1,0:T(1,128)} %param.12), channel_id=1, source_target_pairs={{0,4},{4,8},{8,12},{12,16},{16,20},{20,24},{24,28},{28,0},{1,5},{5... | collective-permute-start | bytes 4616 | tf_op jit(solution)/shard_map/ppermute | solution.py:10
  7.7 14.6 %collective-permute-start.3 = (f32[1,1,384]{2,1,0:T(1,128)}, f32[1,1,384]{2,1,0:T(1,128)S(1)}, u32[]{:S(2)}, u32[]{:S(2)}) collective-permute-start(f32[1,1,384]{2,1,0:T(1,128)} %param.14), channel_id=1, source_target_pairs={{0,1},{1,2},{2,3},{3,0},{4,5},{5,6},{6,7},{7,4},{8,9},{9,10},{10,1... | collective-permute-start | bytes 4616 | tf_op jit(solution)/shard_map/ppermute | solution.py:10
  10.4 12.0 %collective-permute-start = (f32[1,1,384,400]{2,3,1,0:T(8,128)}, f32[1,1,384,400]{2,3,1,0:T(8,128)}, u32[]{:S(2)}, u32[]{:S(2)}) collective-permute-start(f32[1,1,384,400]{2,3,1,0:T(8,128)} %param.11), channel_id=1, source_target_pairs={{0,4},{4,8},{8,12},{12,16},{16,20},{20,24},{24,28},{28,0},{1,5},{5... | collective-permute-start | bytes 1843208 | tf_op jit(solution)/shard_map/ppermute | solution.py:10
  11.6 23.5 %collective-permute-start.1 = (f32[1,1,384,400]{2,3,1,0:T(8,128)}, f32[1,1,384,400]{2,3,1,0:T(8,128)}, u32[]{:S(2)}, u32[]{:S(2)}) collective-permute-start(f32[1,1,384,400]{2,3,1,0:T(8,128)} %param.13), channel_id=1, source_target_pairs={{0,1},{1,2},{2,3},{3,0},{4,5},{5,6},{6,7},{7,4},{8,9},{9,10},{10,1... | collective-permute-start | bytes 1843208 | tf_op jit(solution)/shard_map/ppermute | solution.py:10
  22.3 7.2 %copy-start = (f32[3,400,400]{2,1,0:T(8,128)}, f32[3,400,400]{2,1,0:T(8,128)S(1)}, u32[]{:S(2)}) copy-start(f32[3,400,400]{2,1,0:T(8,128)S(1)} %gather_fusion.1) | copy-start | bytes 5760004
  26.4 3.0 %copy-start.4 = (f32[384,400]{1,0:T(8,128)S(1)}, f32[384,400]{1,0:T(8,128)}, u32[]{:S(2)}) copy-start(f32[384,400]{1,0:T(8,128)} %gather_fusion) | copy-start | bytes 1843204
  40.7 4.5 %copy-start.2 = (f32[3,128,400]{1,2,0:T(8,128)S(1)}, f32[3,128,400]{1,2,0:T(8,128)}, u32[]{:S(2)}) copy-start(f32[3,128,400]{1,2,0:T(8,128)} %get-tuple-element.19) | copy-start | bytes 1843204
  46.3 3.8 %copy-start.8 = (f32[384,400]{0,1:T(8,128)S(1)}, f32[384,400]{0,1:T(8,128)}, u32[]{:S(2)}) copy-start(f32[384,400]{0,1:T(8,128)} %copy.49) | copy-start | bytes 1843204
  51.8 1.7 copy-start.1
  53.4 3.1 %copy-start.5 = (f32[384,400]{1,0:T(8,128)S(1)}, f32[384,400]{1,0:T(8,128)}, u32[]{:S(2)}) copy-start(f32[384,400]{1,0:T(8,128)} %gather_fusion) | copy-start | bytes 1843204
  71.0 5.2 %copy-start.3 = (f32[2,400,400]{2,1,0:T(8,128)S(1)}, f32[2,400,400]{2,1,0:T(8,128)}, u32[]{:S(2)}) copy-start(f32[2,400,400]{2,1,0:T(8,128)} %param.15) | copy-start | bytes 3840004
  71.0 5.2 %copy-start.7 = (f32[3,128,400]{1,2,0:T(8,128)S(1)}, f32[3,128,400]{1,2,0:T(8,128)}, u32[]{:S(2)}) copy-start(f32[3,128,400]{1,2,0:T(8,128)} %fusion.14) | copy-start | bytes 1843204
  92.4 131.7 %copy-start.9 = (f32[2,400]{1,0:T(2,128)S(1)}, f32[2,400]{1,0:T(2,128)}, u32[]{:S(2)}) copy-start(f32[2,400]{1,0:T(2,128)} %param.16) | copy-start | bytes 9604
  222.4 1.9 copy-start.6
Sparse Core Ops, SparseCore 0:
  91.3 131.0 all-reduce.2
where the time goes:
time: 233 us
  waiting for transfers between devices  128 us (55%)
  other arithmetic  29.4 us (13%)
  local copies, waits for them, and re-layouts  27 us (12%)
  matrix products  24.9 us (11%)
  between operations  17.6 us (8%)
  starting transfers between devices  6.02 us (3%)
    psum x1, waiting for transfers between devices, body(): summed = lax.psum(operator_grad, ('lhs', 'rhs'))  128 us
    dot_general x3, matrix products, map_edges(): jnp.einsum('nbw,nwv->nbv', shaped, picked, precision=lax.Precision.HIGHEST)  12.8 us
    scatter-add x1, other arithmetic, map_edges(): picked = operators[firsts]  6.91 us
    gather x3, local copies, waits for them, and re-layouts, bucket_loss(): positive = jnp.sum(unit_mapped * unit_right[targets], -1)  6.74 us
    dot_general x3, matrix products, map_edges(): jnp.dot(boundary, operators[operators.shape[0] - 1], precision=lax.Precis...  6.66 us
    unnamed x23, local copies, waits for them, and re-layouts  6.31 us
    ppermute x4, starting transfers between devices, from_behind(): return lax.ppermute(value, axis, pairs)  5.98 us
    dot_general x3, matrix products, bucket_loss(): jnp.dot(unit_mapped, unit_right[negatives].T, precision=lax.Precision.HIG...  5.4 us
  transfers between devices with their start and end apart: 5, of which 1 were waited for; matrix products, arithmetic and copies ran while one was open for 9% of the time, Pallas kernels for 0%

commit v1 on v0

v1 whole, which is shorter than its diff:
```python
import functools

import jax
import jax.numpy as jnp
from jax import lax
from jax.experimental import pallas as pl
from jax.experimental.pallas import tpu as pltpu
from jax.sharding import PartitionSpec as P

F32 = jnp.float32
BF16 = jnp.bfloat16
LANES = 128
NN = ((1,), (0,))
NT = ((1,), (1,))
TN = ((0,), (0,))
EPS = 1e-06


def cut(x):
    high = x.astype(BF16)
    low = (x - high.astype(F32)).astype(BF16)
    return high, low


def mul(a, b, dims):
    return lax.dot_general(a, b, (dims, ((), ())), preferred_element_type=F32)


def mul3(a, b, dims):
    return mul(a[0], b[0], dims) + (mul(a[0], b[1], dims) + mul(a[1], b[0], dims))


def deep3(a, b, dims):
    (da,), (db,) = dims
    left = jnp.concatenate([a[0], a[0], a[1]], axis=da)
    right = jnp.concatenate([b[0], b[1], b[0]], axis=db)
    return mul(left, right, dims)


def one_hot(index_row, rows):
    shape = (rows, index_row.shape[1])
    return lax.broadcasted_iota(jnp.int32, shape, 0) == index_row


def prepare_kernel(
    count, src, tgt, neg, ops, op_sums,
    pick, weight, hit, live, column, ops_high, ops_low,
):
    rows, slots = pick.shape
    w = ops.shape[1]
    pick[...] = one_hot(src[...], rows).astype(BF16)
    target = jnp.transpose(one_hot(tgt[...], rows).astype(F32))
    sample = jnp.transpose(one_hot(neg[...], rows).astype(F32))
    alive = (lax.broadcasted_iota(jnp.int32, (slots, 1), 0) < count[0, 0]).astype(F32)
    weight[...] = target + jnp.sum(sample, axis=0, keepdims=True)
    hit[...] = target * alive
    live[...] = alive
    diagonal = one_hot(lax.broadcasted_iota(jnp.int32, (1, w), 1), w)
    for i in range(ops.shape[0]):
        column[i] = jnp.sum(jnp.where(diagonal, op_sums[i:i + 1, :], 0.0), axis=1, keepdims=True)
        high, low = cut(ops[i])
        ops_high[i] = high
        ops_low[i] = low


def left_kernel(after, left, ops_high, ops_low, pick, rel, x_high, x_low, unit, scale, turned_high, turned_low):
    high, low = cut(left[...])
    xh = mul(high, pick[...], NN).astype(BF16)
    xl = mul(low, pick[...], NN).astype(BF16)
    x_high[...] = xh
    x_low[...] = xl
    first = mul3((ops_high[0], ops_low[0]), (xh, xl), TN)
    second = mul3((ops_high[1], ops_low[1]), (xh, xl), TN)
    mapped = jnp.where(rel[...] == 0, first, second)
    inv = lax.rsqrt(jnp.sum(mapped * mapped, axis=0, keepdims=True) + EPS)
    u = mapped * inv
    unit[...] = u
    scale[...] = inv
    high, low = cut(jnp.transpose(u))
    turned_high[...] = high
    turned_low[...] = low


def operator_grad(which, relations, d_high, d_low, x, out):
    own = relations == which
    masked = [jnp.where(own, part.astype(F32), 0.0).astype(BF16) for part in (d_high, d_low)]
    grad = deep3(x, masked, NT)
    w = grad.shape[0]
    tiles, rest = w // LANES, w % LANES
    for t in range(tiles):
        out[pl.ds(t * w, w), :] = grad[:, t * LANES:(t + 1) * LANES]
    tail = jnp.transpose(grad[:, tiles * LANES:])
    base = tiles * w
    out[pl.ds(base, out.shape[0] - base), :] = jnp.zeros((out.shape[0] - base, LANES), F32)
    for t in range(-(-w // LANES)):
        width = min(LANES, w - t * LANES)
        out[pl.ds(base + t * rest, rest), 0:width] = tail[:, t * LANES:t * LANES + width]


def right_kernel(
    after, right, unit, scale, turned_high, turned_low, weight, hit, live, rel, x_high, x_low,
    send, d_high, d_low, p_high, p_low,
):
    r = right[...]
    split = cut(r)
    inv = lax.rsqrt(jnp.sum(r * r, axis=0, keepdims=True) + EPS)
    scores = mul3((turned_high[...], turned_low[...]), split, NN) * inv
    weighted = jnp.exp(scores) * weight[...]
    total = jnp.sum(weighted, axis=1, keepdims=True)
    push = weighted * (live[...] / total) - hit[...]
    p_high[...], p_low[...] = cut(push)
    du = deep3(split, cut(push * inv), NT)
    u = unit[...]
    along = jnp.sum(u * du, axis=0, keepdims=True)
    dh, dl = cut(scale[...] * (du - u * along))
    d_high[...] = dh
    d_low[...] = dl
    operator_grad(1 - core(), rel[...], dh, dl, (x_high[...], x_low[...]), send)


def keep_kernel(rel, d_high, d_low, x_high, x_low, keep):
    operator_grad(core(), rel[...], d_high[...], d_low[...], (x_high[...], x_low[...]), keep)


def adagrad_t(weights, sums, grad):
    summed = sums + jnp.sum(grad * grad, axis=0, keepdims=True) / grad.shape[0]
    return weights - grad * (0.1 / jnp.sqrt(summed))


def left_update_kernel(
    after, left, left_sum, ops_high, ops_low, pick, rel, d_high, d_low, new_left, done,
):
    d = (d_high[...], d_low[...])
    first = mul3((ops_high[0], ops_low[0]), d, NN)
    second = mul3((ops_high[1], ops_low[1]), d, NN)
    dx = cut(jnp.where(rel[...] == 0, first, second))
    grad = mul(dx[0], pick[...], NT) + mul(dx[1], pick[...], NT)
    new_left[...] = adagrad_t(left[...], left_sum[...], grad)
    done[...] = jnp.zeros_like(done)


def right_update_kernel(after, right, right_sum, unit, p_high, p_low, new_right, done):
    r = right[...]
    inv = lax.rsqrt(jnp.sum(r * r, axis=0, keepdims=True) + EPS)
    v = r * inv
    dv = deep3(cut(unit[...]), (p_high[...], p_low[...]), NN)
    grad = inv * (dv - v * jnp.sum(v * dv, axis=0, keepdims=True))
    new_right[...] = adagrad_t(r, right_sum[...], grad)
    done[...] = jnp.zeros_like(done)


def core():
    return lax.rem(lax.axis_index("lhs"), 2)


def chip():
    return lax.div(lax.axis_index("lhs"), 2)


def side():
    return lax.rem(lax.axis_index("rhs"), 2)


def deal_kernel(one, two, *outs):
    direct, distant = peers_of(one.shape[0])
    for half, own in enumerate((1 - side(), side())):
        own_outs = outs[half * (len(direct) + 1):]

        def part(j):
            spot = jnp.bitwise_xor(chip(), j)
            return one[spot, own] + two[spot, own]

        for j, out in zip(direct, own_outs):
            out[...] = part(j)
        for i, j in enumerate(distant):
            own_outs[len(direct)][i] = part(j)


def merge_kernel(one, two, *outs):
    for i, out in enumerate(outs):
        out[...] = one[i] + two[i]


def sum_kernel(*refs, after):
    refs = refs[after:]
    refs[-1][...] = functools.reduce(jnp.add, [ref[...] for ref in refs[:-1]])


def join_kernel(*refs):
    out = refs[-1]
    for j, ref in zip(walk_of(len(refs) - 1), refs):
        out[jnp.bitwise_xor(chip(), j)] = ref[...]


def copy_kernel(after, value, out):
    out[...] = value[...]


def operator_rows(which, ops, sums, near, far, flat, store):
    chunk = near.shape[1]
    for j in range(near.shape[0]):
        for own, ref in ((side(), near), (1 - side(), far)):
            flat[pl.ds(pl.multiple_of((2 * j + own) * chunk, 8), chunk), :] = ref[j]
    w = ops.shape[1]
    main = w // LANES
    rest = w - main * LANES
    tiles = [flat[pl.ds(t * w, w), :] for t in range(main)]
    tail = jnp.concatenate(
        [flat[pl.ds(main * w + t * rest, rest), :] for t in range(-(-w // LANES))], axis=1
    )
    tail = jnp.transpose(tail)[:w]
    square = jnp.sum(tail * tail, axis=1, keepdims=True)
    square = square + jnp.sum(sum(tile * tile for tile in tiles), axis=1, keepdims=True)
    rate = 0.1 / jnp.sqrt(sums[which] + square / w)
    for t, part in enumerate([*tiles, tail]):
        span = slice(t * LANES, min(w, (t + 1) * LANES))
        store(span, ops[which, :, span] - part * rate)


def own_operator_kernel(ops, sums, near, far, out, flat):
    def store(span, value):
        out[:, span] = value

    operator_rows(core(), ops, sums, near, far, flat, store)


def operator_kernel(own, ops, sums, near, far, out, flat, half, sem):
    first = pltpu.make_async_copy(own, out.at[core()], sem.at[0])
    first.start()

    def store(span, value):
        half[:, span] = value

    operator_rows(1 - core(), ops, sums, near, far, flat, store)
    second = pltpu.make_async_copy(half, out.at[1 - core()], sem.at[1])
    second.start()
    first.wait()
    second.wait()


def shaped(shape, dtype=F32):
    return jax.ShapeDtypeStruct(shape, dtype)


VMEM = pl.BlockSpec(memory_space=pltpu.VMEM)
ANY = pl.BlockSpec(memory_space=pl.ANY)
SMEM = pl.BlockSpec(memory_space=pltpu.SMEM)


def run(kernel, out_shape, scalars, *args, after=(), scratch=(), out_specs=None, flops=0, name=None):
    specs = [SMEM] * len(scalars) + [ANY] * len(after) + [VMEM] * len(args)
    return pl.pallas_call(
        kernel,
        out_shape=out_shape,
        in_specs=specs,
        out_specs=out_specs or jax.tree.map(lambda _: VMEM, out_shape),
        scratch_shapes=scratch,
        compiler_params=pltpu.CompilerParams(vmem_limit_bytes=24 * 2**20),
        cost_estimate=pl.CostEstimate(flops=flops, bytes_accessed=2**20, transcendentals=0),
        name=name,
    )(*scalars, *after, *args)


def around(value, axis, steps):
    count = lax.axis_size(axis)
    return lax.ppermute(value, axis, [(i, (i + steps) % count) for i in range(count)])


def swap(value, axis, bit):
    count = lax.axis_size(axis)
    return lax.ppermute(value, axis, [(i, i ^ bit) for i in range(count)])


def across_cores(value):
    return swap(value, "lhs", 1)


def peers_of(count):
    return [j for j in range(count) if j.bit_count() < 2], [j for j in range(count) if j.bit_count() > 1]


def walk_of(count):
    return [j ^ (j // 2) for j in range(count)]


def across_chips(value, j):
    return swap(value, "lhs", 2 * j)


def body(
    left_table, left_state, right_table, right_state, operators, operator_state,
    sources, targets, relations, negatives, counts,
):
    rows, w = left_table.shape[2:]
    slots = sources.shape[2]
    chips = lax.axis_size("lhs") // 2
    layers = lax.axis_size("rhs")
    unit_rows = 16 * chips
    used = w // LANES * w + (w % LANES) * -(-w // LANES)
    packed = -(-used // unit_rows) * unit_rows

    right = around(jnp.swapaxes(right_table[0, 0], 0, 1), "rhs", 1)
    left = around(jnp.swapaxes(left_table[0, 0], 0, 1), "lhs", 1)
    left_sum = around(left_state[0], "lhs", 1)
    right_sum = around(right_state[0], "rhs", 1)
    rel = relations[0]
    wide = shaped((w, slots), BF16)
    turned = shaped((slots, w), BF16)
    cross = shaped((slots, rows))
    halves = shaped(operators.shape, BF16)
    pick, weight, hit, live, column, ops_high, ops_low = run(
        prepare_kernel,
        [shaped((rows, slots), BF16), cross, cross, shaped((slots, 1)), shaped((*operator_state.shape, 1)),
         halves, halves],
        [counts], sources[0], targets[0], negatives[0], operators, operator_state, name="prepare",
    )
    x_high, x_low, unit, scale, turned_high, turned_low = run(
        left_kernel,
        [wide, wide, shaped((w, slots)), shaped((1, slots)), turned, turned],
        [], left, ops_high, ops_low, pick, rel, after=[left_sum], flops=2 * 10**9, name="left_side",
    )
    square = shaped((slots, rows), BF16)
    send, d_high, d_low, p_high, p_low = run(
        right_kernel,
        [shaped((packed, LANES)), wide, wide, square, square],
        [], right, unit, scale, turned_high, turned_low, weight, hit, live, rel, x_high, x_low,
        after=[right_sum], flops=3 * 10**9, name="right_side",
    )
    got = across_cores(send)
    keep = run(
        keep_kernel, shaped((packed, LANES)), [], rel, d_high, d_low, x_high, x_low,
        flops=10**9, name="own_relation",
    )

    part = shaped((packed // chips // 2, LANES))
    direct, distant = peers_of(chips)
    bundle = shaped((len(distant), *part.shape))
    dealt = run(
        deal_kernel, ([part] * len(direct) + [bundle]) * 2, [],
        *[t.reshape(chips, 2, *part.shape) for t in (keep, got)], name="sum_cores",
    )
    away, home = dealt[:len(direct)], dealt[len(direct) + 1:-1]
    merged = run(
        merge_kernel, [part] * len(distant), [], dealt[-1], swap(dealt[len(direct)], "rhs", 1), name="merge_layers",
    )
    away = [away[0]] + [across_chips(t, j) for j, t in zip(direct[1:], away[1:])]
    home = [home[0]] + [across_chips(t, j) for j, t in zip(direct[1:] + distant, home[1:] + merged)]
    passed = run(functools.partial(sum_kernel, after=0), part, [], *away, name="sum_away")
    done = shaped((8, LANES))
    new_left, done_left = run(
        left_update_kernel, [shaped((w, rows)), done],
        [], left, left_sum, ops_high, ops_low, pick, rel, d_high, d_low,
        after=[passed], flops=2 * 10**9, name="left_update",
    )
    mine = run(
        functools.partial(sum_kernel, after=1), part, [], *home, swap(passed, "rhs", 1),
        after=[done_left], name="sum_home",
    )
    new_right, done_right = run(
        right_update_kernel, [shaped((w, rows)), done],
        [], right, right_sum, unit, p_high, p_low,
        after=[mine], flops=10**9, name="right_update",
    )
    bit, after = 2, [done_right]
    while bit < layers:
        mine = run(
            functools.partial(sum_kernel, after=len(after)), part,
            [], mine, swap(mine, "rhs", bit), after=after, name="sum_layers",
        )
        bit, after = 2 * bit, []
    next_layer = swap(mine, "rhs", 1)

    def spread(value):
        taken = [value]
        for j in walk_of(chips)[1:]:
            taken.append(run(copy_kernel, part, [], across_chips(value, j), after=taken[-1:], name="take"))
        return taken

    joined = shaped((chips, *part.shape))
    near = run(join_kernel, joined, [], *spread(mine), name="join_near")
    far = run(join_kernel, joined, [], *spread(next_layer), name="join_far")
    other_near, other_far = across_cores(near), across_cores(far)
    flat = [pltpu.VMEM((packed, LANES), F32)]
    own = run(
        own_operator_kernel, shaped(operators.shape[1:]), [], operators, column, near, far,
        scratch=flat, name="own_operator",
    )
    new_operators = run(
        operator_kernel, shaped(operators.shape), [], own, operators, column, other_near, other_far,
        scratch=[*flat, pltpu.VMEM(operators.shape[1:], F32), pltpu.SemaphoreType.DMA((2,))],
        out_specs=ANY, name="operator_update",
    )
    return (
        jnp.swapaxes(new_left, 0, 1)[None, None],
        jnp.swapaxes(new_right, 0, 1)[None, None],
        new_operators,
    )


def solution(mesh):
    return jax.shard_map(
        body,
        mesh=mesh,
        in_specs=(
            P("lhs", "rhs", None, None),
            P("lhs", "rhs", None),
            P("lhs", "rhs", None, None),
            P("lhs", "rhs", None),
            P(),
            P(),
            P("lhs", "rhs", None),
            P("lhs", "rhs", None),
            P("lhs", "rhs", None),
            P("lhs", "rhs", None),
            P("lhs", "rhs"),
        ),
        out_specs=(P("lhs", "rhs", None, None), P("lhs", "rhs", None, None), P()),
        check_vma=False,
    )
```

time: 233 us -> 59.8 us (0.26)
  waiting for transfers between devices: 128 us -> 20.6 us
  other arithmetic: 29.4 us -> 0 us
  matrix products: 24.9 us -> 0 us
  local copies, waits for them, and re-layouts: 27 us -> 4.16 us
  between operations: 17.6 us -> 1.45 us
  starting transfers between devices: 6.02 us -> 20.2 us
  Pallas kernels: 0 us -> 13.1 us
    psum x1 -> x0, waiting for transfers between devices: 128 us -> none  [body(): summed = lax.psum(operator_grad, ('lhs', 'rhs'))]
    dot_general x9 -> x0, matrix products: 24.9 us -> none  [the longest x3 12.8 us: map_edges(): jnp.einsum('nbw,nwv->nbv', shaped, picked, precision=lax.Precision.HIGHEST)]
    ppermute x4 -> x22, waiting for transfers between devices: 0.01 us -> 20.6 us  [the longest x18 15.2 us: swap(): return lax.ppermute(value, axis, [(i, i ^ bit) for i in range(count)])]
    scatter-add x4 -> x0, other arithmetic: 18 us -> none  [the longest x1 6.91 us: map_edges(): picked = operators[firsts]]
    ppermute x4 -> x22, starting transfers between devices: 5.98 us -> 20.2 us  [the longest x18 14.3 us: swap(): return lax.ppermute(value, axis, [(i, i ^ bit) for i in range(count)])]
    pallas_call x0 -> x21, Pallas kernels: none -> 13.1 us  [run(): pl.pallas_call(kernel, out_shape=out_shape, in_specs=specs, out_specs=out...]
    gather x6 -> x0, local copies, waits for them, and re-layouts: 12.7 us -> none  [the longest x3 6.74 us: bucket_loss(): positive = jnp.sum(unit_mapped * unit_right[targets], -1)]
    reduce_sum x8 -> x0, other arithmetic: 5.11 us -> none  [the longest x3 2.26 us: adagrad(): summed = sums_in + jnp.mean(gradient * gradient, -1)]
  transfers between devices with their start and end apart: 5 -> 22, of which waited for: 1 -> 13; matrix products, arithmetic and copies ran while one was open for 9% -> 0% of each run, Pallas kernels for 0% -> 15%
where the time goes in v1:
time: 59.8 us; the launch traced here: 59.5 us
  waiting for transfers between devices  20.6 us (34%)
  starting transfers between devices  20.2 us (34%)
  Pallas kernels  13.1 us (22%)
  local copies, waits for them, and re-layouts  4.16 us (7%)
  between operations  1.45 us (2%)
    ppermute x18, waiting for transfers between devices, swap(): return lax.ppermute(value, axis, [(i, i ^ bit) for i in range(count)])  15.2 us
    ppermute x18, starting transfers between devices, swap(): return lax.ppermute(value, axis, [(i, i ^ bit) for i in range(count)])  14.3 us
    pallas_call x21, Pallas kernels, run(): pl.pallas_call(kernel, out_shape=out_shape, in_specs=specs, out_specs=out...  13.1 us
    ppermute x4, starting transfers between devices, around(): lax.ppermute(value, axis, [(i, (i + steps) % count) for i in range(count)])  5.98 us
    ppermute x4, waiting for transfers between devices, around(): lax.ppermute(value, axis, [(i, (i + steps) % count) for i in range(count)])  5.41 us
    unnamed x14, local copies, waits for them, and re-layouts  4.16 us
  transfers between devices with their start and end apart: 22, of which 13 were waited for; matrix products, arithmetic and copies ran while one was open for 0% of the time, Pallas kernels for 15%

profile of v1, /device:TPU:0, one launch (start us, length us, event | category | flops | bytes accessed | tf_op | source)
XLA Modules:
  0.0 59.5 jit_solution(17306883132097901985)
XLA Ops:
  0.6 0.0 copy-start.6
  0.6 0.5 collective-permute-start.3
  1.1 2.6 %collective-permute-start.1 = (f32[400,384]{1,0:T(8,128)}, f32[400,384]{1,0:T(8,128)S(1)}, u32[]{:S(2)}, u32[]{:S(2)}) collective-permute-start(f32[400,384]{1,0:T(8,128)} %bitcast.30), channel_id=1, source_target_pairs={{0,1},{1,2},{2,3},{3,0},{4,5},{5,6},{6,7},{7,4},{8,9},{9,10},{10,1... | collective-permute-start | bytes 1843208 | tf_op jit(solution)/shard_map/ppermute | solution.py:266
  3.8 1.3 %collective-permute-start.2 = (f32[1,384]{1,0:T(1,128)}, f32[1,384]{1,0:T(1,128)S(1)}, u32[]{:S(2)}, u32[]{:S(2)}) collective-permute-start(f32[1,384]{1,0:T(1,128)} %bitcast.31), channel_id=1, source_target_pairs={{0,4},{4,8},{8,12},{12,16},{16,20},{20,24},{24,28},{28,0},{1,5},{5... | collective-permute-start | bytes 4616 | tf_op jit(solution)/shard_map/ppermute | solution.py:266
  5.0 1.6 %collective-permute-start = (f32[1,384]{1,0:T(1,128)}, f32[1,384]{1,0:T(1,128)S(1)}, u32[]{:S(2)}, u32[]{:S(2)}) collective-permute-start(f32[1,384]{1,0:T(1,128)} %bitcast.32), channel_id=1, source_target_pairs={{0,1},{1,2},{2,3},{3,0},{4,5},{5,6},{6,7},{7,4},{8,9},{9,10},{10,1... | collective-permute-start | bytes 4616 | tf_op jit(solution)/shard_map/ppermute | solution.py:266
  7.3 0.0 copy-start
  7.3 1.4 %copy-done = f32[2,400,400]{2,1,0:T(8,128)S(1)} copy-done((f32[2,400,400]{2,1,0:T(8,128)S(1)}, f32[2,400,400]{2,1,0:T(8,128)}, u32[]{:S(2)}) %copy-start) | copy-done | bytes 1280024
  8.7 0.0 copy-start.2
  8.7 0.7 %copy-done.2 = f32[2,400]{1,0:T(2,128)S(1)} copy-done((f32[2,400]{1,0:T(2,128)S(1)}, f32[2,400]{1,0:T(2,128)}, u32[]{:S(2)}) %copy-start.2) | copy-done | bytes 3224
  9.4 0.0 copy-start.3
  9.4 0.7 %copy-done.3 = s32[1,1,384]{2,1,0:T(1,128)S(1)} copy-done((s32[1,1,384]{2,1,0:T(1,128)S(1)}, s32[1,1,384]{2,1,0:T(1,128)}, u32[]{:S(2)}) %copy-start.3) | copy-done | bytes 1560
  10.1 0.7 %copy-done.4 = s32[1,1,384]{2,1,0:T(1,128)S(1)} copy-done((s32[1,1,384]{2,1,0:T(1,128)S(1)}, s32[1,1,384]{2,1,0:T(1,128)}, u32[]{:S(2)}) %copy-start.4) | copy-done | bytes 1560
  10.8 0.7 %copy-done.5 = s32[1,1,384]{2,1,0:T(1,128)S(1)} copy-done((s32[1,1,384]{2,1,0:T(1,128)S(1)}, s32[1,1,384]{2,1,0:T(1,128)}, u32[]{:S(2)}) %copy-start.5) | copy-done | bytes 1560
  11.4 0.8 %prepare.1 = (bf16[384,384]{1,0:T(8,128)(2,1)S(1)}, f32[384,384]{1,0:T(8,128)S(1)}, f32[384,384]{1,0:T(8,128)S(1)}, f32[384,1]{1,0:T(8,128)S(1)}, f32[2,400,1]{2...) custom-call(s32[1,1]{1,0:T(1,128)S(6)} %copy.14.count, s32[1,384]{1,0:T(1,128)S(1)} %bitcast.22, ...), custom_call_target="tpu_custom_call" | custom-call | bytes 1048576 | tf_op jit(solution)/shard_map/prepare/pallas_call | solution.py:252
  12.3 0.0 collective-permute-done.2.after.left_sum
  12.3 0.0 collective-permute-done.3.left
  12.3 0.0 copy-done.6
  12.3 2.2 %left_side.1 = (bf16[400,384]{1,0:T(8,128)(2,1)S(1)}, bf16[400,384]{1,0:T(8,128)(2,1)S(1)}, f32[400,384]{1,0:T(8,128)S(1)}, f32[1,384]{1,0:T(1,128)S(1)}, bf16[3...) custom-call(f32[1,384]{1,0:T(1,128)S(1)} %collective-permute-done.2.after.left_sum, ...), custom_call_target="tpu_custom_call" | custom-call | flops 2000000000 | bytes 1048576 | tf_op jit(solution)/shard_map/left_side/pallas_call | solution.py:252
  14.5 5.4 %collective-permute-done.after.right_sum = f32[1,384]{1,0:T(1,128)S(1)} collective-permute-done((f32[1,384]{1,0:T(1,128)}, f32[1,384]{1,0:T(1,128)S(1)}, u32[]{:S(2)}, u32[]{:S(2)}) %collective-permute-start) | collective-permute-done | bytes 1568 | tf_op jit(solution)/shard_map/ppermute | solution.py:266
  19.9 0.0 collective-permute-done.1.right
  19.9 2.6 %right_side.1 = (f32[1280,128]{1,0:T(8,128)S(1)}, bf16[400,384]{1,0:T(8,128)(2,1)S(1)}, bf16[400,384]{1,0:T(8,128)(2,1)S(1)}, bf16[384,384]{1,0:T(8,128)(2,1)S(1)}, bf16[384,384]{1,0:T(8,128)(2,1)S(1)}) custom-call(f32[1,384]{1,0:T(1,128)S(1)} %collective-permute-done.after.right_sum, f32[400,384]{1,0:T(8,128)S(1)} %collective-permute-done.1.right, ...), custom_call_target="tpu_custom_call" | custom-call | flops 3000000000 | bytes 1048576 | tf_op jit(solution)/shard_map/right_side/pallas_call | solution.py:252
  22.5 0.7 %collective-permute-start.4 = (f32[1280,128]{1,0:T(8,128)S(1)}, f32[1280,128]{1,0:T(8,128)S(1)}, u32[]{:S(2)}, u32[]{:S(2)}) collective-permute-start(f32[1280,128]{1,0:T(8,128)S(1)} %get-tuple-element.47), channel_id=1, source_target_pairs={{0,4},{4,0},{8,12},{12,8},{16,20},{20,16},{24,28},{28,24},{1,5},{5... | collective-permute-start | bytes 1966088 | tf_op jit(solution)/shard_map/ppermute | solution.py:271
  23.2 0.8 %own_relation.1 = f32[1280,128]{1,0:T(8,128)S(1)} custom-call(s32[1,384]{1,0:T(1,128)S(1)} %bitcast.27, bf16[400,384]{1,0:T(8,128)(2,1)S(1)} %get-tuple-element.45.d_high, bf16[400,384]{1,0:T(8,128)(2,1)S(1)} %get-tuple-element.46.d_low, bf16[400,384]{1,0:T(8,128)(2,1)S(1)} %get-tuple-element.43.x_high, bf16[400,384]{1,0:T(8,128)(2,1)S(1)} %get-tuple-element.44.x_low), custom_call_target="tpu_custom_call" | custom-call | flops 1000000000 | bytes 1048576 | tf_op jit(solution)/shard_map/own_relation/pallas_call | solution.py:252
  24.0 1.0 %collective-permute-done.4 = f32[1280,128]{1,0:T(8,128)S(1)} collective-permute-done((f32[1280,128]{1,0:T(8,128)S(1)}, f32[1280,128]{1,0:T(8,128)S(1)}, u32[]{:S(2)}, u32[]{:S(2)}) %collective-permute-start.4) | collective-permute-done | bytes 655392 | tf_op jit(solution)/shard_map/ppermute | solution.py:271
  24.9 0.1 sum_cores.1
  25.0 1.8 %collective-permute-start.5 = (f32[160,128]{1,0:T(8,128)S(1)}, f32[160,128]{1,0:T(8,128)S(1)}, u32[]{:S(2)}, u32[]{:S(2)}) collective-permute-start(f32[160,128]{1,0:T(8,128)S(1)} %get-tuple-element.49), channel_id=1, source_target_pairs={{0,8},{4,12},{8,0},{12,4},{16,24},{20,28},{24,16},{28,20},{1,9},{5... | collective-permute-start | bytes 245768 | tf_op jit(solution)/shard_map/ppermute | solution.py:271
  26.8 1.7 %collective-permute-start.6 = (f32[160,128]{1,0:T(8,128)S(1)}, f32[160,128]{1,0:T(8,128)S(1)}, u32[]{:S(2)}, u32[]{:S(2)}) collective-permute-start(f32[160,128]{1,0:T(8,128)S(1)} %get-tuple-element.50), channel_id=1, source_target_pairs={{0,16},{4,20},{8,24},{12,28},{16,0},{20,4},{24,8},{28,12},{1,17},{... | collective-permute-start | bytes 245768 | tf_op jit(solution)/shard_map/ppermute | solution.py:271
  28.5 0.0 collective-permute-start.9
  28.5 0.4 collective-permute-start.7
  28.8 0.3 collective-permute-start.8
  29.1 0.7 %collective-permute-done.5.refs_1_ = f32[160,128]{1,0:T(8,128)S(1)} collective-permute-done((f32[160,128]{1,0:T(8,128)S(1)}, f32[160,128]{1,0:T(8,128)S(1)}, u32[]{:S(2)}, u32[]{:S(2)}) %collective-permute-start.5) | collective-permute-done | bytes 81952 | tf_op jit(solution)/shard_map/ppermute | solution.py:271
  29.8 1.8 %collective-permute-done.6.refs_2_ = f32[160,128]{1,0:T(8,128)S(1)} collective-permute-done((f32[160,128]{1,0:T(8,128)S(1)}, f32[160,128]{1,0:T(8,128)S(1)}, u32[]{:S(2)}, u32[]{:S(2)}) %collective-permute-start.6) | collective-permute-done | bytes 81952 | tf_op jit(solution)/shard_map/ppermute | solution.py:271
  31.6 0.1 collective-permute-start.11
  31.6 1.3 %collective-permute-done.9.two = f32[1,160,128]{2,1,0:T(8,128)S(1)} collective-permute-done((f32[1,160,128]{2,1,0:T(8,128)S(1)}, f32[1,160,128]{2,1,0:T(8,128)S(1)}, u32[]{:S(2)}, u32[]{:S(2)}) %collective-permute-start.9) | collective-permute-done | bytes 81952 | tf_op jit(solution)/shard_map/ppermute | solution.py:271
  33.0 1.1 %collective-permute-start.10 = (f32[160,128]{1,0:T(8,128)S(1)}, f32[160,128]{1,0:T(8,128)S(1)}, u32[]{:S(2)}, u32[]{:S(2)}) collective-permute-start(f32[160,128]{1,0:T(8,128)S(1)} %merge_layers.1), channel_id=1, source_target_pairs={{0,24},{4,28},{8,16},{12,20},{16,8},{20,12},{24,0},{28,4},{1,25},{... | collective-permute-start | bytes 245768 | tf_op jit(solution)/shard_map/ppermute | solution.py:271
  34.1 2.8 %left_update.1 = (f32[400,384]{1,0:T(8,128)}, f32[8,128]{1,0:T(8,128)S(1)}) custom-call(f32[160,128]{1,0:T(8,128)S(1)} %sum_away.1.after, f32[400,384]{1,0:T(8,128)S(1)} %collective-permute-done.3.left, f32[1,384]{1,0:T(1,128)S(1)} %collective-permute-done.2.after.left_sum, bf16[2,400,400]{2,1,0:T(8,128)(2,1)S(1)} %get-tuple-element.33.ops_high, ...), custom_call_target="tpu_custom_call" | custom-call | flops 2000000000 | bytes 1048576 | tf_op jit(solution)/shard_map/left_update/pallas_call | solution.py:252
  37.0 0.0 collective-permute-done.7.refs_2_
  37.0 0.0 collective-permute-done.8.refs_3_
  37.0 0.0 collective-permute-done.11.refs_5_
  37.0 1.4 %collective-permute-done.10.refs_4_ = f32[160,128]{1,0:T(8,128)S(1)} collective-permute-done((f32[160,128]{1,0:T(8,128)S(1)}, f32[160,128]{1,0:T(8,128)S(1)}, u32[]{:S(2)}, u32[]{:S(2)}) %collective-permute-start.10) | collective-permute-done | bytes 81952 | tf_op jit(solution)/shard_map/ppermute | solution.py:271
  38.4 0.9 %collective-permute-start.12 = (f32[160,128]{1,0:T(8,128)S(1)}, f32[160,128]{1,0:T(8,128)S(1)}, u32[]{:S(2)}, u32[]{:S(2)}) collective-permute-start(f32[160,128]{1,0:T(8,128)S(1)} %sum_home.1.after.refs_1_), channel_id=1, source_target_pairs={{0,2},{1,3},{2,0},{3,1},{4,6},{5,7},{6,4},{7,5},{8,10},{9,11},{10,... | collective-permute-start | bytes 245768 | tf_op jit(solution)/shard_map/ppermute | solution.py:271
  39.3 1.8 %right_update.1 = (f32[400,384]{1,0:T(8,128)}, f32[8,128]{1,0:T(8,128)S(1)}) custom-call(f32[160,128]{1,0:T(8,128)S(1)} %sum_home.1.after.refs_1_, f32[400,384]{1,0:T(8,128)S(1)} %collective-permute-done.1.right, f32[1,384]{1,0:T(1,128)S(1)} %collective-permute-done.after.right_sum, f32[400,384]{1,0:T(8,128)S(1)} %get-tuple-element.36.unit, ...), custom_call_target="tpu_custom_call" | custom-call | flops 1000000000 | bytes 1048576 | tf_op jit(solution)/shard_map/right_update/pallas_call | solution.py:252
  41.1 3.7 %collective-permute-done.12.refs_2_ = f32[160,128]{1,0:T(8,128)S(1)} collective-permute-done((f32[160,128]{1,0:T(8,128)S(1)}, f32[160,128]{1,0:T(8,128)S(1)}, u32[]{:S(2)}, u32[]{:S(2)}) %collective-permute-start.12) | collective-permute-done | bytes 81952 | tf_op jit(solution)/shard_map/ppermute | solution.py:271
  44.8 0.1 collective-permute-start.16
  45.0 1.1 %collective-permute-start.13 = (f32[160,128]{1,0:T(8,128)S(1)}, f32[160,128]{1,0:T(8,128)S(1)}, u32[]{:S(2)}, u32[]{:S(2)}) collective-permute-start(f32[160,128]{1,0:T(8,128)S(1)} %sum_layers.1.after.refs_0_), channel_id=1, source_target_pairs={{0,8},{4,12},{8,0},{12,4},{16,24},{20,28},{24,16},{28,20},{1,9},{5... | collective-permute-start | bytes 245768 | tf_op jit(solution)/shard_map/ppermute | solution.py:271
  46.1 2.4 %collective-permute-start.14 = (f32[160,128]{1,0:T(8,128)S(1)}, f32[160,128]{1,0:T(8,128)S(1)}, u32[]{:S(2)}, u32[]{:S(2)}) collective-permute-start(f32[160,128]{1,0:T(8,128)S(1)} %sum_layers.1.after.refs_0_), channel_id=1, source_target_pairs={{0,24},{4,28},{8,16},{12,20},{16,8},{20,12},{24,0},{28,4},{1,25},{... | collective-permute-start | bytes 245768 | tf_op jit(solution)/shard_map/ppermute | solution.py:271
  48.5 0.0 collective-permute-start.15
  48.5 0.8 %collective-permute-done.16.after.refs_0_ = f32[160,128]{1,0:T(8,128)S(1)} collective-permute-done((f32[160,128]{1,0:T(8,128)S(1)}, f32[160,128]{1,0:T(8,128)S(1)}, u32[]{:S(2)}, u32[]{:S(2)}) %collective-permute-start.16) | collective-permute-done | bytes 81952 | tf_op jit(solution)/shard_map/ppermute | solution.py:271
  49.3 0.3 collective-permute-start.17
  49.6 2.4 %collective-permute-start.18 = (f32[160,128]{1,0:T(8,128)S(1)}, f32[160,128]{1,0:T(8,128)S(1)}, u32[]{:S(2)}, u32[]{:S(2)}) collective-permute-start(f32[160,128]{1,0:T(8,128)S(1)} %collective-permute-done.16.after.refs_0_), channel_id=1, source_target_pairs={{0,24},{4,28},{8,16},{12,20},{16,8},{20,12},{24,0},{28,4},{1,25},{... | collective-permute-start | bytes 245768 | tf_op jit(solution)/shard_map/ppermute | solution.py:271
  52.0 0.0 collective-permute-done.13.value
  52.0 0.8 %collective-permute-start.19 = (f32[160,128]{1,0:T(8,128)S(1)}, f32[160,128]{1,0:T(8,128)S(1)}, u32[]{:S(2)}, u32[]{:S(2)}) collective-permute-start(f32[160,128]{1,0:T(8,128)S(1)} %collective-permute-done.16.after.refs_0_), channel_id=1, source_target_pairs={{0,16},{4,20},{8,24},{12,28},{16,0},{20,4},{24,8},{28,12},{1,17},{... | collective-permute-start | bytes 245768 | tf_op jit(solution)/shard_map/ppermute | solution.py:271
  52.8 0.0 collective-permute-done.14.value
  52.9 0.1 collective-permute-done.15.value
  53.0 0.1 collective-permute-start.20
  53.1 0.7 %collective-permute-done.17.value = f32[160,128]{1,0:T(8,128)S(1)} collective-permute-done((f32[160,128]{1,0:T(8,128)S(1)}, f32[160,128]{1,0:T(8,128)S(1)}, u32[]{:S(2)}, u32[]{:S(2)}) %collective-permute-start.17) | collective-permute-done | bytes 81952 | tf_op jit(solution)/shard_map/ppermute | solution.py:271
  53.8 1.5 %collective-permute-done.18.value = f32[160,128]{1,0:T(8,128)S(1)} collective-permute-done((f32[160,128]{1,0:T(8,128)S(1)}, f32[160,128]{1,0:T(8,128)S(1)}, u32[]{:S(2)}, u32[]{:S(2)}) %collective-permute-start.18) | collective-permute-done | bytes 81952 | tf_op jit(solution)/shard_map/ppermute | solution.py:271
  55.3 1.1 %collective-permute-done.19.value = f32[160,128]{1,0:T(8,128)S(1)} collective-permute-done((f32[160,128]{1,0:T(8,128)S(1)}, f32[160,128]{1,0:T(8,128)S(1)}, u32[]{:S(2)}, u32[]{:S(2)}) %collective-permute-start.19) | collective-permute-done | bytes 81952 | tf_op jit(solution)/shard_map/ppermute | solution.py:271
  56.5 0.1 collective-permute-start.21
  56.6 0.0 copy-done.1
  56.6 0.4 own_operator.1.own
  57.0 0.0 collective-permute-done.20.near
  57.0 1.1 %collective-permute-done.21.far = f32[4,160,128]{2,1,0:T(8,128)S(1)} collective-permute-done((f32[4,160,128]{2,1,0:T(8,128)S(1)}, f32[4,160,128]{2,1,0:T(8,128)S(1)}, u32[]{:S(2)}, u32[]{:S(2)}) %collective-permute-start.21) | collective-permute-done | bytes 327712 | tf_op jit(solution)/shard_map/ppermute | solution.py:271
  58.2 1.4 %operator_update.1 = f32[2,400,400]{2,1,0:T(8,128)} custom-call(f32[400,400]{1,0:T(8,128)S(1)} %own_operator.1.own, f32[2,400,400]{2,1,0:T(8,128)S(1)} %copy-done.1, f32[2,400,1]{2,1,0:T(8,128)S(1)} %get-tuple-element.61.sums, f32[4,160,128]{2,1,0:T(8,128)S(1)} %collective-permute-done.20.near, f32[4,160,128]{2,1,0:T(8,128)S(1)} %collective-permute-done.21.far), custom_call_target="tpu_custom_call" | custom-call | bytes 1048576 | tf_op jit(solution)/shard_map/operator_update/pallas_call | solution.py:252
  (15 shorter events, 0.2 us)
Async XLA Ops:
  0.6 11.7 %copy-start.6 = (s32[1,1,384]{2,1,0:T(1,128)S(1)}, s32[1,1,384]{2,1,0:T(1,128)}, u32[]{:S(2)}) copy-start(s32[1,1,384]{2,1,0:T(1,128)} %param.19) | copy-start | bytes 4612
  0.6 11.7 %collective-permute-start.3 = (f32[400,384]{1,0:T(8,128)}, f32[400,384]{1,0:T(8,128)S(1)}, u32[]{:S(2)}, u32[]{:S(2)}) collective-permute-start(f32[400,384]{1,0:T(8,128)} %bitcast.29), channel_id=1, source_target_pairs={{0,4},{4,8},{8,12},{12,16},{16,20},{20,24},{24,28},{28,0},{1,5},{5... | collective-permute-start | bytes 1843208 | tf_op jit(solution)/shard_map/ppermute | solution.py:266
  1.1 18.8 %collective-permute-start.1 = (f32[400,384]{1,0:T(8,128)}, f32[400,384]{1,0:T(8,128)S(1)}, u32[]{:S(2)}, u32[]{:S(2)}) collective-permute-start(f32[400,384]{1,0:T(8,128)} %bitcast.30), channel_id=1, source_target_pairs={{0,1},{1,2},{2,3},{3,0},{4,5},{5,6},{6,7},{7,4},{8,9},{9,10},{10,1... | collective-permute-start | bytes 1843208 | tf_op jit(solution)/shard_map/ppermute | solution.py:266
  3.8 8.5 %collective-permute-start.2 = (f32[1,384]{1,0:T(1,128)}, f32[1,384]{1,0:T(1,128)S(1)}, u32[]{:S(2)}, u32[]{:S(2)}) collective-permute-start(f32[1,384]{1,0:T(1,128)} %bitcast.31), channel_id=1, source_target_pairs={{0,4},{4,8},{8,12},{12,16},{16,20},{20,24},{24,28},{28,0},{1,5},{5... | collective-permute-start | bytes 4616 | tf_op jit(solution)/shard_map/ppermute | solution.py:266
  5.0 14.9 %collective-permute-start = (f32[1,384]{1,0:T(1,128)}, f32[1,384]{1,0:T(1,128)S(1)}, u32[]{:S(2)}, u32[]{:S(2)}) collective-permute-start(f32[1,384]{1,0:T(1,128)} %bitcast.32), channel_id=1, source_target_pairs={{0,1},{1,2},{2,3},{3,0},{4,5},{5,6},{6,7},{7,4},{8,9},{9,10},{10,1... | collective-permute-start | bytes 4616 | tf_op jit(solution)/shard_map/ppermute | solution.py:266
  7.3 1.4 %copy-start = (f32[2,400,400]{2,1,0:T(8,128)S(1)}, f32[2,400,400]{2,1,0:T(8,128)}, u32[]{:S(2)}) copy-start(f32[2,400,400]{2,1,0:T(8,128)} %ops.5) | copy-start | bytes 3840004
  8.7 0.7 %copy-start.2 = (f32[2,400]{1,0:T(2,128)S(1)}, f32[2,400]{1,0:T(2,128)}, u32[]{:S(2)}) copy-start(f32[2,400]{1,0:T(2,128)} %op_sums.1) | copy-start | bytes 9604
  9.4 0.7 %copy-start.3 = (s32[1,1,384]{2,1,0:T(1,128)S(1)}, s32[1,1,384]{2,1,0:T(1,128)}, u32[]{:S(2)}) copy-start(s32[1,1,384]{2,1,0:T(1,128)} %param.17) | copy-start | bytes 4612
  10.1 0.7 %copy-start.4 = (s32[1,1,384]{2,1,0:T(1,128)S(1)}, s32[1,1,384]{2,1,0:T(1,128)}, u32[]{:S(2)}) copy-start(s32[1,1,384]{2,1,0:T(1,128)} %param.18) | copy-start | bytes 4612
  10.8 0.7 %copy-start.5 = (s32[1,1,384]{2,1,0:T(1,128)S(1)}, s32[1,1,384]{2,1,0:T(1,128)}, u32[]{:S(2)}) copy-start(s32[1,1,384]{2,1,0:T(1,128)} %param.20) | copy-start | bytes 4612
  22.5 2.4 %collective-permute-start.4 = (f32[1280,128]{1,0:T(8,128)S(1)}, f32[1280,128]{1,0:T(8,128)S(1)}, u32[]{:S(2)}, u32[]{:S(2)}) collective-permute-start(f32[1280,128]{1,0:T(8,128)S(1)} %get-tuple-element.47), channel_id=1, source_target_pairs={{0,4},{4,0},{8,12},{12,8},{16,20},{20,16},{24,28},{28,24},{1,5},{5... | collective-permute-start | bytes 1966088 | tf_op jit(solution)/shard_map/ppermute | solution.py:271
  25.0 4.8 %collective-permute-start.5 = (f32[160,128]{1,0:T(8,128)S(1)}, f32[160,128]{1,0:T(8,128)S(1)}, u32[]{:S(2)}, u32[]{:S(2)}) collective-permute-start(f32[160,128]{1,0:T(8,128)S(1)} %get-tuple-element.49), channel_id=1, source_target_pairs={{0,8},{4,12},{8,0},{12,4},{16,24},{20,28},{24,16},{28,20},{1,9},{5... | collective-permute-start | bytes 245768 | tf_op jit(solution)/shard_map/ppermute | solution.py:271
  26.8 4.8 %collective-permute-start.6 = (f32[160,128]{1,0:T(8,128)S(1)}, f32[160,128]{1,0:T(8,128)S(1)}, u32[]{:S(2)}, u32[]{:S(2)}) collective-permute-start(f32[160,128]{1,0:T(8,128)S(1)} %get-tuple-element.50), channel_id=1, source_target_pairs={{0,16},{4,20},{8,24},{12,28},{16,0},{20,4},{24,8},{28,12},{1,17},{... | collective-permute-start | bytes 245768 | tf_op jit(solution)/shard_map/ppermute | solution.py:271
  28.5 4.5 %collective-permute-start.9 = (f32[1,160,128]{2,1,0:T(8,128)S(1)}, f32[1,160,128]{2,1,0:T(8,128)S(1)}, u32[]{:S(2)}, u32[]{:S(2)}) collective-permute-start(f32[1,160,128]{2,1,0:T(8,128)S(1)} %get-tuple-element.57), channel_id=1, source_target_pairs={{0,1},{1,0},{2,3},{3,2},{4,5},{5,4},{6,7},{7,6},{8,9},{9,8},{10,11... | collective-permute-start | bytes 245768 | tf_op jit(solution)/shard_map/ppermute | solution.py:271
  28.5 8.5 %collective-permute-start.7 = (f32[160,128]{1,0:T(8,128)S(1)}, f32[160,128]{1,0:T(8,128)S(1)}, u32[]{:S(2)}, u32[]{:S(2)}) collective-permute-start(f32[160,128]{1,0:T(8,128)S(1)} %get-tuple-element.54), channel_id=1, source_target_pairs={{0,8},{4,12},{8,0},{12,4},{16,24},{20,28},{24,16},{28,20},{1,9},{5... | collective-permute-start | bytes 245768 | tf_op jit(solution)/shard_map/ppermute | solution.py:271
  28.8 8.2 %collective-permute-start.8 = (f32[160,128]{1,0:T(8,128)S(1)}, f32[160,128]{1,0:T(8,128)S(1)}, u32[]{:S(2)}, u32[]{:S(2)}) collective-permute-start(f32[160,128]{1,0:T(8,128)S(1)} %get-tuple-element.55), channel_id=1, source_target_pairs={{0,16},{4,20},{8,24},{12,28},{16,0},{20,4},{24,8},{28,12},{1,17},{... | collective-permute-start | bytes 245768 | tf_op jit(solution)/shard_map/ppermute | solution.py:271
  31.6 5.4 %collective-permute-start.11 = (f32[160,128]{1,0:T(8,128)S(1)}, f32[160,128]{1,0:T(8,128)S(1)}, u32[]{:S(2)}, u32[]{:S(2)}) collective-permute-start(f32[160,128]{1,0:T(8,128)S(1)} %sum_away.1.after), channel_id=1, source_target_pairs={{0,1},{1,0},{2,3},{3,2},{4,5},{5,4},{6,7},{7,6},{8,9},{9,8},{10,11... | collective-permute-start | bytes 245768 | tf_op jit(solution)/shard_map/ppermute | solution.py:271
  33.0 5.4 %collective-permute-start.10 = (f32[160,128]{1,0:T(8,128)S(1)}, f32[160,128]{1,0:T(8,128)S(1)}, u32[]{:S(2)}, u32[]{:S(2)}) collective-permute-start(f32[160,128]{1,0:T(8,128)S(1)} %merge_layers.1), channel_id=1, source_target_pairs={{0,24},{4,28},{8,16},{12,20},{16,8},{20,12},{24,0},{28,4},{1,25},{... | collective-permute-start | bytes 245768 | tf_op jit(solution)/shard_map/ppermute | solution.py:271
  38.4 6.4 %collective-permute-start.12 = (f32[160,128]{1,0:T(8,128)S(1)}, f32[160,128]{1,0:T(8,128)S(1)}, u32[]{:S(2)}, u32[]{:S(2)}) collective-permute-start(f32[160,128]{1,0:T(8,128)S(1)} %sum_home.1.after.refs_1_), channel_id=1, source_target_pairs={{0,2},{1,3},{2,0},{3,1},{4,6},{5,7},{6,4},{7,5},{8,10},{9,11},{10,... | collective-permute-start | bytes 245768 | tf_op jit(solution)/shard_map/ppermute | solution.py:271
  41.1 15.4 %copy-start.1 = (f32[2,400,400]{2,1,0:T(8,128)S(1)}, f32[2,400,400]{2,1,0:T(8,128)}, u32[]{:S(2)}) copy-start(f32[2,400,400]{2,1,0:T(8,128)} %ops.5) | copy-start | bytes 3840004
  44.8 4.5 %collective-permute-start.16 = (f32[160,128]{1,0:T(8,128)S(1)}, f32[160,128]{1,0:T(8,128)S(1)}, u32[]{:S(2)}, u32[]{:S(2)}) collective-permute-start(f32[160,128]{1,0:T(8,128)S(1)} %sum_layers.1.after.refs_0_), channel_id=1, source_target_pairs={{0,1},{1,0},{2,3},{3,2},{4,5},{5,4},{6,7},{7,6},{8,9},{9,8},{10,11... | collective-permute-start | bytes 245768 | tf_op jit(solution)/shard_map/ppermute | solution.py:271
  45.0 7.0 %collective-permute-start.13 = (f32[160,128]{1,0:T(8,128)S(1)}, f32[160,128]{1,0:T(8,128)S(1)}, u32[]{:S(2)}, u32[]{:S(2)}) collective-permute-start(f32[160,128]{1,0:T(8,128)S(1)} %sum_layers.1.after.refs_0_), channel_id=1, source_target_pairs={{0,8},{4,12},{8,0},{12,4},{16,24},{20,28},{24,16},{28,20},{1,9},{5... | collective-permute-start | bytes 245768 | tf_op jit(solution)/shard_map/ppermute | solution.py:271
  46.1 6.7 %collective-permute-start.14 = (f32[160,128]{1,0:T(8,128)S(1)}, f32[160,128]{1,0:T(8,128)S(1)}, u32[]{:S(2)}, u32[]{:S(2)}) collective-permute-start(f32[160,128]{1,0:T(8,128)S(1)} %sum_layers.1.after.refs_0_), channel_id=1, source_target_pairs={{0,24},{4,28},{8,16},{12,20},{16,8},{20,12},{24,0},{28,4},{1,25},{... | collective-permute-start | bytes 245768 | tf_op jit(solution)/shard_map/ppermute | solution.py:271
  48.5 4.4 %collective-permute-start.15 = (f32[160,128]{1,0:T(8,128)S(1)}, f32[160,128]{1,0:T(8,128)S(1)}, u32[]{:S(2)}, u32[]{:S(2)}) collective-permute-start(f32[160,128]{1,0:T(8,128)S(1)} %sum_layers.1.after.refs_0_), channel_id=1, source_target_pairs={{0,16},{4,20},{8,24},{12,28},{16,0},{20,4},{24,8},{28,12},{1,17},{... | collective-permute-start | bytes 245768 | tf_op jit(solution)/shard_map/ppermute | solution.py:271
  49.3 4.4 %collective-permute-start.17 = (f32[160,128]{1,0:T(8,128)S(1)}, f32[160,128]{1,0:T(8,128)S(1)}, u32[]{:S(2)}, u32[]{:S(2)}) collective-permute-start(f32[160,128]{1,0:T(8,128)S(1)} %collective-permute-done.16.after.refs_0_), channel_id=1, source_target_pairs={{0,8},{4,12},{8,0},{12,4},{16,24},{20,28},{24,16},{28,20},{1,9},{5... | collective-permute-start | bytes 245768 | tf_op jit(solution)/shard_map/ppermute | solution.py:271
  49.6 5.7 %collective-permute-start.18 = (f32[160,128]{1,0:T(8,128)S(1)}, f32[160,128]{1,0:T(8,128)S(1)}, u32[]{:S(2)}, u32[]{:S(2)}) collective-permute-start(f32[160,128]{1,0:T(8,128)S(1)} %collective-permute-done.16.after.refs_0_), channel_id=1, source_target_pairs={{0,24},{4,28},{8,16},{12,20},{16,8},{20,12},{24,0},{28,4},{1,25},{... | collective-permute-start | bytes 245768 | tf_op jit(solution)/shard_map/ppermute | solution.py:271
  52.0 4.4 %collective-permute-start.19 = (f32[160,128]{1,0:T(8,128)S(1)}, f32[160,128]{1,0:T(8,128)S(1)}, u32[]{:S(2)}, u32[]{:S(2)}) collective-permute-start(f32[160,128]{1,0:T(8,128)S(1)} %collective-permute-done.16.after.refs_0_), channel_id=1, source_target_pairs={{0,16},{4,20},{8,24},{12,28},{16,0},{20,4},{24,8},{28,12},{1,17},{... | collective-permute-start | bytes 245768 | tf_op jit(solution)/shard_map/ppermute | solution.py:271
  53.0 4.0 %collective-permute-start.20 = (f32[4,160,128]{2,1,0:T(8,128)S(1)}, f32[4,160,128]{2,1,0:T(8,128)S(1)}, u32[]{:S(2)}, u32[]{:S(2)}) collective-permute-start(f32[4,160,128]{2,1,0:T(8,128)S(1)} %join_near.1.near), channel_id=1, source_target_pairs={{0,4},{4,0},{8,12},{12,8},{16,20},{20,16},{24,28},{28,24},{1,5},{5... | collective-permute-start | bytes 983048 | tf_op jit(solution)/shard_map/ppermute | solution.py:271
  56.5 1.7 %collective-permute-start.21 = (f32[4,160,128]{2,1,0:T(8,128)S(1)}, f32[4,160,128]{2,1,0:T(8,128)S(1)}, u32[]{:S(2)}, u32[]{:S(2)}) collective-permute-start(f32[4,160,128]{2,1,0:T(8,128)S(1)} %join_far.1.far), channel_id=1, source_target_pairs={{0,4},{4,0},{8,12},{12,8},{16,20},{20,16},{24,28},{28,24},{1,5},{5... | collective-permute-start | bytes 983048 | tf_op jit(solution)/shard_map/ppermute | solution.py:271

commit v2 on v1

--- a/solution.py
+++ b/solution.py
@@ -186,9 +186,9 @@
     refs[-1][...] = functools.reduce(jnp.add, [ref[...] for ref in refs[:-1]])
 
 
-def join_kernel(*refs):
+def join_kernel(*refs, after=0):
     out = refs[-1]
-    for j, ref in zip(walk_of(len(refs) - 1), refs):
+    for j, ref in zip(walk_of(out.shape[0]), refs[after:]):
         out[jnp.bitwise_xor(chip(), j)] = ref[...]
 
 
@@ -196,7 +196,7 @@
     out[...] = value[...]
 
 
-def operator_rows(which, ops, sums, near, far, flat, store):
+def operator_rows(which, ops, sums, near, far, flat, out, finish):
     chunk = near.shape[1]
     for j in range(near.shape[0]):
         for own, ref in ((side(), near), (1 - side(), far)):
@@ -212,30 +212,29 @@
     square = jnp.sum(tail * tail, axis=1, keepdims=True)
     square = square + jnp.sum(sum(tile * tile for tile in tiles), axis=1, keepdims=True)
     rate = 0.1 / jnp.sqrt(sums[which] + square / w)
-    for t, part in enumerate([*tiles, tail]):
-        span = slice(t * LANES, min(w, (t + 1) * LANES))
-        store(span, ops[which, :, span] - part * rate)
+    for block in (slice(0, w // 16 * 8), slice(w // 16 * 8, w)):
+        for t, part in enumerate([*tiles, tail]):
+            span = slice(t * LANES, min(w, (t + 1) * LANES))
+            out[block, span] = ops[which, block, span] - part[block] * rate[block]
+        finish(block)
 
 
 def own_operator_kernel(ops, sums, near, far, out, flat):
-    def store(span, value):
-        out[:, span] = value
-
-    operator_rows(core(), ops, sums, near, far, flat, store)
+    operator_rows(core(), ops, sums, near, far, flat, out, lambda block: None)
 
 
 def operator_kernel(own, ops, sums, near, far, out, flat, half, sem):
-    first = pltpu.make_async_copy(own, out.at[core()], sem.at[0])
-    first.start()
-
-    def store(span, value):
-        half[:, span] = value
-
-    operator_rows(1 - core(), ops, sums, near, far, flat, store)
-    second = pltpu.make_async_copy(half, out.at[1 - core()], sem.at[1])
-    second.start()
-    first.wait()
-    second.wait()
+    copies = [pltpu.make_async_copy(own, out.at[core()], sem.at[0])]
+    copies[0].start()
+
+    def finish(block):
+        target = out.at[1 - core(), block, :]
+        copies.append(pltpu.make_async_copy(half.at[block, :], target, sem.at[len(copies)]))
+        copies[-1].start()
+
+    operator_rows(1 - core(), ops, sums, near, far, flat, half, finish)
+    for copy in copies:
+        copy.wait()
 
 
 def shaped(shape, dtype=F32):
@@ -247,7 +246,7 @@
 SMEM = pl.BlockSpec(memory_space=pltpu.SMEM)
 
 
-def run(kernel, out_shape, scalars, *args, after=(), scratch=(), out_specs=None, flops=0, name=None):
+def run(kernel, out_shape, scalars, *args, after=(), scratch=(), out_specs=None, flops=0, size=2**20, name=None):
     specs = [SMEM] * len(scalars) + [ANY] * len(after) + [VMEM] * len(args)
     return pl.pallas_call(
         kernel,
@@ -256,7 +255,7 @@
         out_specs=out_specs or jax.tree.map(lambda _: VMEM, out_shape),
         scratch_shapes=scratch,
         compiler_params=pltpu.CompilerParams(vmem_limit_bytes=24 * 2**20),
-        cost_estimate=pl.CostEstimate(flops=flops, bytes_accessed=2**20, transcendentals=0),
+        cost_estimate=pl.CostEstimate(flops=flops, bytes_accessed=size, transcendentals=0),
         name=name,
     )(*scalars, *after, *args)
 
@@ -345,23 +344,17 @@
     )
     away = [away[0]] + [across_chips(t, j) for j, t in zip(direct[1:], away[1:])]
     home = [home[0]] + [across_chips(t, j) for j, t in zip(direct[1:] + distant, home[1:] + merged)]
-    passed = run(functools.partial(sum_kernel, after=0), part, [], *away, name="sum_away")
+    passed = run(functools.partial(sum_kernel, after=1), part, [], *away, after=merged[:1], name="sum_away")
     done = shaped((8, LANES))
+    mine = run(
+        functools.partial(sum_kernel, after=0), part, [], *home, swap(passed, "rhs", 1), name="sum_home",
+    )
     new_left, done_left = run(
         left_update_kernel, [shaped((w, rows)), done],
         [], left, left_sum, ops_high, ops_low, pick, rel, d_high, d_low,
-        after=[passed], flops=2 * 10**9, name="left_update",
-    )
-    mine = run(
-        functools.partial(sum_kernel, after=1), part, [], *home, swap(passed, "rhs", 1),
-        after=[done_left], name="sum_home",
-    )
-    new_right, done_right = run(
-        right_update_kernel, [shaped((w, rows)), done],
-        [], right, right_sum, unit, p_high, p_low,
-        after=[mine], flops=10**9, name="right_update",
-    )
-    bit, after = 2, [done_right]
+        after=[mine], flops=2 * 10**9, name="left_update",
+    )
+    bit, after = 2, [done_left]
     while bit < layers:
         mine = run(
             functools.partial(sum_kernel, after=len(after)), part,
@@ -378,7 +371,14 @@
 
     joined = shaped((chips, *part.shape))
     near = run(join_kernel, joined, [], *spread(mine), name="join_near")
-    far = run(join_kernel, joined, [], *spread(next_layer), name="join_far")
+    new_right, done_right = run(
+        right_update_kernel, [shaped((w, rows)), done],
+        [], right, right_sum, unit, p_high, p_low,
+        after=[near], size=0, name="right_update",
+    )
+    far = run(
+        functools.partial(join_kernel, after=1), joined, [], *spread(next_layer), after=[done_right], name="join_far",
+    )
     other_near, other_far = across_cores(near), across_cores(far)
     flat = [pltpu.VMEM((packed, LANES), F32)]
     own = run(
@@ -387,7 +387,7 @@
     )
     new_operators = run(
         operator_kernel, shaped(operators.shape), [], own, operators, column, other_near, other_far,
-        scratch=[*flat, pltpu.VMEM(operators.shape[1:], F32), pltpu.SemaphoreType.DMA((2,))],
+        scratch=[*flat, pltpu.VMEM(operators.shape[1:], F32), pltpu.SemaphoreType.DMA((3,))],
         out_specs=ANY, name="operator_update",
     )
     return (

time: 59.8 us -> 58.9 us (0.985)
  waiting for transfers between devices: 20.6 us -> 13.5 us
  starting transfers between devices: 20.2 us -> 26.5 us
    ppermute x18, waiting for transfers between devices: 15.2 us -> 8.1 us  [swap(): return lax.ppermute(value, axis, [(i, i ^ bit) for i in range(count)])]
    ppermute x18, starting transfers between devices: 14.3 us -> 20.5 us  [swap(): return lax.ppermute(value, axis, [(i, i ^ bit) for i in range(count)])]
  transfers between devices with their start and end apart: 22 -> 22, of which waited for: 13 -> 11; matrix products, arithmetic and copies ran while one was open for 0% -> 0% of each run, Pallas kernels for 15% -> 15%
where the time goes in v2:
time: 58.9 us; the launch traced here: 58.7 us
  starting transfers between devices  26.5 us (45%)
  waiting for transfers between devices  13.5 us (23%)
  Pallas kernels  13 us (22%)
  local copies, waits for them, and re-layouts  4.16 us (7%)
  between operations  1.45 us (2%)
    ppermute x18, starting transfers between devices, swap(): return lax.ppermute(value, axis, [(i, i ^ bit) for i in range(count)])  20.5 us
    pallas_call x21, Pallas kernels, run(): pl.pallas_call(kernel, out_shape=out_shape, in_specs=specs, out_specs=out...  13 us
    ppermute x18, waiting for transfers between devices, swap(): return lax.ppermute(value, axis, [(i, i ^ bit) for i in range(count)])  8.1 us
    ppermute x4, starting transfers between devices, around(): lax.ppermute(value, axis, [(i, (i + steps) % count) for i in range(count)])  5.98 us
    ppermute x4, waiting for transfers between devices, around(): lax.ppermute(value, axis, [(i, (i + steps) % count) for i in range(count)])  5.41 us
    unnamed x14, local copies, waits for them, and re-layouts  4.16 us
  transfers between devices with their start and end apart: 22, of which 11 were waited for; matrix products, arithmetic and copies ran while one was open for 0% of the time, Pallas kernels for 15%

profile of v2, /device:TPU:0, one launch (start us, length us, event | category | flops | bytes accessed | tf_op | source)
XLA Modules:
  0.0 58.7 jit_solution(4428120593243076634)
XLA Ops:
  0.6 0.0 copy-start.6
  0.6 0.5 collective-permute-start.3
  1.1 2.6 %collective-permute-start.1 = (f32[400,384]{1,0:T(8,128)}, f32[400,384]{1,0:T(8,128)S(1)}, u32[]{:S(2)}, u32[]{:S(2)}) collective-permute-start(f32[400,384]{1,0:T(8,128)} %bitcast.30), channel_id=1, source_target_pairs={{0,1},{1,2},{2,3},{3,0},{4,5},{5,6},{6,7},{7,4},{8,9},{9,10},{10,1... | collective-permute-start | bytes 1843208 | tf_op jit(solution)/shard_map/ppermute | solution.py:265
  3.8 1.3 %collective-permute-start.2 = (f32[1,384]{1,0:T(1,128)}, f32[1,384]{1,0:T(1,128)S(1)}, u32[]{:S(2)}, u32[]{:S(2)}) collective-permute-start(f32[1,384]{1,0:T(1,128)} %bitcast.32), channel_id=1, source_target_pairs={{0,4},{4,8},{8,12},{12,16},{16,20},{20,24},{24,28},{28,0},{1,5},{5... | collective-permute-start | bytes 4616 | tf_op jit(solution)/shard_map/ppermute | solution.py:265
  5.0 1.6 %collective-permute-start = (f32[1,384]{1,0:T(1,128)}, f32[1,384]{1,0:T(1,128)S(1)}, u32[]{:S(2)}, u32[]{:S(2)}) collective-permute-start(f32[1,384]{1,0:T(1,128)} %bitcast.33), channel_id=1, source_target_pairs={{0,1},{1,2},{2,3},{3,0},{4,5},{5,6},{6,7},{7,4},{8,9},{9,10},{10,1... | collective-permute-start | bytes 4616 | tf_op jit(solution)/shard_map/ppermute | solution.py:265
  7.3 0.0 copy-start
  7.3 1.4 %copy-done = f32[2,400,400]{2,1,0:T(8,128)S(1)} copy-done((f32[2,400,400]{2,1,0:T(8,128)S(1)}, f32[2,400,400]{2,1,0:T(8,128)}, u32[]{:S(2)}) %copy-start) | copy-done | bytes 1280024
  8.7 0.0 copy-start.2
  8.7 0.7 %copy-done.2 = f32[2,400]{1,0:T(2,128)S(1)} copy-done((f32[2,400]{1,0:T(2,128)S(1)}, f32[2,400]{1,0:T(2,128)}, u32[]{:S(2)}) %copy-start.2) | copy-done | bytes 3224
  9.4 0.7 %copy-done.3 = s32[1,1,384]{2,1,0:T(1,128)S(1)} copy-done((s32[1,1,384]{2,1,0:T(1,128)S(1)}, s32[1,1,384]{2,1,0:T(1,128)}, u32[]{:S(2)}) %copy-start.3) | copy-done | bytes 1560
  10.1 0.7 %copy-done.4 = s32[1,1,384]{2,1,0:T(1,128)S(1)} copy-done((s32[1,1,384]{2,1,0:T(1,128)S(1)}, s32[1,1,384]{2,1,0:T(1,128)}, u32[]{:S(2)}) %copy-start.4) | copy-done | bytes 1560
  10.8 0.7 %copy-done.5 = s32[1,1,384]{2,1,0:T(1,128)S(1)} copy-done((s32[1,1,384]{2,1,0:T(1,128)S(1)}, s32[1,1,384]{2,1,0:T(1,128)}, u32[]{:S(2)}) %copy-start.5) | copy-done | bytes 1560
  11.4 0.8 %prepare.1 = (bf16[384,384]{1,0:T(8,128)(2,1)S(1)}, f32[384,384]{1,0:T(8,128)S(1)}, f32[384,384]{1,0:T(8,128)S(1)}, f32[384,1]{1,0:T(8,128)S(1)}, f32[2,400,1]{2...) custom-call(s32[1,1]{1,0:T(1,128)S(6)} %copy.14.count, s32[1,384]{1,0:T(1,128)S(1)} %bitcast.22, ...), custom_call_target="tpu_custom_call" | custom-call | bytes 1048576 | tf_op jit(solution)/shard_map/prepare/pallas_call | solution.py:251
  12.3 0.0 collective-permute-done.2.after.left_sum
  12.3 0.0 collective-permute-done.3.left
  12.3 0.0 copy-done.6
  12.3 2.2 %left_side.1 = (bf16[400,384]{1,0:T(8,128)(2,1)S(1)}, bf16[400,384]{1,0:T(8,128)(2,1)S(1)}, f32[400,384]{1,0:T(8,128)S(1)}, f32[1,384]{1,0:T(1,128)S(1)}, bf16[3...) custom-call(f32[1,384]{1,0:T(1,128)S(1)} %collective-permute-done.2.after.left_sum, ...), custom_call_target="tpu_custom_call" | custom-call | flops 2000000000 | bytes 1048576 | tf_op jit(solution)/shard_map/left_side/pallas_call | solution.py:251
  14.5 5.4 %collective-permute-done.after.right_sum = f32[1,384]{1,0:T(1,128)S(1)} collective-permute-done((f32[1,384]{1,0:T(1,128)}, f32[1,384]{1,0:T(1,128)S(1)}, u32[]{:S(2)}, u32[]{:S(2)}) %collective-permute-start) | collective-permute-done | bytes 1568 | tf_op jit(solution)/shard_map/ppermute | solution.py:265
  19.9 0.0 collective-permute-done.1.right
  19.9 2.6 %right_side.1 = (f32[1280,128]{1,0:T(8,128)S(1)}, bf16[400,384]{1,0:T(8,128)(2,1)S(1)}, bf16[400,384]{1,0:T(8,128)(2,1)S(1)}, bf16[384,384]{1,0:T(8,128)(2,1)S(1)}, bf16[384,384]{1,0:T(8,128)(2,1)S(1)}) custom-call(f32[1,384]{1,0:T(1,128)S(1)} %collective-permute-done.after.right_sum, f32[400,384]{1,0:T(8,128)S(1)} %collective-permute-done.1.right, ...), custom_call_target="tpu_custom_call" | custom-call | flops 3000000000 | bytes 1048576 | tf_op jit(solution)/shard_map/right_side/pallas_call | solution.py:251
  22.5 0.7 %collective-permute-start.4 = (f32[1280,128]{1,0:T(8,128)S(1)}, f32[1280,128]{1,0:T(8,128)S(1)}, u32[]{:S(2)}, u32[]{:S(2)}) collective-permute-start(f32[1280,128]{1,0:T(8,128)S(1)} %get-tuple-element.47), channel_id=1, source_target_pairs={{0,4},{4,0},{8,12},{12,8},{16,20},{20,16},{24,28},{28,24},{1,5},{5... | collective-permute-start | bytes 1966088 | tf_op jit(solution)/shard_map/ppermute | solution.py:270
  23.2 0.8 %own_relation.1 = f32[1280,128]{1,0:T(8,128)S(1)} custom-call(s32[1,384]{1,0:T(1,128)S(1)} %bitcast.27, bf16[400,384]{1,0:T(8,128)(2,1)S(1)} %get-tuple-element.45.d_high, bf16[400,384]{1,0:T(8,128)(2,1)S(1)} %get-tuple-element.46.d_low, bf16[400,384]{1,0:T(8,128)(2,1)S(1)} %get-tuple-element.43.x_high, bf16[400,384]{1,0:T(8,128)(2,1)S(1)} %get-tuple-element.44.x_low), custom_call_target="tpu_custom_call" | custom-call | flops 1000000000 | bytes 1048576 | tf_op jit(solution)/shard_map/own_relation/pallas_call | solution.py:251
  24.0 1.0 %collective-permute-done.4 = f32[1280,128]{1,0:T(8,128)S(1)} collective-permute-done((f32[1280,128]{1,0:T(8,128)S(1)}, f32[1280,128]{1,0:T(8,128)S(1)}, u32[]{:S(2)}, u32[]{:S(2)}) %collective-permute-start.4) | collective-permute-done | bytes 655392 | tf_op jit(solution)/shard_map/ppermute | solution.py:270
  24.9 0.1 sum_cores.1
  25.0 0.1 collective-permute-start.7
  25.1 1.8 %collective-permute-start.9 = (f32[160,128]{1,0:T(8,128)S(1)}, f32[160,128]{1,0:T(8,128)S(1)}, u32[]{:S(2)}, u32[]{:S(2)}) collective-permute-start(f32[160,128]{1,0:T(8,128)S(1)} %get-tuple-element.54), channel_id=1, source_target_pairs={{0,8},{4,12},{8,0},{12,4},{16,24},{20,28},{24,16},{28,20},{1,9},{5... | collective-permute-start | bytes 245768 | tf_op jit(solution)/shard_map/ppermute | solution.py:270
  26.9 1.7 %collective-permute-start.10 = (f32[160,128]{1,0:T(8,128)S(1)}, f32[160,128]{1,0:T(8,128)S(1)}, u32[]{:S(2)}, u32[]{:S(2)}) collective-permute-start(f32[160,128]{1,0:T(8,128)S(1)} %get-tuple-element.55), channel_id=1, source_target_pairs={{0,16},{4,20},{8,24},{12,28},{16,0},{20,4},{24,8},{28,12},{1,17},{... | collective-permute-start | bytes 245768 | tf_op jit(solution)/shard_map/ppermute | solution.py:270
  28.5 0.4 collective-permute-start.5
  28.9 0.3 collective-permute-start.6
  29.2 0.6 collective-permute-done.7.two
  29.8 2.7 %collective-permute-start.8 = (f32[160,128]{1,0:T(8,128)S(1)}, f32[160,128]{1,0:T(8,128)S(1)}, u32[]{:S(2)}, u32[]{:S(2)}) collective-permute-start(f32[160,128]{1,0:T(8,128)S(1)} %merge_layers.1.refs_0_), channel_id=1, source_target_pairs={{0,24},{4,28},{8,16},{12,20},{16,8},{20,12},{24,0},{28,4},{1,25},{... | collective-permute-start | bytes 245768 | tf_op jit(solution)/shard_map/ppermute | solution.py:270
  32.5 0.0 collective-permute-done.9.refs_2_
  32.5 0.0 collective-permute-done.10.refs_3_
  32.5 1.7 %collective-permute-start.11 = (f32[160,128]{1,0:T(8,128)S(1)}, f32[160,128]{1,0:T(8,128)S(1)}, u32[]{:S(2)}, u32[]{:S(2)}) collective-permute-start(f32[160,128]{1,0:T(8,128)S(1)} %sum_away.1), channel_id=1, source_target_pairs={{0,1},{1,0},{2,3},{3,2},{4,5},{5,4},{6,7},{7,6},{8,9},{9,8},{10,11... | collective-permute-start | bytes 245768 | tf_op jit(solution)/shard_map/ppermute | solution.py:270
  34.2 0.0 collective-permute-done.5.refs_1_
  34.2 0.1 collective-permute-done.6.refs_2_
  34.2 1.0 %collective-permute-done.8.refs_3_ = f32[160,128]{1,0:T(8,128)S(1)} collective-permute-done((f32[160,128]{1,0:T(8,128)S(1)}, f32[160,128]{1,0:T(8,128)S(1)}, u32[]{:S(2)}, u32[]{:S(2)}) %collective-permute-start.8) | collective-permute-done | bytes 81952 | tf_op jit(solution)/shard_map/ppermute | solution.py:270
  35.2 1.8 %collective-permute-done.11.refs_4_ = f32[160,128]{1,0:T(8,128)S(1)} collective-permute-done((f32[160,128]{1,0:T(8,128)S(1)}, f32[160,128]{1,0:T(8,128)S(1)}, u32[]{:S(2)}, u32[]{:S(2)}) %collective-permute-start.11) | collective-permute-done | bytes 81952 | tf_op jit(solution)/shard_map/ppermute | solution.py:270
  37.0 1.9 %collective-permute-start.12 = (f32[160,128]{1,0:T(8,128)S(1)}, f32[160,128]{1,0:T(8,128)S(1)}, u32[]{:S(2)}, u32[]{:S(2)}) collective-permute-start(f32[160,128]{1,0:T(8,128)S(1)} %sum_home.1.after.refs_1_), channel_id=1, source_target_pairs={{0,2},{1,3},{2,0},{3,1},{4,6},{5,7},{6,4},{7,5},{8,10},{9,11},{10,... | collective-permute-start | bytes 245768 | tf_op jit(solution)/shard_map/ppermute | solution.py:270
  39.0 2.9 %left_update.1 = (f32[400,384]{1,0:T(8,128)}, f32[8,128]{1,0:T(8,128)S(1)}) custom-call(f32[160,128]{1,0:T(8,128)S(1)} %sum_home.1.after.refs_1_, f32[400,384]{1,0:T(8,128)S(1)} %collective-permute-done.3.left, f32[1,384]{1,0:T(1,128)S(1)} %collective-permute-done.2.after.left_sum, bf16[2,400,400]{2,1,0:T(8,128)(2,1)S(1)} %get-tuple-element.33.ops_high, ...), custom_call_target="tpu_custom_call" | custom-call | flops 2000000000 | bytes 1048576 | tf_op jit(solution)/shard_map/left_update/pallas_call | solution.py:251
  41.8 0.6 %collective-permute-done.12.refs_2_ = f32[160,128]{1,0:T(8,128)S(1)} collective-permute-done((f32[160,128]{1,0:T(8,128)S(1)}, f32[160,128]{1,0:T(8,128)S(1)}, u32[]{:S(2)}, u32[]{:S(2)}) %collective-permute-start.12) | collective-permute-done | bytes 81952 | tf_op jit(solution)/shard_map/ppermute | solution.py:270
  42.4 2.2 %collective-permute-start.16 = (f32[160,128]{1,0:T(8,128)S(1)}, f32[160,128]{1,0:T(8,128)S(1)}, u32[]{:S(2)}, u32[]{:S(2)}) collective-permute-start(f32[160,128]{1,0:T(8,128)S(1)} %sum_layers.1.after.refs_0_), channel_id=1, source_target_pairs={{0,1},{1,0},{2,3},{3,2},{4,5},{5,4},{6,7},{7,6},{8,9},{9,8},{10,11... | collective-permute-start | bytes 245768 | tf_op jit(solution)/shard_map/ppermute | solution.py:270
  44.6 0.0 collective-permute-start.13
  44.6 3.0 %collective-permute-start.14 = (f32[160,128]{1,0:T(8,128)S(1)}, f32[160,128]{1,0:T(8,128)S(1)}, u32[]{:S(2)}, u32[]{:S(2)}) collective-permute-start(f32[160,128]{1,0:T(8,128)S(1)} %sum_layers.1.after.refs_0_), channel_id=1, source_target_pairs={{0,24},{4,28},{8,16},{12,20},{16,8},{20,12},{24,0},{28,4},{1,25},{... | collective-permute-start | bytes 245768 | tf_op jit(solution)/shard_map/ppermute | solution.py:270
  47.6 0.5 collective-permute-start.15
  48.1 0.0 collective-permute-done.16.after.refs_1_
  48.1 0.1 collective-permute-start.17
  48.2 2.9 %collective-permute-start.18 = (f32[160,128]{1,0:T(8,128)S(1)}, f32[160,128]{1,0:T(8,128)S(1)}, u32[]{:S(2)}, u32[]{:S(2)}) collective-permute-start(f32[160,128]{1,0:T(8,128)S(1)} %collective-permute-done.16.after.refs_1_), channel_id=1, source_target_pairs={{0,24},{4,28},{8,16},{12,20},{16,8},{20,12},{24,0},{28,4},{1,25},{... | collective-permute-start | bytes 245768 | tf_op jit(solution)/shard_map/ppermute | solution.py:270
  51.1 0.0 collective-permute-done.13.value
  51.1 0.5 collective-permute-start.19
  51.6 0.0 collective-permute-done.14.value
  51.7 0.4 collective-permute-done.15.value
  52.1 0.1 collective-permute-start.20
  52.2 0.0 copy-start.1
  52.2 1.8 %right_update.1 = (f32[400,384]{1,0:T(8,128)}, f32[8,128]{1,0:T(8,128)S(1)}) custom-call(f32[4,160,128]{2,1,0:T(8,128)S(1)} %join_near.1.after.near, f32[400,384]{1,0:T(8,128)S(1)} %collective-permute-done.1.right, f32[1,384]{1,0:T(1,128)S(1)} %collective-permute-done.after.right_sum, f32[400,384]{1,0:T(8,128)S(1)} %get-tuple-element.36.unit, ...), custom_call_target="tpu_custom_call" | custom-call | tf_op jit(solution)/shard_map/right_update/pallas_call | solution.py:251
  54.0 0.0 collective-permute-done.17.value
  54.0 0.4 collective-permute-done.18.value
  54.4 1.1 %collective-permute-done.19.value = f32[160,128]{1,0:T(8,128)S(1)} collective-permute-done((f32[160,128]{1,0:T(8,128)S(1)}, f32[160,128]{1,0:T(8,128)S(1)}, u32[]{:S(2)}, u32[]{:S(2)}) %collective-permute-start.19) | collective-permute-done | bytes 81952 | tf_op jit(solution)/shard_map/ppermute | solution.py:270
  55.6 0.1 collective-permute-start.21
  55.7 0.0 copy-done.1
  55.7 0.4 own_operator.1.own
  56.2 0.0 collective-permute-done.20.near
  56.2 1.1 %collective-permute-done.21.far = f32[4,160,128]{2,1,0:T(8,128)S(1)} collective-permute-done((f32[4,160,128]{2,1,0:T(8,128)S(1)}, f32[4,160,128]{2,1,0:T(8,128)S(1)}, u32[]{:S(2)}, u32[]{:S(2)}) %collective-permute-start.21) | collective-permute-done | bytes 327712 | tf_op jit(solution)/shard_map/ppermute | solution.py:270
  57.3 1.3 %operator_update.1 = f32[2,400,400]{2,1,0:T(8,128)} custom-call(f32[400,400]{1,0:T(8,128)S(1)} %own_operator.1.own, f32[2,400,400]{2,1,0:T(8,128)S(1)} %copy-done.1, f32[2,400,1]{2,1,0:T(8,128)S(1)} %get-tuple-element.61.sums, f32[4,160,128]{2,1,0:T(8,128)S(1)} %collective-permute-done.20.near, f32[4,160,128]{2,1,0:T(8,128)S(1)} %collective-permute-done.21.far), custom_call_target="tpu_custom_call" | custom-call | bytes 1048576 | tf_op jit(solution)/shard_map/operator_update/pallas_call | solution.py:251
  (15 shorter events, 0.2 us)
Async XLA Ops:
  0.6 11.7 %copy-start.6 = (s32[1,1,384]{2,1,0:T(1,128)S(1)}, s32[1,1,384]{2,1,0:T(1,128)}, u32[]{:S(2)}) copy-start(s32[1,1,384]{2,1,0:T(1,128)} %param.19) | copy-start | bytes 4612
  0.6 11.7 %collective-permute-start.3 = (f32[400,384]{1,0:T(8,128)}, f32[400,384]{1,0:T(8,128)S(1)}, u32[]{:S(2)}, u32[]{:S(2)}) collective-permute-start(f32[400,384]{1,0:T(8,128)} %bitcast.29), channel_id=1, source_target_pairs={{0,4},{4,8},{8,12},{12,16},{16,20},{20,24},{24,28},{28,0},{1,5},{5... | collective-permute-start | bytes 1843208 | tf_op jit(solution)/shard_map/ppermute | solution.py:265
  1.1 18.8 %collective-permute-start.1 = (f32[400,384]{1,0:T(8,128)}, f32[400,384]{1,0:T(8,128)S(1)}, u32[]{:S(2)}, u32[]{:S(2)}) collective-permute-start(f32[400,384]{1,0:T(8,128)} %bitcast.30), channel_id=1, source_target_pairs={{0,1},{1,2},{2,3},{3,0},{4,5},{5,6},{6,7},{7,4},{8,9},{9,10},{10,1... | collective-permute-start | bytes 1843208 | tf_op jit(solution)/shard_map/ppermute | solution.py:265
  3.8 8.5 %collective-permute-start.2 = (f32[1,384]{1,0:T(1,128)}, f32[1,384]{1,0:T(1,128)S(1)}, u32[]{:S(2)}, u32[]{:S(2)}) collective-permute-start(f32[1,384]{1,0:T(1,128)} %bitcast.32), channel_id=1, source_target_pairs={{0,4},{4,8},{8,12},{12,16},{16,20},{20,24},{24,28},{28,0},{1,5},{5... | collective-permute-start | bytes 4616 | tf_op jit(solution)/shard_map/ppermute | solution.py:265
  5.0 14.9 %collective-permute-start = (f32[1,384]{1,0:T(1,128)}, f32[1,384]{1,0:T(1,128)S(1)}, u32[]{:S(2)}, u32[]{:S(2)}) collective-permute-start(f32[1,384]{1,0:T(1,128)} %bitcast.33), channel_id=1, source_target_pairs={{0,1},{1,2},{2,3},{3,0},{4,5},{5,6},{6,7},{7,4},{8,9},{9,10},{10,1... | collective-permute-start | bytes 4616 | tf_op jit(solution)/shard_map/ppermute | solution.py:265
  7.3 1.4 %copy-start = (f32[2,400,400]{2,1,0:T(8,128)S(1)}, f32[2,400,400]{2,1,0:T(8,128)}, u32[]{:S(2)}) copy-start(f32[2,400,400]{2,1,0:T(8,128)} %ops.5) | copy-start | bytes 3840004
  8.7 0.7 %copy-start.2 = (f32[2,400]{1,0:T(2,128)S(1)}, f32[2,400]{1,0:T(2,128)}, u32[]{:S(2)}) copy-start(f32[2,400]{1,0:T(2,128)} %op_sums.1) | copy-start | bytes 9604
  9.4 0.7 %copy-start.3 = (s32[1,1,384]{2,1,0:T(1,128)S(1)}, s32[1,1,384]{2,1,0:T(1,128)}, u32[]{:S(2)}) copy-start(s32[1,1,384]{2,1,0:T(1,128)} %param.17) | copy-start | bytes 4612
  10.1 0.7 %copy-start.4 = (s32[1,1,384]{2,1,0:T(1,128)S(1)}, s32[1,1,384]{2,1,0:T(1,128)}, u32[]{:S(2)}) copy-start(s32[1,1,384]{2,1,0:T(1,128)} %param.18) | copy-start | bytes 4612
  10.8 0.7 %copy-start.5 = (s32[1,1,384]{2,1,0:T(1,128)S(1)}, s32[1,1,384]{2,1,0:T(1,128)}, u32[]{:S(2)}) copy-start(s32[1,1,384]{2,1,0:T(1,128)} %param.20) | copy-start | bytes 4612
  22.5 2.4 %collective-permute-start.4 = (f32[1280,128]{1,0:T(8,128)S(1)}, f32[1280,128]{1,0:T(8,128)S(1)}, u32[]{:S(2)}, u32[]{:S(2)}) collective-permute-start(f32[1280,128]{1,0:T(8,128)S(1)} %get-tuple-element.47), channel_id=1, source_target_pairs={{0,4},{4,0},{8,12},{12,8},{16,20},{20,16},{24,28},{28,24},{1,5},{5... | collective-permute-start | bytes 1966088 | tf_op jit(solution)/shard_map/ppermute | solution.py:270
  25.0 4.8 %collective-permute-start.7 = (f32[1,160,128]{2,1,0:T(8,128)S(1)}, f32[1,160,128]{2,1,0:T(8,128)S(1)}, u32[]{:S(2)}, u32[]{:S(2)}) collective-permute-start(f32[1,160,128]{2,1,0:T(8,128)S(1)} %get-tuple-element.52), channel_id=1, source_target_pairs={{0,1},{1,0},{2,3},{3,2},{4,5},{5,4},{6,7},{7,6},{8,9},{9,8},{10,11... | collective-permute-start | bytes 245768 | tf_op jit(solution)/shard_map/ppermute | solution.py:270
  25.1 7.4 %collective-permute-start.9 = (f32[160,128]{1,0:T(8,128)S(1)}, f32[160,128]{1,0:T(8,128)S(1)}, u32[]{:S(2)}, u32[]{:S(2)}) collective-permute-start(f32[160,128]{1,0:T(8,128)S(1)} %get-tuple-element.54), channel_id=1, source_target_pairs={{0,8},{4,12},{8,0},{12,4},{16,24},{20,28},{24,16},{28,20},{1,9},{5... | collective-permute-start | bytes 245768 | tf_op jit(solution)/shard_map/ppermute | solution.py:270
  26.9 5.6 %collective-permute-start.10 = (f32[160,128]{1,0:T(8,128)S(1)}, f32[160,128]{1,0:T(8,128)S(1)}, u32[]{:S(2)}, u32[]{:S(2)}) collective-permute-start(f32[160,128]{1,0:T(8,128)S(1)} %get-tuple-element.55), channel_id=1, source_target_pairs={{0,16},{4,20},{8,24},{12,28},{16,0},{20,4},{24,8},{28,12},{1,17},{... | collective-permute-start | bytes 245768 | tf_op jit(solution)/shard_map/ppermute | solution.py:270
  28.5 5.6 %collective-permute-start.5 = (f32[160,128]{1,0:T(8,128)S(1)}, f32[160,128]{1,0:T(8,128)S(1)}, u32[]{:S(2)}, u32[]{:S(2)}) collective-permute-start(f32[160,128]{1,0:T(8,128)S(1)} %get-tuple-element.49), channel_id=1, source_target_pairs={{0,8},{4,12},{8,0},{12,4},{16,24},{20,28},{24,16},{28,20},{1,9},{5... | collective-permute-start | bytes 245768 | tf_op jit(solution)/shard_map/ppermute | solution.py:270
  28.9 5.3 %collective-permute-start.6 = (f32[160,128]{1,0:T(8,128)S(1)}, f32[160,128]{1,0:T(8,128)S(1)}, u32[]{:S(2)}, u32[]{:S(2)}) collective-permute-start(f32[160,128]{1,0:T(8,128)S(1)} %get-tuple-element.50), channel_id=1, source_target_pairs={{0,16},{4,20},{8,24},{12,28},{16,0},{20,4},{24,8},{28,12},{1,17},{... | collective-permute-start | bytes 245768 | tf_op jit(solution)/shard_map/ppermute | solution.py:270
  29.8 5.4 %collective-permute-start.8 = (f32[160,128]{1,0:T(8,128)S(1)}, f32[160,128]{1,0:T(8,128)S(1)}, u32[]{:S(2)}, u32[]{:S(2)}) collective-permute-start(f32[160,128]{1,0:T(8,128)S(1)} %merge_layers.1.refs_0_), channel_id=1, source_target_pairs={{0,24},{4,28},{8,16},{12,20},{16,8},{20,12},{24,0},{28,4},{1,25},{... | collective-permute-start | bytes 245768 | tf_op jit(solution)/shard_map/ppermute | solution.py:270
  32.5 4.5 %collective-permute-start.11 = (f32[160,128]{1,0:T(8,128)S(1)}, f32[160,128]{1,0:T(8,128)S(1)}, u32[]{:S(2)}, u32[]{:S(2)}) collective-permute-start(f32[160,128]{1,0:T(8,128)S(1)} %sum_away.1), channel_id=1, source_target_pairs={{0,1},{1,0},{2,3},{3,2},{4,5},{5,4},{6,7},{7,6},{8,9},{9,8},{10,11... | collective-permute-start | bytes 245768 | tf_op jit(solution)/shard_map/ppermute | solution.py:270
  37.0 5.4 %collective-permute-start.12 = (f32[160,128]{1,0:T(8,128)S(1)}, f32[160,128]{1,0:T(8,128)S(1)}, u32[]{:S(2)}, u32[]{:S(2)}) collective-permute-start(f32[160,128]{1,0:T(8,128)S(1)} %sum_home.1.after.refs_1_), channel_id=1, source_target_pairs={{0,2},{1,3},{2,0},{3,1},{4,6},{5,7},{6,4},{7,5},{8,10},{9,11},{10,... | collective-permute-start | bytes 245768 | tf_op jit(solution)/shard_map/ppermute | solution.py:270
  42.4 5.7 %collective-permute-start.16 = (f32[160,128]{1,0:T(8,128)S(1)}, f32[160,128]{1,0:T(8,128)S(1)}, u32[]{:S(2)}, u32[]{:S(2)}) collective-permute-start(f32[160,128]{1,0:T(8,128)S(1)} %sum_layers.1.after.refs_0_), channel_id=1, source_target_pairs={{0,1},{1,0},{2,3},{3,2},{4,5},{5,4},{6,7},{7,6},{8,9},{9,8},{10,11... | collective-permute-start | bytes 245768 | tf_op jit(solution)/shard_map/ppermute | solution.py:270
  44.6 6.5 %collective-permute-start.13 = (f32[160,128]{1,0:T(8,128)S(1)}, f32[160,128]{1,0:T(8,128)S(1)}, u32[]{:S(2)}, u32[]{:S(2)}) collective-permute-start(f32[160,128]{1,0:T(8,128)S(1)} %sum_layers.1.after.refs_0_), channel_id=1, source_target_pairs={{0,8},{4,12},{8,0},{12,4},{16,24},{20,28},{24,16},{28,20},{1,9},{5... | collective-permute-start | bytes 245768 | tf_op jit(solution)/shard_map/ppermute | solution.py:270
  44.6 7.0 %collective-permute-start.14 = (f32[160,128]{1,0:T(8,128)S(1)}, f32[160,128]{1,0:T(8,128)S(1)}, u32[]{:S(2)}, u32[]{:S(2)}) collective-permute-start(f32[160,128]{1,0:T(8,128)S(1)} %sum_layers.1.after.refs_0_), channel_id=1, source_target_pairs={{0,24},{4,28},{8,16},{12,20},{16,8},{20,12},{24,0},{28,4},{1,25},{... | collective-permute-start | bytes 245768 | tf_op jit(solution)/shard_map/ppermute | solution.py:270
  47.6 4.4 %collective-permute-start.15 = (f32[160,128]{1,0:T(8,128)S(1)}, f32[160,128]{1,0:T(8,128)S(1)}, u32[]{:S(2)}, u32[]{:S(2)}) collective-permute-start(f32[160,128]{1,0:T(8,128)S(1)} %sum_layers.1.after.refs_0_), channel_id=1, source_target_pairs={{0,16},{4,20},{8,24},{12,28},{16,0},{20,4},{24,8},{28,12},{1,17},{... | collective-permute-start | bytes 245768 | tf_op jit(solution)/shard_map/ppermute | solution.py:270
  48.1 5.9 %collective-permute-start.17 = (f32[160,128]{1,0:T(8,128)S(1)}, f32[160,128]{1,0:T(8,128)S(1)}, u32[]{:S(2)}, u32[]{:S(2)}) collective-permute-start(f32[160,128]{1,0:T(8,128)S(1)} %collective-permute-done.16.after.refs_1_), channel_id=1, source_target_pairs={{0,8},{4,12},{8,0},{12,4},{16,24},{20,28},{24,16},{28,20},{1,9},{5... | collective-permute-start | bytes 245768 | tf_op jit(solution)/shard_map/ppermute | solution.py:270
  48.2 6.2 %collective-permute-start.18 = (f32[160,128]{1,0:T(8,128)S(1)}, f32[160,128]{1,0:T(8,128)S(1)}, u32[]{:S(2)}, u32[]{:S(2)}) collective-permute-start(f32[160,128]{1,0:T(8,128)S(1)} %collective-permute-done.16.after.refs_1_), channel_id=1, source_target_pairs={{0,24},{4,28},{8,16},{12,20},{16,8},{20,12},{24,0},{28,4},{1,25},{... | collective-permute-start | bytes 245768 | tf_op jit(solution)/shard_map/ppermute | solution.py:270
  51.1 4.4 %collective-permute-start.19 = (f32[160,128]{1,0:T(8,128)S(1)}, f32[160,128]{1,0:T(8,128)S(1)}, u32[]{:S(2)}, u32[]{:S(2)}) collective-permute-start(f32[160,128]{1,0:T(8,128)S(1)} %collective-permute-done.16.after.refs_1_), channel_id=1, source_target_pairs={{0,16},{4,20},{8,24},{12,28},{16,0},{20,4},{24,8},{28,12},{1,17},{... | collective-permute-start | bytes 245768 | tf_op jit(solution)/shard_map/ppermute | solution.py:270
  52.1 4.0 %collective-permute-start.20 = (f32[4,160,128]{2,1,0:T(8,128)S(1)}, f32[4,160,128]{2,1,0:T(8,128)S(1)}, u32[]{:S(2)}, u32[]{:S(2)}) collective-permute-start(f32[4,160,128]{2,1,0:T(8,128)S(1)} %join_near.1.after.near), channel_id=1, source_target_pairs={{0,4},{4,0},{8,12},{12,8},{16,20},{20,16},{24,28},{28,24},{1,5},{5... | collective-permute-start | bytes 983048 | tf_op jit(solution)/shard_map/ppermute | solution.py:270
  52.2 3.5 %copy-start.1 = (f32[2,400,400]{2,1,0:T(8,128)S(1)}, f32[2,400,400]{2,1,0:T(8,128)}, u32[]{:S(2)}) copy-start(f32[2,400,400]{2,1,0:T(8,128)} %ops.5) | copy-start | bytes 3840004
  55.6 1.7 %collective-permute-start.21 = (f32[4,160,128]{2,1,0:T(8,128)S(1)}, f32[4,160,128]{2,1,0:T(8,128)S(1)}, u32[]{:S(2)}, u32[]{:S(2)}) collective-permute-start(f32[4,160,128]{2,1,0:T(8,128)S(1)} %join_far.1.far), channel_id=1, source_target_pairs={{0,4},{4,0},{8,12},{12,8},{16,20},{20,16},{24,28},{28,24},{1,5},{5... | collective-permute-start | bytes 983048 | tf_op jit(solution)/shard_map/ppermute | solution.py:270

commit v3 on v2

--- a/solution.py
+++ b/solution.py
@@ -63,7 +63,7 @@
         ops_low[i] = low
 
 
-def left_kernel(after, left, ops_high, ops_low, pick, rel, x_high, x_low, unit, scale, turned_high, turned_low):
+def left_kernel(after, left, ops_high, ops_low, pick, rel, x_high, x_low, unit, scale, turned):
     high, low = cut(left[...])
     xh = mul(high, pick[...], NN).astype(BF16)
     xl = mul(low, pick[...], NN).astype(BF16)
@@ -77,8 +77,7 @@
     unit[...] = u
     scale[...] = inv
     high, low = cut(jnp.transpose(u))
-    turned_high[...] = high
-    turned_low[...] = low
+    turned[...] = jnp.concatenate([high, high, low], axis=1)
 
 
 def operator_grad(which, relations, d_high, d_low, x, out):
@@ -98,13 +97,13 @@
 
 
 def right_kernel(
-    after, right, unit, scale, turned_high, turned_low, weight, hit, live, rel, x_high, x_low,
+    after, right, unit, scale, turned, weight, hit, live, rel, x_high, x_low,
     send, d_high, d_low, p_high, p_low,
 ):
     r = right[...]
     split = cut(r)
     inv = lax.rsqrt(jnp.sum(r * r, axis=0, keepdims=True) + EPS)
-    scores = mul3((turned_high[...], turned_low[...]), split, NN) * inv
+    scores = mul(turned[...], jnp.concatenate([split[0], split[1], split[0]], axis=0), NN) * inv
     weighted = jnp.exp(scores) * weight[...]
     total = jnp.sum(weighted, axis=1, keepdims=True)
     push = weighted * (live[...] / total) - hit[...]
@@ -188,12 +187,17 @@
 
 def join_kernel(*refs, after=0):
     out = refs[-1]
-    for j, ref in zip(walk_of(out.shape[0]), refs[after:]):
+    direct, distant = peers_of(out.shape[0])
+    rest = refs[after + len(direct):-1]
+    for j, ref in zip(direct, refs[after:]):
         out[jnp.bitwise_xor(chip(), j)] = ref[...]
-
-
-def copy_kernel(after, value, out):
-    out[...] = value[...]
+    for i, j in enumerate(distant):
+        out[jnp.bitwise_xor(chip(), j)] = rest[0][i] if len(rest[0].shape) == 3 else rest[i][...]
+
+
+def stack_kernel(*refs):
+    for i, ref in enumerate(refs[:-1]):
+        refs[-1][i] = ref[...]
 
 
 def operator_rows(which, ops, sums, near, far, flat, out, finish):
@@ -219,20 +223,17 @@
         finish(block)
 
 
-def own_operator_kernel(ops, sums, near, far, out, flat):
-    operator_rows(core(), ops, sums, near, far, flat, out, lambda block: None)
-
-
-def operator_kernel(own, ops, sums, near, far, out, flat, half, sem):
-    copies = [pltpu.make_async_copy(own, out.at[core()], sem.at[0])]
-    copies[0].start()
+def operator_kernel(ops, sums, near, far, *refs, own):
+    out, flat, half, sem = refs[-4:]
+    which = core() if own else 1 - core()
+    copies = []
 
     def finish(block):
-        target = out.at[1 - core(), block, :]
+        target = out.at[which, block, :]
         copies.append(pltpu.make_async_copy(half.at[block, :], target, sem.at[len(copies)]))
         copies[-1].start()
 
-    operator_rows(1 - core(), ops, sums, near, far, flat, half, finish)
+    operator_rows(which, ops, sums, near, far, flat, half, finish)
     for copy in copies:
         copy.wait()
 
@@ -243,17 +244,21 @@
 
 VMEM = pl.BlockSpec(memory_space=pltpu.VMEM)
 ANY = pl.BlockSpec(memory_space=pl.ANY)
+HBM = pl.BlockSpec(memory_space=pltpu.HBM)
 SMEM = pl.BlockSpec(memory_space=pltpu.SMEM)
 
 
-def run(kernel, out_shape, scalars, *args, after=(), scratch=(), out_specs=None, flops=0, size=2**20, name=None):
+def run(kernel, out_shape, scalars, *args, after=(), scratch=(), out_specs=None, in_place=False, flops=0, size=2**20, name=None):
     specs = [SMEM] * len(scalars) + [ANY] * len(after) + [VMEM] * len(args)
+    if in_place:
+        specs[-1] = HBM
     return pl.pallas_call(
         kernel,
         out_shape=out_shape,
         in_specs=specs,
         out_specs=out_specs or jax.tree.map(lambda _: VMEM, out_shape),
         scratch_shapes=scratch,
+        input_output_aliases={len(specs) - 1: 0} if in_place else {},
         compiler_params=pltpu.CompilerParams(vmem_limit_bytes=24 * 2**20),
         cost_estimate=pl.CostEstimate(flops=flops, bytes_accessed=size, transcendentals=0),
         name=name,
@@ -276,10 +281,6 @@
 
 def peers_of(count):
     return [j for j in range(count) if j.bit_count() < 2], [j for j in range(count) if j.bit_count() > 1]
-
-
-def walk_of(count):
-    return [j ^ (j // 2) for j in range(count)]
 
 
 def across_chips(value, j):
@@ -304,7 +305,7 @@
     right_sum = around(right_state[0], "rhs", 1)
     rel = relations[0]
     wide = shaped((w, slots), BF16)
-    turned = shaped((slots, w), BF16)
+    turned = shaped((slots, 3 * w), BF16)
     cross = shaped((slots, rows))
     halves = shaped(operators.shape, BF16)
     pick, weight, hit, live, column, ops_high, ops_low = run(
@@ -313,16 +314,16 @@
          halves, halves],
         [counts], sources[0], targets[0], negatives[0], operators, operator_state, name="prepare",
     )
-    x_high, x_low, unit, scale, turned_high, turned_low = run(
+    x_high, x_low, unit, scale, turned = run(
         left_kernel,
-        [wide, wide, shaped((w, slots)), shaped((1, slots)), turned, turned],
+        [wide, wide, shaped((w, slots)), shaped((1, slots)), turned],
         [], left, ops_high, ops_low, pick, rel, after=[left_sum], flops=2 * 10**9, name="left_side",
     )
     square = shaped((slots, rows), BF16)
     send, d_high, d_low, p_high, p_low = run(
         right_kernel,
         [shaped((packed, LANES)), wide, wide, square, square],
-        [], right, unit, scale, turned_high, turned_low, weight, hit, live, rel, x_high, x_low,
+        [], right, unit, scale, turned, weight, hit, live, rel, x_high, x_low,
         after=[right_sum], flops=3 * 10**9, name="right_side",
     )
     got = across_cores(send)
@@ -363,32 +364,37 @@
         bit, after = 2 * bit, []
     next_layer = swap(mine, "rhs", 1)
 
+    distant_parts = [across_chips(mine, j) for j in distant]
+    if len(distant) > 1:
+        handed = [swap(run(stack_kernel, bundle, [], *distant_parts, name="stack_distant"), "rhs", 1)]
+    else:
+        handed = [swap(t, "rhs", 1) for t in distant_parts]
+
     def spread(value):
-        taken = [value]
-        for j in walk_of(chips)[1:]:
-            taken.append(run(copy_kernel, part, [], across_chips(value, j), after=taken[-1:], name="take"))
-        return taken
+        return [value] + [across_chips(value, j) for j in direct[1:]]
 
     joined = shaped((chips, *part.shape))
-    near = run(join_kernel, joined, [], *spread(mine), name="join_near")
+    near = run(join_kernel, joined, [], *spread(mine), *distant_parts, name="join_near")
     new_right, done_right = run(
         right_update_kernel, [shaped((w, rows)), done],
         [], right, right_sum, unit, p_high, p_low,
         after=[near], size=0, name="right_update",
     )
     far = run(
-        functools.partial(join_kernel, after=1), joined, [], *spread(next_layer), after=[done_right], name="join_far",
+        functools.partial(join_kernel, after=1), joined, [], *spread(next_layer), *handed, after=[done_right], name="join_far",
     )
     other_near, other_far = across_cores(near), across_cores(far)
-    flat = [pltpu.VMEM((packed, LANES), F32)]
-    own = run(
-        own_operator_kernel, shaped(operators.shape[1:]), [], operators, column, near, far,
-        scratch=flat, name="own_operator",
+    scratch = [
+        pltpu.VMEM((packed, LANES), F32), pltpu.VMEM(operators.shape[1:], F32), pltpu.SemaphoreType.DMA((2,)),
+    ]
+    half_done = run(
+        functools.partial(operator_kernel, own=True), shaped(operators.shape), [], operators, column, near, far,
+        scratch=scratch, out_specs=HBM, name="own_operator",
     )
     new_operators = run(
-        operator_kernel, shaped(operators.shape), [], own, operators, column, other_near, other_far,
-        scratch=[*flat, pltpu.VMEM(operators.shape[1:], F32), pltpu.SemaphoreType.DMA((3,))],
-        out_specs=ANY, name="operator_update",
+        functools.partial(operator_kernel, own=False), shaped(operators.shape),
+        [], operators, column, other_near, other_far, half_done,
+        scratch=scratch, out_specs=HBM, in_place=True, name="operator_update",
     )
     return (
         jnp.swapaxes(new_left, 0, 1)[None, None],

time: 58.9 us -> 57.8 us (0.981)
  waiting for transfers between devices: 13.5 us -> 11.6 us
  Pallas kernels: 13 us -> 14 us
    ppermute x18, waiting for transfers between devices: 8.1 us -> 6.42 us  [swap(): return lax.ppermute(value, axis, [(i, i ^ bit) for i in range(count)])]
    pallas_call x21 -> x15, Pallas kernels: 13 us -> 14 us  [run(): pl.pallas_call(kernel, out_shape=out_shape, in_specs=specs, out_specs=out...]
  transfers between devices with their start and end apart: 22 -> 22, of which waited for: 11 -> 10; matrix products, arithmetic and copies ran while one was open for 0% -> 0% of each run, Pallas kernels for 15% -> 18%
where the time goes in v3:
time: 57.8 us; the launch traced here: 57.5 us
  starting transfers between devices  26.3 us (46%)
  Pallas kernels  14 us (24%)
  waiting for transfers between devices  11.6 us (20%)
  local copies, waits for them, and re-layouts  4.16 us (7%)
  between operations  1.44 us (2%)
    ppermute x18, starting transfers between devices, swap(): return lax.ppermute(value, axis, [(i, i ^ bit) for i in range(count)])  20.3 us
    pallas_call x15, Pallas kernels, run(): pl.pallas_call(kernel, out_shape=out_shape, in_specs=specs, out_specs=out...  14 us
    ppermute x18, waiting for transfers between devices, swap(): return lax.ppermute(value, axis, [(i, i ^ bit) for i in range(count)])  6.42 us
    ppermute x4, starting transfers between devices, around(): lax.ppermute(value, axis, [(i, (i + steps) % count) for i in range(count)])  5.98 us
    ppermute x4, waiting for transfers between devices, around(): lax.ppermute(value, axis, [(i, (i + steps) % count) for i in range(count)])  5.19 us
    unnamed x14, local copies, waits for them, and re-layouts  4.16 us
  transfers between devices with their start and end apart: 22, of which 10 were waited for; matrix products, arithmetic and copies ran while one was open for 0% of the time, Pallas kernels for 18%

profile of v3, /device:TPU:0, one launch (start us, length us, event | category | flops | bytes accessed | tf_op | source)
XLA Modules:
  0.0 57.5 jit_solution(4224854626425511068)
XLA Ops:
  0.6 0.0 copy-start.6
  0.6 0.5 collective-permute-start.3
  1.1 2.6 %collective-permute-start.1 = (f32[400,384]{1,0:T(8,128)}, f32[400,384]{1,0:T(8,128)S(1)}, u32[]{:S(2)}, u32[]{:S(2)}) collective-permute-start(f32[400,384]{1,0:T(8,128)} %bitcast.30), channel_id=1, source_target_pairs={{0,1},{1,2},{2,3},{3,0},{4,5},{5,6},{6,7},{7,4},{8,9},{9,10},{10,1... | collective-permute-start | bytes 1843208 | tf_op jit(solution)/shard_map/ppermute | solution.py:270
  3.8 1.3 %collective-permute-start.2 = (f32[1,384]{1,0:T(1,128)}, f32[1,384]{1,0:T(1,128)S(1)}, u32[]{:S(2)}, u32[]{:S(2)}) collective-permute-start(f32[1,384]{1,0:T(1,128)} %bitcast.32), channel_id=1, source_target_pairs={{0,4},{4,8},{8,12},{12,16},{16,20},{20,24},{24,28},{28,0},{1,5},{5... | collective-permute-start | bytes 4616 | tf_op jit(solution)/shard_map/ppermute | solution.py:270
  5.0 1.6 %collective-permute-start = (f32[1,384]{1,0:T(1,128)}, f32[1,384]{1,0:T(1,128)S(1)}, u32[]{:S(2)}, u32[]{:S(2)}) collective-permute-start(f32[1,384]{1,0:T(1,128)} %bitcast.33), channel_id=1, source_target_pairs={{0,1},{1,2},{2,3},{3,0},{4,5},{5,6},{6,7},{7,4},{8,9},{9,10},{10,1... | collective-permute-start | bytes 4616 | tf_op jit(solution)/shard_map/ppermute | solution.py:270
  7.3 0.0 copy-start
  7.3 1.4 %copy-done = f32[2,400,400]{2,1,0:T(8,128)S(1)} copy-done((f32[2,400,400]{2,1,0:T(8,128)S(1)}, f32[2,400,400]{2,1,0:T(8,128)}, u32[]{:S(2)}) %copy-start) | copy-done | bytes 1280024
  8.7 0.7 %copy-done.2 = f32[2,400]{1,0:T(2,128)S(1)} copy-done((f32[2,400]{1,0:T(2,128)S(1)}, f32[2,400]{1,0:T(2,128)}, u32[]{:S(2)}) %copy-start.2) | copy-done | bytes 3224
  9.4 0.0 copy-start.3
  9.4 0.7 %copy-done.3 = s32[1,1,384]{2,1,0:T(1,128)S(1)} copy-done((s32[1,1,384]{2,1,0:T(1,128)S(1)}, s32[1,1,384]{2,1,0:T(1,128)}, u32[]{:S(2)}) %copy-start.3) | copy-done | bytes 1560
  10.1 0.7 %copy-done.4 = s32[1,1,384]{2,1,0:T(1,128)S(1)} copy-done((s32[1,1,384]{2,1,0:T(1,128)S(1)}, s32[1,1,384]{2,1,0:T(1,128)}, u32[]{:S(2)}) %copy-start.4) | copy-done | bytes 1560
  10.8 0.7 %copy-done.5 = s32[1,1,384]{2,1,0:T(1,128)S(1)} copy-done((s32[1,1,384]{2,1,0:T(1,128)S(1)}, s32[1,1,384]{2,1,0:T(1,128)}, u32[]{:S(2)}) %copy-start.5) | copy-done | bytes 1560
  11.4 0.8 %prepare.1 = (bf16[384,384]{1,0:T(8,128)(2,1)S(1)}, f32[384,384]{1,0:T(8,128)S(1)}, f32[384,384]{1,0:T(8,128)S(1)}, f32[384,1]{1,0:T(8,128)S(1)}, f32[2,400,1]{2...) custom-call(s32[1,1]{1,0:T(1,128)S(6)} %copy.16.count, s32[1,384]{1,0:T(1,128)S(1)} %bitcast.22, ...), custom_call_target="tpu_custom_call" | custom-call | bytes 1048576 | tf_op jit(solution)/shard_map/prepare/pallas_call | solution.py:255
  12.3 0.0 collective-permute-done.2.after.left_sum
  12.3 0.0 collective-permute-done.3.left
  12.3 0.0 copy-done.6
  12.3 2.4 %left_side.1 = (bf16[400,384]{1,0:T(8,128)(2,1)S(1)}, bf16[400,384]{1,0:T(8,128)(2,1)S(1)}, f32[400,384]{1,0:T(8,128)S(1)}, f32[1,384]{1,0:T(1,128)S(1)}, bf16[384,1200]{1,0:T(8,128)(2,1)S(1)}) custom-call(f32[1,384]{1,0:T(1,128)S(1)} %collective-permute-done.2.after.left_sum, f32[400,384]{1,0:T(8,128)S(1)} %collective-permute-done.3.left, ...), custom_call_target="tpu_custom_call" | custom-call | flops 2000000000 | bytes 1048576 | tf_op jit(solution)/shard_map/left_side/pallas_call | solution.py:255
  14.8 5.2 %collective-permute-done.after.right_sum = f32[1,384]{1,0:T(1,128)S(1)} collective-permute-done((f32[1,384]{1,0:T(1,128)}, f32[1,384]{1,0:T(1,128)S(1)}, u32[]{:S(2)}, u32[]{:S(2)}) %collective-permute-start) | collective-permute-done | bytes 1568 | tf_op jit(solution)/shard_map/ppermute | solution.py:270
  19.9 0.0 collective-permute-done.1.right
  19.9 2.5 %right_side.1 = (f32[1280,128]{1,0:T(8,128)S(1)}, bf16[400,384]{1,0:T(8,128)(2,1)S(1)}, bf16[400,384]{1,0:T(8,128)(2,1)S(1)}, bf16[384,384]{1,0:T(8,128)(2,1)S(1)}, bf16[384,384]{1,0:T(8,128)(2,1)S(1)}) custom-call(f32[1,384]{1,0:T(1,128)S(1)} %collective-permute-done.after.right_sum, f32[400,384]{1,0:T(8,128)S(1)} %collective-permute-done.1.right, ...), custom_call_target="tpu_custom_call" | custom-call | flops 3000000000 | bytes 1048576 | tf_op jit(solution)/shard_map/right_side/pallas_call | solution.py:255
  22.4 0.7 %collective-permute-start.4 = (f32[1280,128]{1,0:T(8,128)S(1)}, f32[1280,128]{1,0:T(8,128)S(1)}, u32[]{:S(2)}, u32[]{:S(2)}) collective-permute-start(f32[1280,128]{1,0:T(8,128)S(1)} %get-tuple-element.45), channel_id=1, source_target_pairs={{0,4},{4,0},{8,12},{12,8},{16,20},{20,16},{24,28},{28,24},{1,5},{5... | collective-permute-start | bytes 1966088 | tf_op jit(solution)/shard_map/ppermute | solution.py:275
  23.1 0.8 %own_relation.1 = f32[1280,128]{1,0:T(8,128)S(1)} custom-call(s32[1,384]{1,0:T(1,128)S(1)} %bitcast.27, bf16[400,384]{1,0:T(8,128)(2,1)S(1)} %get-tuple-element.43.d_high, bf16[400,384]{1,0:T(8,128)(2,1)S(1)} %get-tuple-element.44.d_low, bf16[400,384]{1,0:T(8,128)(2,1)S(1)} %get-tuple-element.41.x_high, bf16[400,384]{1,0:T(8,128)(2,1)S(1)} %get-tuple-element.42.x_low), custom_call_target="tpu_custom_call" | custom-call | flops 1000000000 | bytes 1048576 | tf_op jit(solution)/shard_map/own_relation/pallas_call | solution.py:255
  23.9 1.0 %collective-permute-done.4 = f32[1280,128]{1,0:T(8,128)S(1)} collective-permute-done((f32[1280,128]{1,0:T(8,128)S(1)}, f32[1280,128]{1,0:T(8,128)S(1)}, u32[]{:S(2)}, u32[]{:S(2)}) %collective-permute-start.4) | collective-permute-done | bytes 655392 | tf_op jit(solution)/shard_map/ppermute | solution.py:275
  24.8 0.1 sum_cores.1
  24.9 0.1 collective-permute-start.7
  25.0 1.8 %collective-permute-start.9 = (f32[160,128]{1,0:T(8,128)S(1)}, f32[160,128]{1,0:T(8,128)S(1)}, u32[]{:S(2)}, u32[]{:S(2)}) collective-permute-start(f32[160,128]{1,0:T(8,128)S(1)} %get-tuple-element.52), channel_id=1, source_target_pairs={{0,8},{4,12},{8,0},{12,4},{16,24},{20,28},{24,16},{28,20},{1,9},{5... | collective-permute-start | bytes 245768 | tf_op jit(solution)/shard_map/ppermute | solution.py:275
  26.8 1.7 %collective-permute-start.10 = (f32[160,128]{1,0:T(8,128)S(1)}, f32[160,128]{1,0:T(8,128)S(1)}, u32[]{:S(2)}, u32[]{:S(2)}) collective-permute-start(f32[160,128]{1,0:T(8,128)S(1)} %get-tuple-element.53), channel_id=1, source_target_pairs={{0,16},{4,20},{8,24},{12,28},{16,0},{20,4},{24,8},{28,12},{1,17},{... | collective-permute-start | bytes 245768 | tf_op jit(solution)/shard_map/ppermute | solution.py:275
  28.4 0.4 collective-permute-start.5
  28.8 0.3 collective-permute-start.6
  29.1 0.6 %collective-permute-done.7.two = f32[1,160,128]{2,1,0:T(8,128)S(1)} collective-permute-done((f32[1,160,128]{2,1,0:T(8,128)S(1)}, f32[1,160,128]{2,1,0:T(8,128)S(1)}, u32[]{:S(2)}, u32[]{:S(2)}) %collective-permute-start.7) | collective-permute-done | bytes 81952 | tf_op jit(solution)/shard_map/ppermute | solution.py:275
  29.7 2.7 %collective-permute-start.8 = (f32[160,128]{1,0:T(8,128)S(1)}, f32[160,128]{1,0:T(8,128)S(1)}, u32[]{:S(2)}, u32[]{:S(2)}) collective-permute-start(f32[160,128]{1,0:T(8,128)S(1)} %merge_layers.1.refs_0_), channel_id=1, source_target_pairs={{0,24},{4,28},{8,16},{12,20},{16,8},{20,12},{24,0},{28,4},{1,25},{... | collective-permute-start | bytes 245768 | tf_op jit(solution)/shard_map/ppermute | solution.py:275
  32.4 0.0 collective-permute-done.9.refs_2_
  32.4 0.0 collective-permute-done.10.refs_3_
  32.4 1.7 %collective-permute-start.11 = (f32[160,128]{1,0:T(8,128)S(1)}, f32[160,128]{1,0:T(8,128)S(1)}, u32[]{:S(2)}, u32[]{:S(2)}) collective-permute-start(f32[160,128]{1,0:T(8,128)S(1)} %sum_away.1), channel_id=1, source_target_pairs={{0,1},{1,0},{2,3},{3,2},{4,5},{5,4},{6,7},{7,6},{8,9},{9,8},{10,11... | collective-permute-start | bytes 245768 | tf_op jit(solution)/shard_map/ppermute | solution.py:275
  34.1 0.0 collective-permute-done.5.refs_1_
  34.1 0.1 collective-permute-done.6.refs_2_
  34.1 1.0 %collective-permute-done.8.refs_3_ = f32[160,128]{1,0:T(8,128)S(1)} collective-permute-done((f32[160,128]{1,0:T(8,128)S(1)}, f32[160,128]{1,0:T(8,128)S(1)}, u32[]{:S(2)}, u32[]{:S(2)}) %collective-permute-start.8) | collective-permute-done | bytes 81952 | tf_op jit(solution)/shard_map/ppermute | solution.py:275
  35.1 1.8 %collective-permute-done.11.refs_4_ = f32[160,128]{1,0:T(8,128)S(1)} collective-permute-done((f32[160,128]{1,0:T(8,128)S(1)}, f32[160,128]{1,0:T(8,128)S(1)}, u32[]{:S(2)}, u32[]{:S(2)}) %collective-permute-start.11) | collective-permute-done | bytes 81952 | tf_op jit(solution)/shard_map/ppermute | solution.py:275
  36.9 1.9 %collective-permute-start.12 = (f32[160,128]{1,0:T(8,128)S(1)}, f32[160,128]{1,0:T(8,128)S(1)}, u32[]{:S(2)}, u32[]{:S(2)}) collective-permute-start(f32[160,128]{1,0:T(8,128)S(1)} %sum_home.1.after.refs_1_), channel_id=1, source_target_pairs={{0,2},{1,3},{2,0},{3,1},{4,6},{5,7},{6,4},{7,5},{8,10},{9,11},{10,... | collective-permute-start | bytes 245768 | tf_op jit(solution)/shard_map/ppermute | solution.py:275
  38.9 2.8 %left_update.1 = (f32[400,384]{1,0:T(8,128)}, f32[8,128]{1,0:T(8,128)S(1)}) custom-call(f32[160,128]{1,0:T(8,128)S(1)} %sum_home.1.after.refs_1_, f32[400,384]{1,0:T(8,128)S(1)} %collective-permute-done.3.left, f32[1,384]{1,0:T(1,128)S(1)} %collective-permute-done.2.after.left_sum, bf16[2,400,400]{2,1,0:T(8,128)(2,1)S(1)} %get-tuple-element.32.ops_high, ...), custom_call_target="tpu_custom_call" | custom-call | flops 2000000000 | bytes 1048576 | tf_op jit(solution)/shard_map/left_update/pallas_call | solution.py:255
  41.7 0.6 %collective-permute-done.12.refs_2_ = f32[160,128]{1,0:T(8,128)S(1)} collective-permute-done((f32[160,128]{1,0:T(8,128)S(1)}, f32[160,128]{1,0:T(8,128)S(1)}, u32[]{:S(2)}, u32[]{:S(2)}) %collective-permute-start.12) | collective-permute-done | bytes 81952 | tf_op jit(solution)/shard_map/ppermute | solution.py:275
  42.3 0.0 copy-start.1
  42.4 2.2 %collective-permute-start.17 = (f32[160,128]{1,0:T(8,128)S(1)}, f32[160,128]{1,0:T(8,128)S(1)}, u32[]{:S(2)}, u32[]{:S(2)}) collective-permute-start(f32[160,128]{1,0:T(8,128)S(1)} %sum_layers.1.refs_0_), channel_id=1, source_target_pairs={{0,1},{1,0},{2,3},{3,2},{4,5},{5,4},{6,7},{7,6},{8,9},{9,8},{10,11... | collective-permute-start | bytes 245768 | tf_op jit(solution)/shard_map/ppermute | solution.py:275
  44.5 1.4 %collective-permute-start.15 = (f32[160,128]{1,0:T(8,128)S(1)}, f32[160,128]{1,0:T(8,128)S(1)}, u32[]{:S(2)}, u32[]{:S(2)}) collective-permute-start(f32[160,128]{1,0:T(8,128)S(1)} %sum_layers.1.refs_0_), channel_id=1, source_target_pairs={{0,24},{4,28},{8,16},{12,20},{16,8},{20,12},{24,0},{28,4},{1,25},{... | collective-permute-start | bytes 245768 | tf_op jit(solution)/shard_map/ppermute | solution.py:275
  46.0 0.2 collective-permute-start.14
  46.1 1.9 %collective-permute-start.13 = (f32[160,128]{1,0:T(8,128)S(1)}, f32[160,128]{1,0:T(8,128)S(1)}, u32[]{:S(2)}, u32[]{:S(2)}) collective-permute-start(f32[160,128]{1,0:T(8,128)S(1)} %sum_layers.1.refs_0_), channel_id=1, source_target_pairs={{0,8},{4,12},{8,0},{12,4},{16,24},{20,28},{24,16},{28,20},{1,9},{5... | collective-permute-start | bytes 245768 | tf_op jit(solution)/shard_map/ppermute | solution.py:275
  48.0 0.0 collective-permute-done.17.refs_1_
  48.0 1.6 %collective-permute-start.19 = (f32[160,128]{1,0:T(8,128)S(1)}, f32[160,128]{1,0:T(8,128)S(1)}, u32[]{:S(2)}, u32[]{:S(2)}) collective-permute-start(f32[160,128]{1,0:T(8,128)S(1)} %collective-permute-done.17.refs_1_), channel_id=1, source_target_pairs={{0,16},{4,20},{8,24},{12,28},{16,0},{20,4},{24,8},{28,12},{1,17},{... | collective-permute-start | bytes 245768 | tf_op jit(solution)/shard_map/ppermute | solution.py:275
  49.6 0.4 collective-permute-start.18
  50.0 0.0 collective-permute-done.15.refs_3_
  50.0 1.4 %collective-permute-start.20 = (f32[160,128]{1,0:T(8,128)S(1)}, f32[160,128]{1,0:T(8,128)S(1)}, u32[]{:S(2)}, u32[]{:S(2)}) collective-permute-start(f32[160,128]{1,0:T(8,128)S(1)} %collective-permute-done.15.refs_3_), channel_id=1, source_target_pairs={{0,1},{1,0},{2,3},{3,2},{4,5},{5,4},{6,7},{7,6},{8,9},{9,8},{10,11... | collective-permute-start | bytes 245768 | tf_op jit(solution)/shard_map/ppermute | solution.py:275
  51.4 0.0 collective-permute-done.14.refs_2_
  51.4 0.0 collective-permute-done.13.refs_1_
  51.4 0.1 collective-permute-start.16
  51.5 1.8 %right_update.1 = (f32[400,384]{1,0:T(8,128)}, f32[8,128]{1,0:T(8,128)S(1)}) custom-call(f32[4,160,128]{2,1,0:T(8,128)S(1)} %join_near.1.after.near, f32[400,384]{1,0:T(8,128)S(1)} %collective-permute-done.1.right, f32[1,384]{1,0:T(1,128)S(1)} %collective-permute-done.after.right_sum, f32[400,384]{1,0:T(8,128)S(1)} %get-tuple-element.35.unit, ...), custom_call_target="tpu_custom_call" | custom-call | tf_op jit(solution)/shard_map/right_update/pallas_call | solution.py:255
  53.3 0.0 collective-permute-done.19.refs_3_
  53.3 0.7 %collective-permute-done.18.refs_2_ = f32[160,128]{1,0:T(8,128)S(1)} collective-permute-done((f32[160,128]{1,0:T(8,128)S(1)}, f32[160,128]{1,0:T(8,128)S(1)}, u32[]{:S(2)}, u32[]{:S(2)}) %collective-permute-start.18) | collective-permute-done | bytes 81952 | tf_op jit(solution)/shard_map/ppermute | solution.py:275
  54.0 0.4 collective-permute-done.20.refs_4_
  54.5 0.1 collective-permute-start.21
  54.6 0.0 copy-done.1
  54.6 1.3 %own_operator.1.refs_0_ = f32[2,400,400]{2,1,0:T(8,128)} custom-call(f32[2,400,400]{2,1,0:T(8,128)S(1)} %copy-done.1, f32[2,400,1]{2,1,0:T(8,128)S(1)} %get-tuple-element.59.sums, f32[4,160,128]{2,1,0:T(8,128)S(1)} %join_near.1.after.near, f32[4,160,128]{2,1,0:T(8,128)S(1)} %join_far.1.far), custom_call_target="tpu_custom_call" | custom-call | bytes 1048576 | tf_op jit(solution)/shard_map/own_operator/pallas_call | solution.py:255
  55.9 0.0 collective-permute-done.16.near
  55.9 0.3 collective-permute-done.21.far
  56.2 1.3 %operator_update.1 = f32[2,400,400]{2,1,0:T(8,128)} custom-call(f32[2,400,400]{2,1,0:T(8,128)S(1)} %copy-done.1, f32[2,400,1]{2,1,0:T(8,128)S(1)} %get-tuple-element.59.sums, f32[4,160,128]{2,1,0:T(8,128)S(1)} %collective-permute-done.16.near, f32[4,160,128]{2,1,0:T(8,128)S(1)} %collective-permute-done.21.far, ...), custom_call_target="tpu_custom_call", output_to_operand_aliasing={{}: (4, {})} | custom-call | bytes 1048576 | tf_op jit(solution)/shard_map/operator_update/pallas_call | solution.py:255
  (9 shorter events, 0.1 us)
Async XLA Ops:
  0.6 11.7 %copy-start.6 = (s32[1,1,384]{2,1,0:T(1,128)S(1)}, s32[1,1,384]{2,1,0:T(1,128)}, u32[]{:S(2)}) copy-start(s32[1,1,384]{2,1,0:T(1,128)} %param.19) | copy-start | bytes 4612
  0.6 11.7 %collective-permute-start.3 = (f32[400,384]{1,0:T(8,128)}, f32[400,384]{1,0:T(8,128)S(1)}, u32[]{:S(2)}, u32[]{:S(2)}) collective-permute-start(f32[400,384]{1,0:T(8,128)} %bitcast.29), channel_id=1, source_target_pairs={{0,4},{4,8},{8,12},{12,16},{16,20},{20,24},{24,28},{28,0},{1,5},{5... | collective-permute-start | bytes 1843208 | tf_op jit(solution)/shard_map/ppermute | solution.py:270
  1.1 18.8 %collective-permute-start.1 = (f32[400,384]{1,0:T(8,128)}, f32[400,384]{1,0:T(8,128)S(1)}, u32[]{:S(2)}, u32[]{:S(2)}) collective-permute-start(f32[400,384]{1,0:T(8,128)} %bitcast.30), channel_id=1, source_target_pairs={{0,1},{1,2},{2,3},{3,0},{4,5},{5,6},{6,7},{7,4},{8,9},{9,10},{10,1... | collective-permute-start | bytes 1843208 | tf_op jit(solution)/shard_map/ppermute | solution.py:270
  3.8 8.5 %collective-permute-start.2 = (f32[1,384]{1,0:T(1,128)}, f32[1,384]{1,0:T(1,128)S(1)}, u32[]{:S(2)}, u32[]{:S(2)}) collective-permute-start(f32[1,384]{1,0:T(1,128)} %bitcast.32), channel_id=1, source_target_pairs={{0,4},{4,8},{8,12},{12,16},{16,20},{20,24},{24,28},{28,0},{1,5},{5... | collective-permute-start | bytes 4616 | tf_op jit(solution)/shard_map/ppermute | solution.py:270
  5.0 14.9 %collective-permute-start = (f32[1,384]{1,0:T(1,128)}, f32[1,384]{1,0:T(1,128)S(1)}, u32[]{:S(2)}, u32[]{:S(2)}) collective-permute-start(f32[1,384]{1,0:T(1,128)} %bitcast.33), channel_id=1, source_target_pairs={{0,1},{1,2},{2,3},{3,0},{4,5},{5,6},{6,7},{7,4},{8,9},{9,10},{10,1... | collective-permute-start | bytes 4616 | tf_op jit(solution)/shard_map/ppermute | solution.py:270
  7.3 1.4 %copy-start = (f32[2,400,400]{2,1,0:T(8,128)S(1)}, f32[2,400,400]{2,1,0:T(8,128)}, u32[]{:S(2)}) copy-start(f32[2,400,400]{2,1,0:T(8,128)} %ops.5) | copy-start | bytes 3840004
  8.7 0.7 %copy-start.2 = (f32[2,400]{1,0:T(2,128)S(1)}, f32[2,400]{1,0:T(2,128)}, u32[]{:S(2)}) copy-start(f32[2,400]{1,0:T(2,128)} %op_sums.1) | copy-start | bytes 9604
  9.4 0.7 %copy-start.3 = (s32[1,1,384]{2,1,0:T(1,128)S(1)}, s32[1,1,384]{2,1,0:T(1,128)}, u32[]{:S(2)}) copy-start(s32[1,1,384]{2,1,0:T(1,128)} %param.17) | copy-start | bytes 4612
  10.1 0.7 %copy-start.4 = (s32[1,1,384]{2,1,0:T(1,128)S(1)}, s32[1,1,384]{2,1,0:T(1,128)}, u32[]{:S(2)}) copy-start(s32[1,1,384]{2,1,0:T(1,128)} %param.18) | copy-start | bytes 4612
  10.8 0.7 %copy-start.5 = (s32[1,1,384]{2,1,0:T(1,128)S(1)}, s32[1,1,384]{2,1,0:T(1,128)}, u32[]{:S(2)}) copy-start(s32[1,1,384]{2,1,0:T(1,128)} %param.20) | copy-start | bytes 4612
  22.4 2.4 %collective-permute-start.4 = (f32[1280,128]{1,0:T(8,128)S(1)}, f32[1280,128]{1,0:T(8,128)S(1)}, u32[]{:S(2)}, u32[]{:S(2)}) collective-permute-start(f32[1280,128]{1,0:T(8,128)S(1)} %get-tuple-element.45), channel_id=1, source_target_pairs={{0,4},{4,0},{8,12},{12,8},{16,20},{20,16},{24,28},{28,24},{1,5},{5... | collective-permute-start | bytes 1966088 | tf_op jit(solution)/shard_map/ppermute | solution.py:275
  24.9 4.8 %collective-permute-start.7 = (f32[1,160,128]{2,1,0:T(8,128)S(1)}, f32[1,160,128]{2,1,0:T(8,128)S(1)}, u32[]{:S(2)}, u32[]{:S(2)}) collective-permute-start(f32[1,160,128]{2,1,0:T(8,128)S(1)} %get-tuple-element.50), channel_id=1, source_target_pairs={{0,1},{1,0},{2,3},{3,2},{4,5},{5,4},{6,7},{7,6},{8,9},{9,8},{10,11... | collective-permute-start | bytes 245768 | tf_op jit(solution)/shard_map/ppermute | solution.py:275
  25.0 7.4 %collective-permute-start.9 = (f32[160,128]{1,0:T(8,128)S(1)}, f32[160,128]{1,0:T(8,128)S(1)}, u32[]{:S(2)}, u32[]{:S(2)}) collective-permute-start(f32[160,128]{1,0:T(8,128)S(1)} %get-tuple-element.52), channel_id=1, source_target_pairs={{0,8},{4,12},{8,0},{12,4},{16,24},{20,28},{24,16},{28,20},{1,9},{5... | collective-permute-start | bytes 245768 | tf_op jit(solution)/shard_map/ppermute | solution.py:275
  26.8 5.6 %collective-permute-start.10 = (f32[160,128]{1,0:T(8,128)S(1)}, f32[160,128]{1,0:T(8,128)S(1)}, u32[]{:S(2)}, u32[]{:S(2)}) collective-permute-start(f32[160,128]{1,0:T(8,128)S(1)} %get-tuple-element.53), channel_id=1, source_target_pairs={{0,16},{4,20},{8,24},{12,28},{16,0},{20,4},{24,8},{28,12},{1,17},{... | collective-permute-start | bytes 245768 | tf_op jit(solution)/shard_map/ppermute | solution.py:275
  28.4 5.6 %collective-permute-start.5 = (f32[160,128]{1,0:T(8,128)S(1)}, f32[160,128]{1,0:T(8,128)S(1)}, u32[]{:S(2)}, u32[]{:S(2)}) collective-permute-start(f32[160,128]{1,0:T(8,128)S(1)} %get-tuple-element.47), channel_id=1, source_target_pairs={{0,8},{4,12},{8,0},{12,4},{16,24},{20,28},{24,16},{28,20},{1,9},{5... | collective-permute-start | bytes 245768 | tf_op jit(solution)/shard_map/ppermute | solution.py:275
  28.8 5.3 %collective-permute-start.6 = (f32[160,128]{1,0:T(8,128)S(1)}, f32[160,128]{1,0:T(8,128)S(1)}, u32[]{:S(2)}, u32[]{:S(2)}) collective-permute-start(f32[160,128]{1,0:T(8,128)S(1)} %get-tuple-element.48), channel_id=1, source_target_pairs={{0,16},{4,20},{8,24},{12,28},{16,0},{20,4},{24,8},{28,12},{1,17},{... | collective-permute-start | bytes 245768 | tf_op jit(solution)/shard_map/ppermute | solution.py:275
  29.7 5.4 %collective-permute-start.8 = (f32[160,128]{1,0:T(8,128)S(1)}, f32[160,128]{1,0:T(8,128)S(1)}, u32[]{:S(2)}, u32[]{:S(2)}) collective-permute-start(f32[160,128]{1,0:T(8,128)S(1)} %merge_layers.1.refs_0_), channel_id=1, source_target_pairs={{0,24},{4,28},{8,16},{12,20},{16,8},{20,12},{24,0},{28,4},{1,25},{... | collective-permute-start | bytes 245768 | tf_op jit(solution)/shard_map/ppermute | solution.py:275
  32.4 4.5 %collective-permute-start.11 = (f32[160,128]{1,0:T(8,128)S(1)}, f32[160,128]{1,0:T(8,128)S(1)}, u32[]{:S(2)}, u32[]{:S(2)}) collective-permute-start(f32[160,128]{1,0:T(8,128)S(1)} %sum_away.1), channel_id=1, source_target_pairs={{0,1},{1,0},{2,3},{3,2},{4,5},{5,4},{6,7},{7,6},{8,9},{9,8},{10,11... | collective-permute-start | bytes 245768 | tf_op jit(solution)/shard_map/ppermute | solution.py:275
  36.9 5.4 %collective-permute-start.12 = (f32[160,128]{1,0:T(8,128)S(1)}, f32[160,128]{1,0:T(8,128)S(1)}, u32[]{:S(2)}, u32[]{:S(2)}) collective-permute-start(f32[160,128]{1,0:T(8,128)S(1)} %sum_home.1.after.refs_1_), channel_id=1, source_target_pairs={{0,2},{1,3},{2,0},{3,1},{4,6},{5,7},{6,4},{7,5},{8,10},{9,11},{10,... | collective-permute-start | bytes 245768 | tf_op jit(solution)/shard_map/ppermute | solution.py:275
  42.3 12.2 %copy-start.1 = (f32[2,400,400]{2,1,0:T(8,128)S(1)}, f32[2,400,400]{2,1,0:T(8,128)}, u32[]{:S(2)}) copy-start(f32[2,400,400]{2,1,0:T(8,128)} %ops.5) | copy-start | bytes 3840004
  42.4 5.7 %collective-permute-start.17 = (f32[160,128]{1,0:T(8,128)S(1)}, f32[160,128]{1,0:T(8,128)S(1)}, u32[]{:S(2)}, u32[]{:S(2)}) collective-permute-start(f32[160,128]{1,0:T(8,128)S(1)} %sum_layers.1.refs_0_), channel_id=1, source_target_pairs={{0,1},{1,0},{2,3},{3,2},{4,5},{5,4},{6,7},{7,6},{8,9},{9,8},{10,11... | collective-permute-start | bytes 245768 | tf_op jit(solution)/shard_map/ppermute | solution.py:275
  44.5 5.5 %collective-permute-start.15 = (f32[160,128]{1,0:T(8,128)S(1)}, f32[160,128]{1,0:T(8,128)S(1)}, u32[]{:S(2)}, u32[]{:S(2)}) collective-permute-start(f32[160,128]{1,0:T(8,128)S(1)} %sum_layers.1.refs_0_), channel_id=1, source_target_pairs={{0,24},{4,28},{8,16},{12,20},{16,8},{20,12},{24,0},{28,4},{1,25},{... | collective-permute-start | bytes 245768 | tf_op jit(solution)/shard_map/ppermute | solution.py:275
  46.0 5.4 %collective-permute-start.14 = (f32[160,128]{1,0:T(8,128)S(1)}, f32[160,128]{1,0:T(8,128)S(1)}, u32[]{:S(2)}, u32[]{:S(2)}) collective-permute-start(f32[160,128]{1,0:T(8,128)S(1)} %sum_layers.1.refs_0_), channel_id=1, source_target_pairs={{0,16},{4,20},{8,24},{12,28},{16,0},{20,4},{24,8},{28,12},{1,17},{... | collective-permute-start | bytes 245768 | tf_op jit(solution)/shard_map/ppermute | solution.py:275
  46.1 5.3 %collective-permute-start.13 = (f32[160,128]{1,0:T(8,128)S(1)}, f32[160,128]{1,0:T(8,128)S(1)}, u32[]{:S(2)}, u32[]{:S(2)}) collective-permute-start(f32[160,128]{1,0:T(8,128)S(1)} %sum_layers.1.refs_0_), channel_id=1, source_target_pairs={{0,8},{4,12},{8,0},{12,4},{16,24},{20,28},{24,16},{28,20},{1,9},{5... | collective-permute-start | bytes 245768 | tf_op jit(solution)/shard_map/ppermute | solution.py:275
  48.0 5.3 %collective-permute-start.19 = (f32[160,128]{1,0:T(8,128)S(1)}, f32[160,128]{1,0:T(8,128)S(1)}, u32[]{:S(2)}, u32[]{:S(2)}) collective-permute-start(f32[160,128]{1,0:T(8,128)S(1)} %collective-permute-done.17.refs_1_), channel_id=1, source_target_pairs={{0,16},{4,20},{8,24},{12,28},{16,0},{20,4},{24,8},{28,12},{1,17},{... | collective-permute-start | bytes 245768 | tf_op jit(solution)/shard_map/ppermute | solution.py:275
  49.6 4.4 %collective-permute-start.18 = (f32[160,128]{1,0:T(8,128)S(1)}, f32[160,128]{1,0:T(8,128)S(1)}, u32[]{:S(2)}, u32[]{:S(2)}) collective-permute-start(f32[160,128]{1,0:T(8,128)S(1)} %collective-permute-done.17.refs_1_), channel_id=1, source_target_pairs={{0,8},{4,12},{8,0},{12,4},{16,24},{20,28},{24,16},{28,20},{1,9},{5... | collective-permute-start | bytes 245768 | tf_op jit(solution)/shard_map/ppermute | solution.py:275
  50.0 4.4 %collective-permute-start.20 = (f32[160,128]{1,0:T(8,128)S(1)}, f32[160,128]{1,0:T(8,128)S(1)}, u32[]{:S(2)}, u32[]{:S(2)}) collective-permute-start(f32[160,128]{1,0:T(8,128)S(1)} %collective-permute-done.15.refs_3_), channel_id=1, source_target_pairs={{0,1},{1,0},{2,3},{3,2},{4,5},{5,4},{6,7},{7,6},{8,9},{9,8},{10,11... | collective-permute-start | bytes 245768 | tf_op jit(solution)/shard_map/ppermute | solution.py:275
  51.4 4.5 %collective-permute-start.16 = (f32[4,160,128]{2,1,0:T(8,128)S(1)}, f32[4,160,128]{2,1,0:T(8,128)S(1)}, u32[]{:S(2)}, u32[]{:S(2)}) collective-permute-start(f32[4,160,128]{2,1,0:T(8,128)S(1)} %join_near.1.after.near), channel_id=1, source_target_pairs={{0,4},{4,0},{8,12},{12,8},{16,20},{20,16},{24,28},{28,24},{1,5},{5... | collective-permute-start | bytes 983048 | tf_op jit(solution)/shard_map/ppermute | solution.py:275
  54.5 1.7 %collective-permute-start.21 = (f32[4,160,128]{2,1,0:T(8,128)S(1)}, f32[4,160,128]{2,1,0:T(8,128)S(1)}, u32[]{:S(2)}, u32[]{:S(2)}) collective-permute-start(f32[4,160,128]{2,1,0:T(8,128)S(1)} %join_far.1.far), channel_id=1, source_target_pairs={{0,4},{4,0},{8,12},{12,8},{16,20},{20,16},{24,28},{28,24},{1,5},{5... | collective-permute-start | bytes 983048 | tf_op jit(solution)/shard_map/ppermute | solution.py:275

commit v4 on v3

--- a/solution.py
+++ b/solution.py
@@ -160,6 +160,11 @@
     return lax.rem(lax.axis_index("rhs"), 2)
 
 
+def by_core(direct):
+    first = core() == 0
+    return [0] + [jnp.where(first, a, b) for a, b in zip(direct[1:], direct[:0:-1])]
+
+
 def deal_kernel(one, two, *outs):
     direct, distant = peers_of(one.shape[0])
     for half, own in enumerate((1 - side(), side())):
@@ -169,7 +174,7 @@
             spot = jnp.bitwise_xor(chip(), j)
             return one[spot, own] + two[spot, own]
 
-        for j, out in zip(direct, own_outs):
+        for j, out in zip(by_core(direct), own_outs):
             out[...] = part(j)
         for i, j in enumerate(distant):
             own_outs[len(direct)][i] = part(j)
@@ -189,7 +194,7 @@
     out = refs[-1]
     direct, distant = peers_of(out.shape[0])
     rest = refs[after + len(direct):-1]
-    for j, ref in zip(direct, refs[after:]):
+    for j, ref in zip(by_core(direct), refs[after:]):
         out[jnp.bitwise_xor(chip(), j)] = ref[...]
     for i, j in enumerate(distant):
         out[jnp.bitwise_xor(chip(), j)] = rest[0][i] if len(rest[0].shape) == 3 else rest[i][...]
@@ -287,6 +292,12 @@
     return swap(value, "lhs", 2 * j)
 
 
+def across_direct(value, spot):
+    count = lax.axis_size("lhs")
+    direct = peers_of(count // 2)[0]
+    return lax.ppermute(value, "lhs", [(i, i ^ (2 * direct[spot if i % 2 == 0 else -spot])) for i in range(count)])
+
+
 def body(
     left_table, left_state, right_table, right_state, operators, operator_state,
     sources, targets, relations, negatives, counts,
@@ -343,8 +354,9 @@
     merged = run(
         merge_kernel, [part] * len(distant), [], dealt[-1], swap(dealt[len(direct)], "rhs", 1), name="merge_layers",
     )
-    away = [away[0]] + [across_chips(t, j) for j, t in zip(direct[1:], away[1:])]
-    home = [home[0]] + [across_chips(t, j) for j, t in zip(direct[1:] + distant, home[1:] + merged)]
+    away = [away[0]] + [across_direct(t, i + 1) for i, t in enumerate(away[1:])]
+    home = [home[0]] + [across_direct(t, i + 1) for i, t in enumerate(home[1:])]
+    home += [across_chips(t, j) for j, t in zip(distant, merged)]
     passed = run(functools.partial(sum_kernel, after=1), part, [], *away, after=merged[:1], name="sum_away")
     done = shaped((8, LANES))
     mine = run(
@@ -371,7 +383,7 @@
         handed = [swap(t, "rhs", 1) for t in distant_parts]
 
     def spread(value):
-        return [value] + [across_chips(value, j) for j in direct[1:]]
+        return [value] + [across_direct(value, i) for i in range(1, len(direct))]
 
     joined = shaped((chips, *part.shape))
     near = run(join_kernel, joined, [], *spread(mine), *distant_parts, name="join_near")

time: 57.8 us -> 57.6 us (level)
  starting transfers between devices: 26.3 us -> 24.8 us
  waiting for transfers between devices: 11.6 us -> 13 us
    ppermute x18 -> x10, starting transfers between devices: 20.3 us -> 10.6 us  [swap(): return lax.ppermute(value, axis, [(i, i ^ bit) for i in range(count)])]
    ppermute x0 -> x8, starting transfers between devices: none -> 8.16 us  [across_direct(): lax.ppermute(value, 'lhs', [(i, i ^ 2 * direct[spot if i % 2 == 0 else -s...]
    ppermute x0 -> x8, waiting for transfers between devices: none -> 1.15 us  [across_direct(): lax.ppermute(value, 'lhs', [(i, i ^ 2 * direct[spot if i % 2 == 0 else -s...]
    ppermute x18 -> x10, waiting for transfers between devices: 6.42 us -> 6.64 us  [swap(): return lax.ppermute(value, axis, [(i, i ^ bit) for i in range(count)])]
  transfers between devices with their start and end apart: 22 -> 22, of which waited for: 10 -> 11; matrix products, arithmetic and copies ran while one was open for 0% -> 0% of each run, Pallas kernels for 18% -> 18%
where the time goes in v4:
time: 57.6 us; the launch traced here: 57.3 us
  starting transfers between devices  24.8 us (43%)
  Pallas kernels  14 us (24%)
  waiting for transfers between devices  13 us (23%)
  local copies, waits for them, and re-layouts  4.16 us (7%)
  between operations  1.44 us (2%)
    pallas_call x15, Pallas kernels, run(): pl.pallas_call(kernel, out_shape=out_shape, in_specs=specs, out_specs=out...  14 us
    ppermute x10, starting transfers between devices, swap(): return lax.ppermute(value, axis, [(i, i ^ bit) for i in range(count)])  10.6 us
    ppermute x8, starting transfers between devices, across_direct(): lax.ppermute(value, 'lhs', [(i, i ^ 2 * direct[spot if i % 2 == 0 else -s...  8.16 us
    ppermute x10, waiting for transfers between devices, swap(): return lax.ppermute(value, axis, [(i, i ^ bit) for i in range(count)])  6.64 us
    ppermute x4, starting transfers between devices, around(): lax.ppermute(value, axis, [(i, (i + steps) % count) for i in range(count)])  5.98 us
    ppermute x4, waiting for transfers between devices, around(): lax.ppermute(value, axis, [(i, (i + steps) % count) for i in range(count)])  5.19 us
    unnamed x14, local copies, waits for them, and re-layouts  4.16 us
  transfers between devices with their start and end apart: 22, of which 11 were waited for; matrix products, arithmetic and copies ran while one was open for 0% of the time, Pallas kernels for 18%

profile of v4, /device:TPU:0, one launch (start us, length us, event | category | flops | bytes accessed | tf_op | source)
XLA Modules:
  0.0 57.3 jit_solution(11699404027928785612)
XLA Ops:
  0.6 0.0 copy-start.6
  0.6 0.5 collective-permute-start.3
  1.1 2.6 %collective-permute-start.1 = (f32[400,384]{1,0:T(8,128)}, f32[400,384]{1,0:T(8,128)S(1)}, u32[]{:S(2)}, u32[]{:S(2)}) collective-permute-start(f32[400,384]{1,0:T(8,128)} %bitcast.30), channel_id=1, source_target_pairs={{0,1},{1,2},{2,3},{3,0},{4,5},{5,6},{6,7},{7,4},{8,9},{9,10},{10,1... | collective-permute-start | bytes 1843208 | tf_op jit(solution)/shard_map/ppermute | solution.py:275
  3.8 1.3 %collective-permute-start.2 = (f32[1,384]{1,0:T(1,128)}, f32[1,384]{1,0:T(1,128)S(1)}, u32[]{:S(2)}, u32[]{:S(2)}) collective-permute-start(f32[1,384]{1,0:T(1,128)} %bitcast.32), channel_id=1, source_target_pairs={{0,4},{4,8},{8,12},{12,16},{16,20},{20,24},{24,28},{28,0},{1,5},{5... | collective-permute-start | bytes 4616 | tf_op jit(solution)/shard_map/ppermute | solution.py:275
  5.0 1.6 %collective-permute-start = (f32[1,384]{1,0:T(1,128)}, f32[1,384]{1,0:T(1,128)S(1)}, u32[]{:S(2)}, u32[]{:S(2)}) collective-permute-start(f32[1,384]{1,0:T(1,128)} %bitcast.33), channel_id=1, source_target_pairs={{0,1},{1,2},{2,3},{3,0},{4,5},{5,6},{6,7},{7,4},{8,9},{9,10},{10,1... | collective-permute-start | bytes 4616 | tf_op jit(solution)/shard_map/ppermute | solution.py:275
  7.3 0.0 copy-start
  7.3 1.4 %copy-done = f32[2,400,400]{2,1,0:T(8,128)S(1)} copy-done((f32[2,400,400]{2,1,0:T(8,128)S(1)}, f32[2,400,400]{2,1,0:T(8,128)}, u32[]{:S(2)}) %copy-start) | copy-done | bytes 1280024
  8.7 0.0 copy-start.2
  8.7 0.7 %copy-done.2 = f32[2,400]{1,0:T(2,128)S(1)} copy-done((f32[2,400]{1,0:T(2,128)S(1)}, f32[2,400]{1,0:T(2,128)}, u32[]{:S(2)}) %copy-start.2) | copy-done | bytes 3224
  9.4 0.7 %copy-done.3 = s32[1,1,384]{2,1,0:T(1,128)S(1)} copy-done((s32[1,1,384]{2,1,0:T(1,128)S(1)}, s32[1,1,384]{2,1,0:T(1,128)}, u32[]{:S(2)}) %copy-start.3) | copy-done | bytes 1560
  10.1 0.7 %copy-done.4 = s32[1,1,384]{2,1,0:T(1,128)S(1)} copy-done((s32[1,1,384]{2,1,0:T(1,128)S(1)}, s32[1,1,384]{2,1,0:T(1,128)}, u32[]{:S(2)}) %copy-start.4) | copy-done | bytes 1560
  10.8 0.7 %copy-done.5 = s32[1,1,384]{2,1,0:T(1,128)S(1)} copy-done((s32[1,1,384]{2,1,0:T(1,128)S(1)}, s32[1,1,384]{2,1,0:T(1,128)}, u32[]{:S(2)}) %copy-start.5) | copy-done | bytes 1560
  11.4 0.8 %prepare.1 = (bf16[384,384]{1,0:T(8,128)(2,1)S(1)}, f32[384,384]{1,0:T(8,128)S(1)}, f32[384,384]{1,0:T(8,128)S(1)}, f32[384,1]{1,0:T(8,128)S(1)}, f32[2,400,1]{2...) custom-call(s32[1,1]{1,0:T(1,128)S(6)} %copy.16.count, s32[1,384]{1,0:T(1,128)S(1)} %bitcast.22, ...), custom_call_target="tpu_custom_call" | custom-call | bytes 1048576 | tf_op jit(solution)/shard_map/prepare/pallas_call | solution.py:260
  12.3 0.0 collective-permute-done.2.after.left_sum
  12.3 0.0 collective-permute-done.3.left
  12.3 0.0 copy-done.6
  12.3 2.4 %left_side.1 = (bf16[400,384]{1,0:T(8,128)(2,1)S(1)}, bf16[400,384]{1,0:T(8,128)(2,1)S(1)}, f32[400,384]{1,0:T(8,128)S(1)}, f32[1,384]{1,0:T(1,128)S(1)}, bf16[384,1200]{1,0:T(8,128)(2,1)S(1)}) custom-call(f32[1,384]{1,0:T(1,128)S(1)} %collective-permute-done.2.after.left_sum, f32[400,384]{1,0:T(8,128)S(1)} %collective-permute-done.3.left, ...), custom_call_target="tpu_custom_call" | custom-call | flops 2000000000 | bytes 1048576 | tf_op jit(solution)/shard_map/left_side/pallas_call | solution.py:260
  14.8 5.2 %collective-permute-done.after.right_sum = f32[1,384]{1,0:T(1,128)S(1)} collective-permute-done((f32[1,384]{1,0:T(1,128)}, f32[1,384]{1,0:T(1,128)S(1)}, u32[]{:S(2)}, u32[]{:S(2)}) %collective-permute-start) | collective-permute-done | bytes 1568 | tf_op jit(solution)/shard_map/ppermute | solution.py:275
  19.9 0.0 collective-permute-done.1.right
  19.9 2.5 %right_side.1 = (f32[1280,128]{1,0:T(8,128)S(1)}, bf16[400,384]{1,0:T(8,128)(2,1)S(1)}, bf16[400,384]{1,0:T(8,128)(2,1)S(1)}, bf16[384,384]{1,0:T(8,128)(2,1)S(1)}, bf16[384,384]{1,0:T(8,128)(2,1)S(1)}) custom-call(f32[1,384]{1,0:T(1,128)S(1)} %collective-permute-done.after.right_sum, f32[400,384]{1,0:T(8,128)S(1)} %collective-permute-done.1.right, ...), custom_call_target="tpu_custom_call" | custom-call | flops 3000000000 | bytes 1048576 | tf_op jit(solution)/shard_map/right_side/pallas_call | solution.py:260
  22.4 0.7 %collective-permute-start.4 = (f32[1280,128]{1,0:T(8,128)S(1)}, f32[1280,128]{1,0:T(8,128)S(1)}, u32[]{:S(2)}, u32[]{:S(2)}) collective-permute-start(f32[1280,128]{1,0:T(8,128)S(1)} %get-tuple-element.45), channel_id=1, source_target_pairs={{0,4},{4,0},{8,12},{12,8},{16,20},{20,16},{24,28},{28,24},{1,5},{5... | collective-permute-start | bytes 1966088 | tf_op jit(solution)/shard_map/ppermute | solution.py:280
  23.1 0.8 %own_relation.1 = f32[1280,128]{1,0:T(8,128)S(1)} custom-call(s32[1,384]{1,0:T(1,128)S(1)} %bitcast.27, bf16[400,384]{1,0:T(8,128)(2,1)S(1)} %get-tuple-element.43.d_high, bf16[400,384]{1,0:T(8,128)(2,1)S(1)} %get-tuple-element.44.d_low, bf16[400,384]{1,0:T(8,128)(2,1)S(1)} %get-tuple-element.41.x_high, bf16[400,384]{1,0:T(8,128)(2,1)S(1)} %get-tuple-element.42.x_low), custom_call_target="tpu_custom_call" | custom-call | flops 1000000000 | bytes 1048576 | tf_op jit(solution)/shard_map/own_relation/pallas_call | solution.py:260
  23.9 1.0 %collective-permute-done.4 = f32[1280,128]{1,0:T(8,128)S(1)} collective-permute-done((f32[1280,128]{1,0:T(8,128)S(1)}, f32[1280,128]{1,0:T(8,128)S(1)}, u32[]{:S(2)}, u32[]{:S(2)}) %collective-permute-start.4) | collective-permute-done | bytes 655392 | tf_op jit(solution)/shard_map/ppermute | solution.py:280
  24.8 0.1 sum_cores.1
  24.9 0.1 collective-permute-start.7
  25.0 1.8 %collective-permute-start.9 = (f32[160,128]{1,0:T(8,128)S(1)}, f32[160,128]{1,0:T(8,128)S(1)}, u32[]{:S(2)}, u32[]{:S(2)}) collective-permute-start(f32[160,128]{1,0:T(8,128)S(1)} %get-tuple-element.52), channel_id=1, source_target_pairs={{0,8},{4,20},{8,0},{12,28},{16,24},{20,4},{24,16},{28,12},{1,9},{5... | collective-permute-start | bytes 245768 | tf_op jit(solution)/shard_map/ppermute | solution.py:298
  26.8 1.7 %collective-permute-start.10 = (f32[160,128]{1,0:T(8,128)S(1)}, f32[160,128]{1,0:T(8,128)S(1)}, u32[]{:S(2)}, u32[]{:S(2)}) collective-permute-start(f32[160,128]{1,0:T(8,128)S(1)} %get-tuple-element.53), channel_id=1, source_target_pairs={{0,16},{4,12},{8,24},{12,4},{16,0},{20,28},{24,8},{28,20},{1,17},{... | collective-permute-start | bytes 245768 | tf_op jit(solution)/shard_map/ppermute | solution.py:298
  28.4 0.4 collective-permute-start.5
  28.8 0.3 collective-permute-start.6
  29.1 0.6 %collective-permute-done.7.two = f32[1,160,128]{2,1,0:T(8,128)S(1)} collective-permute-done((f32[1,160,128]{2,1,0:T(8,128)S(1)}, f32[1,160,128]{2,1,0:T(8,128)S(1)}, u32[]{:S(2)}, u32[]{:S(2)}) %collective-permute-start.7) | collective-permute-done | bytes 81952 | tf_op jit(solution)/shard_map/ppermute | solution.py:280
  29.7 2.7 %collective-permute-start.8 = (f32[160,128]{1,0:T(8,128)S(1)}, f32[160,128]{1,0:T(8,128)S(1)}, u32[]{:S(2)}, u32[]{:S(2)}) collective-permute-start(f32[160,128]{1,0:T(8,128)S(1)} %merge_layers.1.refs_0_), channel_id=1, source_target_pairs={{0,24},{4,28},{8,16},{12,20},{16,8},{20,12},{24,0},{28,4},{1,25},{... | collective-permute-start | bytes 245768 | tf_op jit(solution)/shard_map/ppermute | solution.py:280
  32.4 0.0 collective-permute-done.9.refs_2_
  32.4 0.0 collective-permute-done.10.refs_3_
  32.4 1.7 %collective-permute-start.11 = (f32[160,128]{1,0:T(8,128)S(1)}, f32[160,128]{1,0:T(8,128)S(1)}, u32[]{:S(2)}, u32[]{:S(2)}) collective-permute-start(f32[160,128]{1,0:T(8,128)S(1)} %sum_away.1), channel_id=1, source_target_pairs={{0,1},{1,0},{2,3},{3,2},{4,5},{5,4},{6,7},{7,6},{8,9},{9,8},{10,11... | collective-permute-start | bytes 245768 | tf_op jit(solution)/shard_map/ppermute | solution.py:280
  34.1 0.0 collective-permute-done.5.refs_1_
  34.1 0.0 collective-permute-done.6.refs_2_
  34.1 1.2 %collective-permute-done.8.refs_3_ = f32[160,128]{1,0:T(8,128)S(1)} collective-permute-done((f32[160,128]{1,0:T(8,128)S(1)}, f32[160,128]{1,0:T(8,128)S(1)}, u32[]{:S(2)}, u32[]{:S(2)}) %collective-permute-start.8) | collective-permute-done | bytes 81952 | tf_op jit(solution)/shard_map/ppermute | solution.py:280
  35.3 1.6 %collective-permute-done.11.refs_4_ = f32[160,128]{1,0:T(8,128)S(1)} collective-permute-done((f32[160,128]{1,0:T(8,128)S(1)}, f32[160,128]{1,0:T(8,128)S(1)}, u32[]{:S(2)}, u32[]{:S(2)}) %collective-permute-start.11) | collective-permute-done | bytes 81952 | tf_op jit(solution)/shard_map/ppermute | solution.py:280
  36.9 2.0 %collective-permute-start.12 = (f32[160,128]{1,0:T(8,128)S(1)}, f32[160,128]{1,0:T(8,128)S(1)}, u32[]{:S(2)}, u32[]{:S(2)}) collective-permute-start(f32[160,128]{1,0:T(8,128)S(1)} %sum_home.1.after.refs_1_), channel_id=1, source_target_pairs={{0,2},{1,3},{2,0},{3,1},{4,6},{5,7},{6,4},{7,5},{8,10},{9,11},{10,... | collective-permute-start | bytes 245768 | tf_op jit(solution)/shard_map/ppermute | solution.py:280
  38.9 2.8 %left_update.1 = (f32[400,384]{1,0:T(8,128)}, f32[8,128]{1,0:T(8,128)S(1)}) custom-call(f32[160,128]{1,0:T(8,128)S(1)} %sum_home.1.after.refs_1_, f32[400,384]{1,0:T(8,128)S(1)} %collective-permute-done.3.left, f32[1,384]{1,0:T(1,128)S(1)} %collective-permute-done.2.after.left_sum, bf16[2,400,400]{2,1,0:T(8,128)(2,1)S(1)} %get-tuple-element.32.ops_high, ...), custom_call_target="tpu_custom_call" | custom-call | flops 2000000000 | bytes 1048576 | tf_op jit(solution)/shard_map/left_update/pallas_call | solution.py:260
  41.8 0.6 %collective-permute-done.12.refs_2_ = f32[160,128]{1,0:T(8,128)S(1)} collective-permute-done((f32[160,128]{1,0:T(8,128)S(1)}, f32[160,128]{1,0:T(8,128)S(1)}, u32[]{:S(2)}, u32[]{:S(2)}) %collective-permute-start.12) | collective-permute-done | bytes 81952 | tf_op jit(solution)/shard_map/ppermute | solution.py:280
  42.4 0.0 copy-start.1
  42.4 2.0 %collective-permute-start.17 = (f32[160,128]{1,0:T(8,128)S(1)}, f32[160,128]{1,0:T(8,128)S(1)}, u32[]{:S(2)}, u32[]{:S(2)}) collective-permute-start(f32[160,128]{1,0:T(8,128)S(1)} %sum_layers.1.refs_0_), channel_id=1, source_target_pairs={{0,1},{1,0},{2,3},{3,2},{4,5},{5,4},{6,7},{7,6},{8,9},{9,8},{10,11... | collective-permute-start | bytes 245768 | tf_op jit(solution)/shard_map/ppermute | solution.py:280
  44.4 0.8 %collective-permute-start.15 = (f32[160,128]{1,0:T(8,128)S(1)}, f32[160,128]{1,0:T(8,128)S(1)}, u32[]{:S(2)}, u32[]{:S(2)}) collective-permute-start(f32[160,128]{1,0:T(8,128)S(1)} %sum_layers.1.refs_0_), channel_id=1, source_target_pairs={{0,24},{4,28},{8,16},{12,20},{16,8},{20,12},{24,0},{28,4},{1,25},{... | collective-permute-start | bytes 245768 | tf_op jit(solution)/shard_map/ppermute | solution.py:280
  45.2 0.8 %collective-permute-start.14 = (f32[160,128]{1,0:T(8,128)S(1)}, f32[160,128]{1,0:T(8,128)S(1)}, u32[]{:S(2)}, u32[]{:S(2)}) collective-permute-start(f32[160,128]{1,0:T(8,128)S(1)} %sum_layers.1.refs_0_), channel_id=1, source_target_pairs={{0,16},{4,12},{8,24},{12,4},{16,0},{20,28},{24,8},{28,20},{1,17},{... | collective-permute-start | bytes 245768 | tf_op jit(solution)/shard_map/ppermute | solution.py:298
  45.9 1.9 %collective-permute-start.13 = (f32[160,128]{1,0:T(8,128)S(1)}, f32[160,128]{1,0:T(8,128)S(1)}, u32[]{:S(2)}, u32[]{:S(2)}) collective-permute-start(f32[160,128]{1,0:T(8,128)S(1)} %sum_layers.1.refs_0_), channel_id=1, source_target_pairs={{0,8},{4,20},{8,0},{12,28},{16,24},{20,4},{24,16},{28,12},{1,9},{5... | collective-permute-start | bytes 245768 | tf_op jit(solution)/shard_map/ppermute | solution.py:298
  47.9 0.0 collective-permute-done.17.refs_1_
  47.9 1.1 %collective-permute-start.19 = (f32[160,128]{1,0:T(8,128)S(1)}, f32[160,128]{1,0:T(8,128)S(1)}, u32[]{:S(2)}, u32[]{:S(2)}) collective-permute-start(f32[160,128]{1,0:T(8,128)S(1)} %collective-permute-done.17.refs_1_), channel_id=1, source_target_pairs={{0,16},{4,12},{8,24},{12,4},{16,0},{20,28},{24,8},{28,20},{1,17},{... | collective-permute-start | bytes 245768 | tf_op jit(solution)/shard_map/ppermute | solution.py:298
  49.0 0.3 collective-permute-start.18
  49.2 0.6 %collective-permute-done.15.refs_3_ = f32[160,128]{1,0:T(8,128)S(1)} collective-permute-done((f32[160,128]{1,0:T(8,128)S(1)}, f32[160,128]{1,0:T(8,128)S(1)}, u32[]{:S(2)}, u32[]{:S(2)}) %collective-permute-start.15) | collective-permute-done | bytes 81952 | tf_op jit(solution)/shard_map/ppermute | solution.py:280
  49.8 0.5 collective-permute-start.20
  50.3 0.1 collective-permute-done.14.refs_2_
  50.5 0.0 collective-permute-done.13.refs_1_
  50.5 0.1 collective-permute-start.16
  50.6 1.8 %right_update.1 = (f32[400,384]{1,0:T(8,128)}, f32[8,128]{1,0:T(8,128)S(1)}) custom-call(f32[4,160,128]{2,1,0:T(8,128)S(1)} %join_near.1.after.near, f32[400,384]{1,0:T(8,128)S(1)} %collective-permute-done.1.right, f32[1,384]{1,0:T(1,128)S(1)} %collective-permute-done.after.right_sum, f32[400,384]{1,0:T(8,128)S(1)} %get-tuple-element.35.unit, ...), custom_call_target="tpu_custom_call" | custom-call | tf_op jit(solution)/shard_map/right_update/pallas_call | solution.py:260
  52.4 0.0 collective-permute-done.19.refs_3_
  52.4 1.0 %collective-permute-done.18.refs_2_ = f32[160,128]{1,0:T(8,128)S(1)} collective-permute-done((f32[160,128]{1,0:T(8,128)S(1)}, f32[160,128]{1,0:T(8,128)S(1)}, u32[]{:S(2)}, u32[]{:S(2)}) %collective-permute-start.18) | collective-permute-done | bytes 81952 | tf_op jit(solution)/shard_map/ppermute | solution.py:298
  53.4 0.9 %collective-permute-done.20.refs_4_ = f32[160,128]{1,0:T(8,128)S(1)} collective-permute-done((f32[160,128]{1,0:T(8,128)S(1)}, f32[160,128]{1,0:T(8,128)S(1)}, u32[]{:S(2)}, u32[]{:S(2)}) %collective-permute-start.20) | collective-permute-done | bytes 81952 | tf_op jit(solution)/shard_map/ppermute | solution.py:280
  54.3 0.1 collective-permute-start.21
  54.4 0.0 copy-done.1
  54.4 1.3 %own_operator.1.refs_0_ = f32[2,400,400]{2,1,0:T(8,128)} custom-call(f32[2,400,400]{2,1,0:T(8,128)S(1)} %copy-done.1, f32[2,400,1]{2,1,0:T(8,128)S(1)} %get-tuple-element.59.sums, f32[4,160,128]{2,1,0:T(8,128)S(1)} %join_near.1.after.near, f32[4,160,128]{2,1,0:T(8,128)S(1)} %join_far.1.far), custom_call_target="tpu_custom_call" | custom-call | bytes 1048576 | tf_op jit(solution)/shard_map/own_operator/pallas_call | solution.py:260
  55.7 0.0 collective-permute-done.16.near
  55.7 0.3 collective-permute-done.21.far
  56.0 1.3 %operator_update.1 = f32[2,400,400]{2,1,0:T(8,128)} custom-call(f32[2,400,400]{2,1,0:T(8,128)S(1)} %copy-done.1, f32[2,400,1]{2,1,0:T(8,128)S(1)} %get-tuple-element.59.sums, f32[4,160,128]{2,1,0:T(8,128)S(1)} %collective-permute-done.16.near, f32[4,160,128]{2,1,0:T(8,128)S(1)} %collective-permute-done.21.far, ...), custom_call_target="tpu_custom_call", output_to_operand_aliasing={{}: (4, {})} | custom-call | bytes 1048576 | tf_op jit(solution)/shard_map/operator_update/pallas_call | solution.py:260
  (9 shorter events, 0.1 us)
Async XLA Ops:
  0.6 11.7 %copy-start.6 = (s32[1,1,384]{2,1,0:T(1,128)S(1)}, s32[1,1,384]{2,1,0:T(1,128)}, u32[]{:S(2)}) copy-start(s32[1,1,384]{2,1,0:T(1,128)} %param.19) | copy-start | bytes 4612
  0.6 11.7 %collective-permute-start.3 = (f32[400,384]{1,0:T(8,128)}, f32[400,384]{1,0:T(8,128)S(1)}, u32[]{:S(2)}, u32[]{:S(2)}) collective-permute-start(f32[400,384]{1,0:T(8,128)} %bitcast.29), channel_id=1, source_target_pairs={{0,4},{4,8},{8,12},{12,16},{16,20},{20,24},{24,28},{28,0},{1,5},{5... | collective-permute-start | bytes 1843208 | tf_op jit(solution)/shard_map/ppermute | solution.py:275
  1.1 18.8 %collective-permute-start.1 = (f32[400,384]{1,0:T(8,128)}, f32[400,384]{1,0:T(8,128)S(1)}, u32[]{:S(2)}, u32[]{:S(2)}) collective-permute-start(f32[400,384]{1,0:T(8,128)} %bitcast.30), channel_id=1, source_target_pairs={{0,1},{1,2},{2,3},{3,0},{4,5},{5,6},{6,7},{7,4},{8,9},{9,10},{10,1... | collective-permute-start | bytes 1843208 | tf_op jit(solution)/shard_map/ppermute | solution.py:275
  3.8 8.5 %collective-permute-start.2 = (f32[1,384]{1,0:T(1,128)}, f32[1,384]{1,0:T(1,128)S(1)}, u32[]{:S(2)}, u32[]{:S(2)}) collective-permute-start(f32[1,384]{1,0:T(1,128)} %bitcast.32), channel_id=1, source_target_pairs={{0,4},{4,8},{8,12},{12,16},{16,20},{20,24},{24,28},{28,0},{1,5},{5... | collective-permute-start | bytes 4616 | tf_op jit(solution)/shard_map/ppermute | solution.py:275
  5.0 14.9 %collective-permute-start = (f32[1,384]{1,0:T(1,128)}, f32[1,384]{1,0:T(1,128)S(1)}, u32[]{:S(2)}, u32[]{:S(2)}) collective-permute-start(f32[1,384]{1,0:T(1,128)} %bitcast.33), channel_id=1, source_target_pairs={{0,1},{1,2},{2,3},{3,0},{4,5},{5,6},{6,7},{7,4},{8,9},{9,10},{10,1... | collective-permute-start | bytes 4616 | tf_op jit(solution)/shard_map/ppermute | solution.py:275
  7.3 1.4 %copy-start = (f32[2,400,400]{2,1,0:T(8,128)S(1)}, f32[2,400,400]{2,1,0:T(8,128)}, u32[]{:S(2)}) copy-start(f32[2,400,400]{2,1,0:T(8,128)} %ops.5) | copy-start | bytes 3840004
  8.7 0.7 %copy-start.2 = (f32[2,400]{1,0:T(2,128)S(1)}, f32[2,400]{1,0:T(2,128)}, u32[]{:S(2)}) copy-start(f32[2,400]{1,0:T(2,128)} %op_sums.1) | copy-start | bytes 9604
  9.4 0.7 %copy-start.3 = (s32[1,1,384]{2,1,0:T(1,128)S(1)}, s32[1,1,384]{2,1,0:T(1,128)}, u32[]{:S(2)}) copy-start(s32[1,1,384]{2,1,0:T(1,128)} %param.17) | copy-start | bytes 4612
  10.1 0.7 %copy-start.4 = (s32[1,1,384]{2,1,0:T(1,128)S(1)}, s32[1,1,384]{2,1,0:T(1,128)}, u32[]{:S(2)}) copy-start(s32[1,1,384]{2,1,0:T(1,128)} %param.18) | copy-start | bytes 4612
  10.8 0.7 %copy-start.5 = (s32[1,1,384]{2,1,0:T(1,128)S(1)}, s32[1,1,384]{2,1,0:T(1,128)}, u32[]{:S(2)}) copy-start(s32[1,1,384]{2,1,0:T(1,128)} %param.20) | copy-start | bytes 4612
  22.4 2.4 %collective-permute-start.4 = (f32[1280,128]{1,0:T(8,128)S(1)}, f32[1280,128]{1,0:T(8,128)S(1)}, u32[]{:S(2)}, u32[]{:S(2)}) collective-permute-start(f32[1280,128]{1,0:T(8,128)S(1)} %get-tuple-element.45), channel_id=1, source_target_pairs={{0,4},{4,0},{8,12},{12,8},{16,20},{20,16},{24,28},{28,24},{1,5},{5... | collective-permute-start | bytes 1966088 | tf_op jit(solution)/shard_map/ppermute | solution.py:280
  24.9 4.8 %collective-permute-start.7 = (f32[1,160,128]{2,1,0:T(8,128)S(1)}, f32[1,160,128]{2,1,0:T(8,128)S(1)}, u32[]{:S(2)}, u32[]{:S(2)}) collective-permute-start(f32[1,160,128]{2,1,0:T(8,128)S(1)} %get-tuple-element.50), channel_id=1, source_target_pairs={{0,1},{1,0},{2,3},{3,2},{4,5},{5,4},{6,7},{7,6},{8,9},{9,8},{10,11... | collective-permute-start | bytes 245768 | tf_op jit(solution)/shard_map/ppermute | solution.py:280
  25.0 7.4 %collective-permute-start.9 = (f32[160,128]{1,0:T(8,128)S(1)}, f32[160,128]{1,0:T(8,128)S(1)}, u32[]{:S(2)}, u32[]{:S(2)}) collective-permute-start(f32[160,128]{1,0:T(8,128)S(1)} %get-tuple-element.52), channel_id=1, source_target_pairs={{0,8},{4,20},{8,0},{12,28},{16,24},{20,4},{24,16},{28,12},{1,9},{5... | collective-permute-start | bytes 245768 | tf_op jit(solution)/shard_map/ppermute | solution.py:298
  26.8 5.6 %collective-permute-start.10 = (f32[160,128]{1,0:T(8,128)S(1)}, f32[160,128]{1,0:T(8,128)S(1)}, u32[]{:S(2)}, u32[]{:S(2)}) collective-permute-start(f32[160,128]{1,0:T(8,128)S(1)} %get-tuple-element.53), channel_id=1, source_target_pairs={{0,16},{4,12},{8,24},{12,4},{16,0},{20,28},{24,8},{28,20},{1,17},{... | collective-permute-start | bytes 245768 | tf_op jit(solution)/shard_map/ppermute | solution.py:298
  28.4 5.7 %collective-permute-start.5 = (f32[160,128]{1,0:T(8,128)S(1)}, f32[160,128]{1,0:T(8,128)S(1)}, u32[]{:S(2)}, u32[]{:S(2)}) collective-permute-start(f32[160,128]{1,0:T(8,128)S(1)} %get-tuple-element.47), channel_id=1, source_target_pairs={{0,8},{4,20},{8,0},{12,28},{16,24},{20,4},{24,16},{28,12},{1,9},{5... | collective-permute-start | bytes 245768 | tf_op jit(solution)/shard_map/ppermute | solution.py:298
  28.8 5.3 %collective-permute-start.6 = (f32[160,128]{1,0:T(8,128)S(1)}, f32[160,128]{1,0:T(8,128)S(1)}, u32[]{:S(2)}, u32[]{:S(2)}) collective-permute-start(f32[160,128]{1,0:T(8,128)S(1)} %get-tuple-element.48), channel_id=1, source_target_pairs={{0,16},{4,12},{8,24},{12,4},{16,0},{20,28},{24,8},{28,20},{1,17},{... | collective-permute-start | bytes 245768 | tf_op jit(solution)/shard_map/ppermute | solution.py:298
  29.7 5.6 %collective-permute-start.8 = (f32[160,128]{1,0:T(8,128)S(1)}, f32[160,128]{1,0:T(8,128)S(1)}, u32[]{:S(2)}, u32[]{:S(2)}) collective-permute-start(f32[160,128]{1,0:T(8,128)S(1)} %merge_layers.1.refs_0_), channel_id=1, source_target_pairs={{0,24},{4,28},{8,16},{12,20},{16,8},{20,12},{24,0},{28,4},{1,25},{... | collective-permute-start | bytes 245768 | tf_op jit(solution)/shard_map/ppermute | solution.py:280
  32.4 4.5 %collective-permute-start.11 = (f32[160,128]{1,0:T(8,128)S(1)}, f32[160,128]{1,0:T(8,128)S(1)}, u32[]{:S(2)}, u32[]{:S(2)}) collective-permute-start(f32[160,128]{1,0:T(8,128)S(1)} %sum_away.1), channel_id=1, source_target_pairs={{0,1},{1,0},{2,3},{3,2},{4,5},{5,4},{6,7},{7,6},{8,9},{9,8},{10,11... | collective-permute-start | bytes 245768 | tf_op jit(solution)/shard_map/ppermute | solution.py:280
  36.9 5.4 %collective-permute-start.12 = (f32[160,128]{1,0:T(8,128)S(1)}, f32[160,128]{1,0:T(8,128)S(1)}, u32[]{:S(2)}, u32[]{:S(2)}) collective-permute-start(f32[160,128]{1,0:T(8,128)S(1)} %sum_home.1.after.refs_1_), channel_id=1, source_target_pairs={{0,2},{1,3},{2,0},{3,1},{4,6},{5,7},{6,4},{7,5},{8,10},{9,11},{10,... | collective-permute-start | bytes 245768 | tf_op jit(solution)/shard_map/ppermute | solution.py:280
  42.4 12.0 %copy-start.1 = (f32[2,400,400]{2,1,0:T(8,128)S(1)}, f32[2,400,400]{2,1,0:T(8,128)}, u32[]{:S(2)}) copy-start(f32[2,400,400]{2,1,0:T(8,128)} %ops.5) | copy-start | bytes 3840004
  42.4 5.5 %collective-permute-start.17 = (f32[160,128]{1,0:T(8,128)S(1)}, f32[160,128]{1,0:T(8,128)S(1)}, u32[]{:S(2)}, u32[]{:S(2)}) collective-permute-start(f32[160,128]{1,0:T(8,128)S(1)} %sum_layers.1.refs_0_), channel_id=1, source_target_pairs={{0,1},{1,0},{2,3},{3,2},{4,5},{5,4},{6,7},{7,6},{8,9},{9,8},{10,11... | collective-permute-start | bytes 245768 | tf_op jit(solution)/shard_map/ppermute | solution.py:280
  44.4 5.4 %collective-permute-start.15 = (f32[160,128]{1,0:T(8,128)S(1)}, f32[160,128]{1,0:T(8,128)S(1)}, u32[]{:S(2)}, u32[]{:S(2)}) collective-permute-start(f32[160,128]{1,0:T(8,128)S(1)} %sum_layers.1.refs_0_), channel_id=1, source_target_pairs={{0,24},{4,28},{8,16},{12,20},{16,8},{20,12},{24,0},{28,4},{1,25},{... | collective-permute-start | bytes 245768 | tf_op jit(solution)/shard_map/ppermute | solution.py:280
  45.2 5.3 %collective-permute-start.14 = (f32[160,128]{1,0:T(8,128)S(1)}, f32[160,128]{1,0:T(8,128)S(1)}, u32[]{:S(2)}, u32[]{:S(2)}) collective-permute-start(f32[160,128]{1,0:T(8,128)S(1)} %sum_layers.1.refs_0_), channel_id=1, source_target_pairs={{0,16},{4,12},{8,24},{12,4},{16,0},{20,28},{24,8},{28,20},{1,17},{... | collective-permute-start | bytes 245768 | tf_op jit(solution)/shard_map/ppermute | solution.py:298
  45.9 4.5 %collective-permute-start.13 = (f32[160,128]{1,0:T(8,128)S(1)}, f32[160,128]{1,0:T(8,128)S(1)}, u32[]{:S(2)}, u32[]{:S(2)}) collective-permute-start(f32[160,128]{1,0:T(8,128)S(1)} %sum_layers.1.refs_0_), channel_id=1, source_target_pairs={{0,8},{4,20},{8,0},{12,28},{16,24},{20,4},{24,16},{28,12},{1,9},{5... | collective-permute-start | bytes 245768 | tf_op jit(solution)/shard_map/ppermute | solution.py:298
  47.9 4.5 %collective-permute-start.19 = (f32[160,128]{1,0:T(8,128)S(1)}, f32[160,128]{1,0:T(8,128)S(1)}, u32[]{:S(2)}, u32[]{:S(2)}) collective-permute-start(f32[160,128]{1,0:T(8,128)S(1)} %collective-permute-done.17.refs_1_), channel_id=1, source_target_pairs={{0,16},{4,12},{8,24},{12,4},{16,0},{20,28},{24,8},{28,20},{1,17},{... | collective-permute-start | bytes 245768 | tf_op jit(solution)/shard_map/ppermute | solution.py:298
  49.0 4.4 %collective-permute-start.18 = (f32[160,128]{1,0:T(8,128)S(1)}, f32[160,128]{1,0:T(8,128)S(1)}, u32[]{:S(2)}, u32[]{:S(2)}) collective-permute-start(f32[160,128]{1,0:T(8,128)S(1)} %collective-permute-done.17.refs_1_), channel_id=1, source_target_pairs={{0,8},{4,20},{8,0},{12,28},{16,24},{20,4},{24,16},{28,12},{1,9},{5... | collective-permute-start | bytes 245768 | tf_op jit(solution)/shard_map/ppermute | solution.py:298
  49.8 4.4 %collective-permute-start.20 = (f32[160,128]{1,0:T(8,128)S(1)}, f32[160,128]{1,0:T(8,128)S(1)}, u32[]{:S(2)}, u32[]{:S(2)}) collective-permute-start(f32[160,128]{1,0:T(8,128)S(1)} %collective-permute-done.15.refs_3_), channel_id=1, source_target_pairs={{0,1},{1,0},{2,3},{3,2},{4,5},{5,4},{6,7},{7,6},{8,9},{9,8},{10,11... | collective-permute-start | bytes 245768 | tf_op jit(solution)/shard_map/ppermute | solution.py:280
  50.5 5.2 %collective-permute-start.16 = (f32[4,160,128]{2,1,0:T(8,128)S(1)}, f32[4,160,128]{2,1,0:T(8,128)S(1)}, u32[]{:S(2)}, u32[]{:S(2)}) collective-permute-start(f32[4,160,128]{2,1,0:T(8,128)S(1)} %join_near.1.after.near), channel_id=1, source_target_pairs={{0,4},{4,0},{8,12},{12,8},{16,20},{20,16},{24,28},{28,24},{1,5},{5... | collective-permute-start | bytes 983048 | tf_op jit(solution)/shard_map/ppermute | solution.py:280
  54.3 1.7 %collective-permute-start.21 = (f32[4,160,128]{2,1,0:T(8,128)S(1)}, f32[4,160,128]{2,1,0:T(8,128)S(1)}, u32[]{:S(2)}, u32[]{:S(2)}) collective-permute-start(f32[4,160,128]{2,1,0:T(8,128)S(1)} %join_far.1.far), channel_id=1, source_target_pairs={{0,4},{4,0},{8,12},{12,8},{16,20},{20,16},{24,28},{28,24},{1,5},{5... | collective-permute-start | bytes 983048 | tf_op jit(solution)/shard_map/ppermute | solution.py:280

commit v5 on v4

--- a/solution.py
+++ b/solution.py
@@ -10,6 +10,7 @@
 F32 = jnp.float32
 BF16 = jnp.bfloat16
 LANES = 128
+BLOCKS = 4
 NN = ((1,), (0,))
 NT = ((1,), (1,))
 TN = ((0,), (0,))
@@ -98,7 +99,7 @@
 
 def right_kernel(
     after, right, unit, scale, turned, weight, hit, live, rel, x_high, x_low,
-    send, d_high, d_low, p_high, p_low,
+    send, d_high, d_low, pushes,
 ):
     r = right[...]
     split = cut(r)
@@ -107,7 +108,7 @@
     weighted = jnp.exp(scores) * weight[...]
     total = jnp.sum(weighted, axis=1, keepdims=True)
     push = weighted * (live[...] / total) - hit[...]
-    p_high[...], p_low[...] = cut(push)
+    pushes[...] = push
     du = deep3(split, cut(push * inv), NT)
     u = unit[...]
     along = jnp.sum(u * du, axis=0, keepdims=True)
@@ -138,11 +139,11 @@
     done[...] = jnp.zeros_like(done)
 
 
-def right_update_kernel(after, right, right_sum, unit, p_high, p_low, new_right, done):
+def right_update_kernel(after, right, right_sum, unit, pushes, new_right, done):
     r = right[...]
     inv = lax.rsqrt(jnp.sum(r * r, axis=0, keepdims=True) + EPS)
     v = r * inv
-    dv = deep3(cut(unit[...]), (p_high[...], p_low[...]), NN)
+    dv = deep3(cut(unit[...]), cut(pushes[...]), NN)
     grad = inv * (dv - v * jnp.sum(v * dv, axis=0, keepdims=True))
     new_right[...] = adagrad_t(r, right_sum[...], grad)
     done[...] = jnp.zeros_like(done)
@@ -221,7 +222,8 @@
     square = jnp.sum(tail * tail, axis=1, keepdims=True)
     square = square + jnp.sum(sum(tile * tile for tile in tiles), axis=1, keepdims=True)
     rate = 0.1 / jnp.sqrt(sums[which] + square / w)
-    for block in (slice(0, w // 16 * 8), slice(w // 16 * 8, w)):
+    cuts = [w * i // (8 * BLOCKS) * 8 for i in range(BLOCKS)] + [w]
+    for block in [slice(low, high) for low, high in zip(cuts, cuts[1:])]:
         for t, part in enumerate([*tiles, tail]):
             span = slice(t * LANES, min(w, (t + 1) * LANES))
             out[block, span] = ops[which, block, span] - part[block] * rate[block]
@@ -330,10 +332,9 @@
         [wide, wide, shaped((w, slots)), shaped((1, slots)), turned],
         [], left, ops_high, ops_low, pick, rel, after=[left_sum], flops=2 * 10**9, name="left_side",
     )
-    square = shaped((slots, rows), BF16)
-    send, d_high, d_low, p_high, p_low = run(
+    send, d_high, d_low, pushes = run(
         right_kernel,
-        [shaped((packed, LANES)), wide, wide, square, square],
+        [shaped((packed, LANES)), wide, wide, cross],
         [], right, unit, scale, turned, weight, hit, live, rel, x_high, x_low,
         after=[right_sum], flops=3 * 10**9, name="right_side",
     )
@@ -389,7 +390,7 @@
     near = run(join_kernel, joined, [], *spread(mine), *distant_parts, name="join_near")
     new_right, done_right = run(
         right_update_kernel, [shaped((w, rows)), done],
-        [], right, right_sum, unit, p_high, p_low,
+        [], right, right_sum, unit, pushes,
         after=[near], size=0, name="right_update",
     )
     far = run(
@@ -397,7 +398,7 @@
     )
     other_near, other_far = across_cores(near), across_cores(far)
     scratch = [
-        pltpu.VMEM((packed, LANES), F32), pltpu.VMEM(operators.shape[1:], F32), pltpu.SemaphoreType.DMA((2,)),
+        pltpu.VMEM((packed, LANES), F32), pltpu.VMEM(operators.shape[1:], F32), pltpu.SemaphoreType.DMA((BLOCKS,)),
     ]
     half_done = run(
         functools.partial(operator_kernel, own=True), shaped(operators.shape), [], operators, column, near, far,

time: 57.6 us -> 57.5 us (level)
  no operation moved by 1% of the time
where the time goes in v5:
time: 57.5 us; the launch traced here: 57.3 us
  starting transfers between devices  24.8 us (43%)
  Pallas kernels  13.9 us (24%)
  waiting for transfers between devices  13 us (23%)
  local copies, waits for them, and re-layouts  4.16 us (7%)
  between operations  1.44 us (3%)
    pallas_call x15, Pallas kernels, run(): pl.pallas_call(kernel, out_shape=out_shape, in_specs=specs, out_specs=out...  13.9 us
    ppermute x10, starting transfers between devices, swap(): return lax.ppermute(value, axis, [(i, i ^ bit) for i in range(count)])  10.6 us
    ppermute x8, starting transfers between devices, across_direct(): lax.ppermute(value, 'lhs', [(i, i ^ 2 * direct[spot if i % 2 == 0 else -s...  8.16 us
    ppermute x10, waiting for transfers between devices, swap(): return lax.ppermute(value, axis, [(i, i ^ bit) for i in range(count)])  6.65 us
    ppermute x4, starting transfers between devices, around(): lax.ppermute(value, axis, [(i, (i + steps) % count) for i in range(count)])  5.98 us
    ppermute x4, waiting for transfers between devices, around(): lax.ppermute(value, axis, [(i, (i + steps) % count) for i in range(count)])  5.19 us
    unnamed x14, local copies, waits for them, and re-layouts  4.16 us
  transfers between devices with their start and end apart: 22, of which 11 were waited for; matrix products, arithmetic and copies ran while one was open for 0% of the time, Pallas kernels for 18%

profile of v5, /device:TPU:0, one launch (start us, length us, event | category | flops | bytes accessed | tf_op | source)
XLA Modules:
  0.0 57.3 jit_solution(16843148944340517212)
XLA Ops:
  0.6 0.0 copy-start.6
  0.6 0.5 collective-permute-start.3
  1.1 2.6 %collective-permute-start.1 = (f32[400,384]{1,0:T(8,128)}, f32[400,384]{1,0:T(8,128)S(1)}, u32[]{:S(2)}, u32[]{:S(2)}) collective-permute-start(f32[400,384]{1,0:T(8,128)} %bitcast.30), channel_id=1, source_target_pairs={{0,1},{1,2},{2,3},{3,0},{4,5},{5,6},{6,7},{7,4},{8,9},{9,10},{10,1... | collective-permute-start | bytes 1843208 | tf_op jit(solution)/shard_map/ppermute | solution.py:277
  3.8 1.3 %collective-permute-start.2 = (f32[1,384]{1,0:T(1,128)}, f32[1,384]{1,0:T(1,128)S(1)}, u32[]{:S(2)}, u32[]{:S(2)}) collective-permute-start(f32[1,384]{1,0:T(1,128)} %bitcast.32), channel_id=1, source_target_pairs={{0,4},{4,8},{8,12},{12,16},{16,20},{20,24},{24,28},{28,0},{1,5},{5... | collective-permute-start | bytes 4616 | tf_op jit(solution)/shard_map/ppermute | solution.py:277
  5.0 1.6 %collective-permute-start = (f32[1,384]{1,0:T(1,128)}, f32[1,384]{1,0:T(1,128)S(1)}, u32[]{:S(2)}, u32[]{:S(2)}) collective-permute-start(f32[1,384]{1,0:T(1,128)} %bitcast.33), channel_id=1, source_target_pairs={{0,1},{1,2},{2,3},{3,0},{4,5},{5,6},{6,7},{7,4},{8,9},{9,10},{10,1... | collective-permute-start | bytes 4616 | tf_op jit(solution)/shard_map/ppermute | solution.py:277
  7.3 0.0 copy-start
  7.3 1.4 %copy-done = f32[2,400,400]{2,1,0:T(8,128)S(1)} copy-done((f32[2,400,400]{2,1,0:T(8,128)S(1)}, f32[2,400,400]{2,1,0:T(8,128)}, u32[]{:S(2)}) %copy-start) | copy-done | bytes 1280024
  8.7 0.0 copy-start.2
  8.7 0.7 %copy-done.2 = f32[2,400]{1,0:T(2,128)S(1)} copy-done((f32[2,400]{1,0:T(2,128)S(1)}, f32[2,400]{1,0:T(2,128)}, u32[]{:S(2)}) %copy-start.2) | copy-done | bytes 3224
  9.4 0.7 %copy-done.3 = s32[1,1,384]{2,1,0:T(1,128)S(1)} copy-done((s32[1,1,384]{2,1,0:T(1,128)S(1)}, s32[1,1,384]{2,1,0:T(1,128)}, u32[]{:S(2)}) %copy-start.3) | copy-done | bytes 1560
  10.1 0.7 %copy-done.4 = s32[1,1,384]{2,1,0:T(1,128)S(1)} copy-done((s32[1,1,384]{2,1,0:T(1,128)S(1)}, s32[1,1,384]{2,1,0:T(1,128)}, u32[]{:S(2)}) %copy-start.4) | copy-done | bytes 1560
  10.8 0.7 %copy-done.5 = s32[1,1,384]{2,1,0:T(1,128)S(1)} copy-done((s32[1,1,384]{2,1,0:T(1,128)S(1)}, s32[1,1,384]{2,1,0:T(1,128)}, u32[]{:S(2)}) %copy-start.5) | copy-done | bytes 1560
  11.4 0.8 %prepare.1 = (bf16[384,384]{1,0:T(8,128)(2,1)S(1)}, f32[384,384]{1,0:T(8,128)S(1)}, f32[384,384]{1,0:T(8,128)S(1)}, f32[384,1]{1,0:T(8,128)S(1)}, f32[2,400,1]{2...) custom-call(s32[1,1]{1,0:T(1,128)S(6)} %copy.16.count, s32[1,384]{1,0:T(1,128)S(1)} %bitcast.22, ...), custom_call_target="tpu_custom_call" | custom-call | bytes 1048576 | tf_op jit(solution)/shard_map/prepare/pallas_call | solution.py:262
  12.3 0.0 collective-permute-done.2.after.left_sum
  12.3 0.0 collective-permute-done.3.left
  12.3 0.0 copy-done.6
  12.3 2.4 %left_side.1 = (bf16[400,384]{1,0:T(8,128)(2,1)S(1)}, bf16[400,384]{1,0:T(8,128)(2,1)S(1)}, f32[400,384]{1,0:T(8,128)S(1)}, f32[1,384]{1,0:T(1,128)S(1)}, bf16[384,1200]{1,0:T(8,128)(2,1)S(1)}) custom-call(f32[1,384]{1,0:T(1,128)S(1)} %collective-permute-done.2.after.left_sum, f32[400,384]{1,0:T(8,128)S(1)} %collective-permute-done.3.left, ...), custom_call_target="tpu_custom_call" | custom-call | flops 2000000000 | bytes 1048576 | tf_op jit(solution)/shard_map/left_side/pallas_call | solution.py:262
  14.8 5.2 %collective-permute-done.after.right_sum = f32[1,384]{1,0:T(1,128)S(1)} collective-permute-done((f32[1,384]{1,0:T(1,128)}, f32[1,384]{1,0:T(1,128)S(1)}, u32[]{:S(2)}, u32[]{:S(2)}) %collective-permute-start) | collective-permute-done | bytes 1568 | tf_op jit(solution)/shard_map/ppermute | solution.py:277
  19.9 0.0 collective-permute-done.1.right
  19.9 2.4 %right_side.1 = (f32[1280,128]{1,0:T(8,128)S(1)}, bf16[400,384]{1,0:T(8,128)(2,1)S(1)}, bf16[400,384]{1,0:T(8,128)(2,1)S(1)}, f32[384,384]{1,0:T(8,128)S(1)}) custom-call(f32[1,384]{1,0:T(1,128)S(1)} %collective-permute-done.after.right_sum, f32[400,384]{1,0:T(8,128)S(1)} %collective-permute-done.1.right, f32[400,384]{1,0:T(8,128)S(1)} %get-tuple-element.34.unit, ...), custom_call_target="tpu_custom_call" | custom-call | flops 3000000000 | bytes 1048576 | tf_op jit(solution)/shard_map/right_side/pallas_call | solution.py:262
  22.4 0.7 %collective-permute-start.4 = (f32[1280,128]{1,0:T(8,128)S(1)}, f32[1280,128]{1,0:T(8,128)S(1)}, u32[]{:S(2)}, u32[]{:S(2)}) collective-permute-start(f32[1280,128]{1,0:T(8,128)S(1)} %get-tuple-element.44), channel_id=1, source_target_pairs={{0,4},{4,0},{8,12},{12,8},{16,20},{20,16},{24,28},{28,24},{1,5},{5... | collective-permute-start | bytes 1966088 | tf_op jit(solution)/shard_map/ppermute | solution.py:282
  23.1 0.8 %own_relation.1 = f32[1280,128]{1,0:T(8,128)S(1)} custom-call(s32[1,384]{1,0:T(1,128)S(1)} %bitcast.27, bf16[400,384]{1,0:T(8,128)(2,1)S(1)} %get-tuple-element.42.d_high, bf16[400,384]{1,0:T(8,128)(2,1)S(1)} %get-tuple-element.43.d_low, bf16[400,384]{1,0:T(8,128)(2,1)S(1)} %get-tuple-element.40.x_high, bf16[400,384]{1,0:T(8,128)(2,1)S(1)} %get-tuple-element.41.x_low), custom_call_target="tpu_custom_call" | custom-call | flops 1000000000 | bytes 1048576 | tf_op jit(solution)/shard_map/own_relation/pallas_call | solution.py:262
  23.9 1.0 %collective-permute-done.4 = f32[1280,128]{1,0:T(8,128)S(1)} collective-permute-done((f32[1280,128]{1,0:T(8,128)S(1)}, f32[1280,128]{1,0:T(8,128)S(1)}, u32[]{:S(2)}, u32[]{:S(2)}) %collective-permute-start.4) | collective-permute-done | bytes 655392 | tf_op jit(solution)/shard_map/ppermute | solution.py:282
  24.8 0.1 sum_cores.1
  24.9 0.1 collective-permute-start.7
  25.0 1.8 %collective-permute-start.9 = (f32[160,128]{1,0:T(8,128)S(1)}, f32[160,128]{1,0:T(8,128)S(1)}, u32[]{:S(2)}, u32[]{:S(2)}) collective-permute-start(f32[160,128]{1,0:T(8,128)S(1)} %get-tuple-element.51), channel_id=1, source_target_pairs={{0,8},{4,20},{8,0},{12,28},{16,24},{20,4},{24,16},{28,12},{1,9},{5... | collective-permute-start | bytes 245768 | tf_op jit(solution)/shard_map/ppermute | solution.py:300
  26.7 1.7 %collective-permute-start.10 = (f32[160,128]{1,0:T(8,128)S(1)}, f32[160,128]{1,0:T(8,128)S(1)}, u32[]{:S(2)}, u32[]{:S(2)}) collective-permute-start(f32[160,128]{1,0:T(8,128)S(1)} %get-tuple-element.52), channel_id=1, source_target_pairs={{0,16},{4,12},{8,24},{12,4},{16,0},{20,28},{24,8},{28,20},{1,17},{... | collective-permute-start | bytes 245768 | tf_op jit(solution)/shard_map/ppermute | solution.py:300
  28.4 0.4 collective-permute-start.5
  28.8 0.3 collective-permute-start.6
  29.1 0.6 %collective-permute-done.7.two = f32[1,160,128]{2,1,0:T(8,128)S(1)} collective-permute-done((f32[1,160,128]{2,1,0:T(8,128)S(1)}, f32[1,160,128]{2,1,0:T(8,128)S(1)}, u32[]{:S(2)}, u32[]{:S(2)}) %collective-permute-start.7) | collective-permute-done | bytes 81952 | tf_op jit(solution)/shard_map/ppermute | solution.py:282
  29.7 2.7 %collective-permute-start.8 = (f32[160,128]{1,0:T(8,128)S(1)}, f32[160,128]{1,0:T(8,128)S(1)}, u32[]{:S(2)}, u32[]{:S(2)}) collective-permute-start(f32[160,128]{1,0:T(8,128)S(1)} %merge_layers.1.refs_0_), channel_id=1, source_target_pairs={{0,24},{4,28},{8,16},{12,20},{16,8},{20,12},{24,0},{28,4},{1,25},{... | collective-permute-start | bytes 245768 | tf_op jit(solution)/shard_map/ppermute | solution.py:282
  32.4 0.0 collective-permute-done.9.refs_2_
  32.4 0.0 collective-permute-done.10.refs_3_
  32.4 1.7 %collective-permute-start.11 = (f32[160,128]{1,0:T(8,128)S(1)}, f32[160,128]{1,0:T(8,128)S(1)}, u32[]{:S(2)}, u32[]{:S(2)}) collective-permute-start(f32[160,128]{1,0:T(8,128)S(1)} %sum_away.1), channel_id=1, source_target_pairs={{0,1},{1,0},{2,3},{3,2},{4,5},{5,4},{6,7},{7,6},{8,9},{9,8},{10,11... | collective-permute-start | bytes 245768 | tf_op jit(solution)/shard_map/ppermute | solution.py:282
  34.1 0.0 collective-permute-done.5.refs_1_
  34.1 0.0 collective-permute-done.6.refs_2_
  34.1 1.2 %collective-permute-done.8.refs_3_ = f32[160,128]{1,0:T(8,128)S(1)} collective-permute-done((f32[160,128]{1,0:T(8,128)S(1)}, f32[160,128]{1,0:T(8,128)S(1)}, u32[]{:S(2)}, u32[]{:S(2)}) %collective-permute-start.8) | collective-permute-done | bytes 81952 | tf_op jit(solution)/shard_map/ppermute | solution.py:282
  35.3 1.6 %collective-permute-done.11.refs_4_ = f32[160,128]{1,0:T(8,128)S(1)} collective-permute-done((f32[160,128]{1,0:T(8,128)S(1)}, f32[160,128]{1,0:T(8,128)S(1)}, u32[]{:S(2)}, u32[]{:S(2)}) %collective-permute-start.11) | collective-permute-done | bytes 81952 | tf_op jit(solution)/shard_map/ppermute | solution.py:282
  36.9 2.0 %collective-permute-start.12 = (f32[160,128]{1,0:T(8,128)S(1)}, f32[160,128]{1,0:T(8,128)S(1)}, u32[]{:S(2)}, u32[]{:S(2)}) collective-permute-start(f32[160,128]{1,0:T(8,128)S(1)} %sum_home.1.after.refs_1_), channel_id=1, source_target_pairs={{0,2},{1,3},{2,0},{3,1},{4,6},{5,7},{6,4},{7,5},{8,10},{9,11},{10,... | collective-permute-start | bytes 245768 | tf_op jit(solution)/shard_map/ppermute | solution.py:282
  38.9 2.8 %left_update.1 = (f32[400,384]{1,0:T(8,128)}, f32[8,128]{1,0:T(8,128)S(1)}) custom-call(f32[160,128]{1,0:T(8,128)S(1)} %sum_home.1.after.refs_1_, f32[400,384]{1,0:T(8,128)S(1)} %collective-permute-done.3.left, f32[1,384]{1,0:T(1,128)S(1)} %collective-permute-done.2.after.left_sum, bf16[2,400,400]{2,1,0:T(8,128)(2,1)S(1)} %get-tuple-element.31.ops_high, ...), custom_call_target="tpu_custom_call" | custom-call | flops 2000000000 | bytes 1048576 | tf_op jit(solution)/shard_map/left_update/pallas_call | solution.py:262
  41.8 0.6 %collective-permute-done.12.refs_2_ = f32[160,128]{1,0:T(8,128)S(1)} collective-permute-done((f32[160,128]{1,0:T(8,128)S(1)}, f32[160,128]{1,0:T(8,128)S(1)}, u32[]{:S(2)}, u32[]{:S(2)}) %collective-permute-start.12) | collective-permute-done | bytes 81952 | tf_op jit(solution)/shard_map/ppermute | solution.py:282
  42.4 0.0 copy-start.1
  42.4 2.0 %collective-permute-start.17 = (f32[160,128]{1,0:T(8,128)S(1)}, f32[160,128]{1,0:T(8,128)S(1)}, u32[]{:S(2)}, u32[]{:S(2)}) collective-permute-start(f32[160,128]{1,0:T(8,128)S(1)} %sum_layers.1.refs_0_), channel_id=1, source_target_pairs={{0,1},{1,0},{2,3},{3,2},{4,5},{5,4},{6,7},{7,6},{8,9},{9,8},{10,11... | collective-permute-start | bytes 245768 | tf_op jit(solution)/shard_map/ppermute | solution.py:282
  44.4 0.8 %collective-permute-start.15 = (f32[160,128]{1,0:T(8,128)S(1)}, f32[160,128]{1,0:T(8,128)S(1)}, u32[]{:S(2)}, u32[]{:S(2)}) collective-permute-start(f32[160,128]{1,0:T(8,128)S(1)} %sum_layers.1.refs_0_), channel_id=1, source_target_pairs={{0,24},{4,28},{8,16},{12,20},{16,8},{20,12},{24,0},{28,4},{1,25},{... | collective-permute-start | bytes 245768 | tf_op jit(solution)/shard_map/ppermute | solution.py:282
  45.2 0.8 %collective-permute-start.14 = (f32[160,128]{1,0:T(8,128)S(1)}, f32[160,128]{1,0:T(8,128)S(1)}, u32[]{:S(2)}, u32[]{:S(2)}) collective-permute-start(f32[160,128]{1,0:T(8,128)S(1)} %sum_layers.1.refs_0_), channel_id=1, source_target_pairs={{0,16},{4,12},{8,24},{12,4},{16,0},{20,28},{24,8},{28,20},{1,17},{... | collective-permute-start | bytes 245768 | tf_op jit(solution)/shard_map/ppermute | solution.py:300
  45.9 1.9 %collective-permute-start.13 = (f32[160,128]{1,0:T(8,128)S(1)}, f32[160,128]{1,0:T(8,128)S(1)}, u32[]{:S(2)}, u32[]{:S(2)}) collective-permute-start(f32[160,128]{1,0:T(8,128)S(1)} %sum_layers.1.refs_0_), channel_id=1, source_target_pairs={{0,8},{4,20},{8,0},{12,28},{16,24},{20,4},{24,16},{28,12},{1,9},{5... | collective-permute-start | bytes 245768 | tf_op jit(solution)/shard_map/ppermute | solution.py:300
  47.9 0.0 collective-permute-done.17.refs_1_
  47.9 1.1 %collective-permute-start.19 = (f32[160,128]{1,0:T(8,128)S(1)}, f32[160,128]{1,0:T(8,128)S(1)}, u32[]{:S(2)}, u32[]{:S(2)}) collective-permute-start(f32[160,128]{1,0:T(8,128)S(1)} %collective-permute-done.17.refs_1_), channel_id=1, source_target_pairs={{0,16},{4,12},{8,24},{12,4},{16,0},{20,28},{24,8},{28,20},{1,17},{... | collective-permute-start | bytes 245768 | tf_op jit(solution)/shard_map/ppermute | solution.py:300
  49.0 0.3 collective-permute-start.18
  49.2 0.6 %collective-permute-done.15.refs_3_ = f32[160,128]{1,0:T(8,128)S(1)} collective-permute-done((f32[160,128]{1,0:T(8,128)S(1)}, f32[160,128]{1,0:T(8,128)S(1)}, u32[]{:S(2)}, u32[]{:S(2)}) %collective-permute-start.15) | collective-permute-done | bytes 81952 | tf_op jit(solution)/shard_map/ppermute | solution.py:282
  49.8 0.5 collective-permute-start.20
  50.3 0.1 collective-permute-done.14.refs_2_
  50.5 0.0 collective-permute-done.13.refs_1_
  50.5 0.1 collective-permute-start.16
  50.6 1.8 %right_update.1 = (f32[400,384]{1,0:T(8,128)}, f32[8,128]{1,0:T(8,128)S(1)}) custom-call(f32[4,160,128]{2,1,0:T(8,128)S(1)} %join_near.1.after.near, f32[400,384]{1,0:T(8,128)S(1)} %collective-permute-done.1.right, f32[1,384]{1,0:T(1,128)S(1)} %collective-permute-done.after.right_sum, f32[400,384]{1,0:T(8,128)S(1)} %get-tuple-element.34.unit, ...), custom_call_target="tpu_custom_call" | custom-call | tf_op jit(solution)/shard_map/right_update/pallas_call | solution.py:262
  52.4 0.0 collective-permute-done.19.refs_3_
  52.4 1.0 %collective-permute-done.18.refs_2_ = f32[160,128]{1,0:T(8,128)S(1)} collective-permute-done((f32[160,128]{1,0:T(8,128)S(1)}, f32[160,128]{1,0:T(8,128)S(1)}, u32[]{:S(2)}, u32[]{:S(2)}) %collective-permute-start.18) | collective-permute-done | bytes 81952 | tf_op jit(solution)/shard_map/ppermute | solution.py:300
  53.4 0.9 %collective-permute-done.20.refs_4_ = f32[160,128]{1,0:T(8,128)S(1)} collective-permute-done((f32[160,128]{1,0:T(8,128)S(1)}, f32[160,128]{1,0:T(8,128)S(1)}, u32[]{:S(2)}, u32[]{:S(2)}) %collective-permute-start.20) | collective-permute-done | bytes 81952 | tf_op jit(solution)/shard_map/ppermute | solution.py:282
  54.3 0.1 collective-permute-start.21
  54.4 0.0 copy-done.1
  54.4 1.3 %own_operator.1.refs_0_ = f32[2,400,400]{2,1,0:T(8,128)} custom-call(f32[2,400,400]{2,1,0:T(8,128)S(1)} %copy-done.1, f32[2,400,1]{2,1,0:T(8,128)S(1)} %get-tuple-element.57.sums, f32[4,160,128]{2,1,0:T(8,128)S(1)} %join_near.1.after.near, f32[4,160,128]{2,1,0:T(8,128)S(1)} %join_far.1.far), custom_call_target="tpu_custom_call" | custom-call | bytes 1048576 | tf_op jit(solution)/shard_map/own_operator/pallas_call | solution.py:262
  55.7 0.0 collective-permute-done.16.near
  55.7 0.3 collective-permute-done.21.far
  56.0 1.3 %operator_update.1 = f32[2,400,400]{2,1,0:T(8,128)} custom-call(f32[2,400,400]{2,1,0:T(8,128)S(1)} %copy-done.1, f32[2,400,1]{2,1,0:T(8,128)S(1)} %get-tuple-element.57.sums, f32[4,160,128]{2,1,0:T(8,128)S(1)} %collective-permute-done.16.near, f32[4,160,128]{2,1,0:T(8,128)S(1)} %collective-permute-done.21.far, ...), custom_call_target="tpu_custom_call", output_to_operand_aliasing={{}: (4, {})} | custom-call | bytes 1048576 | tf_op jit(solution)/shard_map/operator_update/pallas_call | solution.py:262
  (9 shorter events, 0.1 us)
Async XLA Ops:
  0.6 11.7 %copy-start.6 = (s32[1,1,384]{2,1,0:T(1,128)S(1)}, s32[1,1,384]{2,1,0:T(1,128)}, u32[]{:S(2)}) copy-start(s32[1,1,384]{2,1,0:T(1,128)} %param.19) | copy-start | bytes 4612
  0.6 11.7 %collective-permute-start.3 = (f32[400,384]{1,0:T(8,128)}, f32[400,384]{1,0:T(8,128)S(1)}, u32[]{:S(2)}, u32[]{:S(2)}) collective-permute-start(f32[400,384]{1,0:T(8,128)} %bitcast.29), channel_id=1, source_target_pairs={{0,4},{4,8},{8,12},{12,16},{16,20},{20,24},{24,28},{28,0},{1,5},{5... | collective-permute-start | bytes 1843208 | tf_op jit(solution)/shard_map/ppermute | solution.py:277
  1.1 18.8 %collective-permute-start.1 = (f32[400,384]{1,0:T(8,128)}, f32[400,384]{1,0:T(8,128)S(1)}, u32[]{:S(2)}, u32[]{:S(2)}) collective-permute-start(f32[400,384]{1,0:T(8,128)} %bitcast.30), channel_id=1, source_target_pairs={{0,1},{1,2},{2,3},{3,0},{4,5},{5,6},{6,7},{7,4},{8,9},{9,10},{10,1... | collective-permute-start | bytes 1843208 | tf_op jit(solution)/shard_map/ppermute | solution.py:277
  3.8 8.5 %collective-permute-start.2 = (f32[1,384]{1,0:T(1,128)}, f32[1,384]{1,0:T(1,128)S(1)}, u32[]{:S(2)}, u32[]{:S(2)}) collective-permute-start(f32[1,384]{1,0:T(1,128)} %bitcast.32), channel_id=1, source_target_pairs={{0,4},{4,8},{8,12},{12,16},{16,20},{20,24},{24,28},{28,0},{1,5},{5... | collective-permute-start | bytes 4616 | tf_op jit(solution)/shard_map/ppermute | solution.py:277
  5.0 14.9 %collective-permute-start = (f32[1,384]{1,0:T(1,128)}, f32[1,384]{1,0:T(1,128)S(1)}, u32[]{:S(2)}, u32[]{:S(2)}) collective-permute-start(f32[1,384]{1,0:T(1,128)} %bitcast.33), channel_id=1, source_target_pairs={{0,1},{1,2},{2,3},{3,0},{4,5},{5,6},{6,7},{7,4},{8,9},{9,10},{10,1... | collective-permute-start | bytes 4616 | tf_op jit(solution)/shard_map/ppermute | solution.py:277
  7.3 1.4 %copy-start = (f32[2,400,400]{2,1,0:T(8,128)S(1)}, f32[2,400,400]{2,1,0:T(8,128)}, u32[]{:S(2)}) copy-start(f32[2,400,400]{2,1,0:T(8,128)} %ops.5) | copy-start | bytes 3840004
  8.7 0.7 %copy-start.2 = (f32[2,400]{1,0:T(2,128)S(1)}, f32[2,400]{1,0:T(2,128)}, u32[]{:S(2)}) copy-start(f32[2,400]{1,0:T(2,128)} %op_sums.1) | copy-start | bytes 9604
  9.4 0.7 %copy-start.3 = (s32[1,1,384]{2,1,0:T(1,128)S(1)}, s32[1,1,384]{2,1,0:T(1,128)}, u32[]{:S(2)}) copy-start(s32[1,1,384]{2,1,0:T(1,128)} %param.17) | copy-start | bytes 4612
  10.1 0.7 %copy-start.4 = (s32[1,1,384]{2,1,0:T(1,128)S(1)}, s32[1,1,384]{2,1,0:T(1,128)}, u32[]{:S(2)}) copy-start(s32[1,1,384]{2,1,0:T(1,128)} %param.18) | copy-start | bytes 4612
  10.8 0.7 %copy-start.5 = (s32[1,1,384]{2,1,0:T(1,128)S(1)}, s32[1,1,384]{2,1,0:T(1,128)}, u32[]{:S(2)}) copy-start(s32[1,1,384]{2,1,0:T(1,128)} %param.20) | copy-start | bytes 4612
  22.4 2.4 %collective-permute-start.4 = (f32[1280,128]{1,0:T(8,128)S(1)}, f32[1280,128]{1,0:T(8,128)S(1)}, u32[]{:S(2)}, u32[]{:S(2)}) collective-permute-start(f32[1280,128]{1,0:T(8,128)S(1)} %get-tuple-element.44), channel_id=1, source_target_pairs={{0,4},{4,0},{8,12},{12,8},{16,20},{20,16},{24,28},{28,24},{1,5},{5... | collective-permute-start | bytes 1966088 | tf_op jit(solution)/shard_map/ppermute | solution.py:282
  24.9 4.8 %collective-permute-start.7 = (f32[1,160,128]{2,1,0:T(8,128)S(1)}, f32[1,160,128]{2,1,0:T(8,128)S(1)}, u32[]{:S(2)}, u32[]{:S(2)}) collective-permute-start(f32[1,160,128]{2,1,0:T(8,128)S(1)} %get-tuple-element.49), channel_id=1, source_target_pairs={{0,1},{1,0},{2,3},{3,2},{4,5},{5,4},{6,7},{7,6},{8,9},{9,8},{10,11... | collective-permute-start | bytes 245768 | tf_op jit(solution)/shard_map/ppermute | solution.py:282
  25.0 7.4 %collective-permute-start.9 = (f32[160,128]{1,0:T(8,128)S(1)}, f32[160,128]{1,0:T(8,128)S(1)}, u32[]{:S(2)}, u32[]{:S(2)}) collective-permute-start(f32[160,128]{1,0:T(8,128)S(1)} %get-tuple-element.51), channel_id=1, source_target_pairs={{0,8},{4,20},{8,0},{12,28},{16,24},{20,4},{24,16},{28,12},{1,9},{5... | collective-permute-start | bytes 245768 | tf_op jit(solution)/shard_map/ppermute | solution.py:300
  26.7 5.6 %collective-permute-start.10 = (f32[160,128]{1,0:T(8,128)S(1)}, f32[160,128]{1,0:T(8,128)S(1)}, u32[]{:S(2)}, u32[]{:S(2)}) collective-permute-start(f32[160,128]{1,0:T(8,128)S(1)} %get-tuple-element.52), channel_id=1, source_target_pairs={{0,16},{4,12},{8,24},{12,4},{16,0},{20,28},{24,8},{28,20},{1,17},{... | collective-permute-start | bytes 245768 | tf_op jit(solution)/shard_map/ppermute | solution.py:300
  28.4 5.7 %collective-permute-start.5 = (f32[160,128]{1,0:T(8,128)S(1)}, f32[160,128]{1,0:T(8,128)S(1)}, u32[]{:S(2)}, u32[]{:S(2)}) collective-permute-start(f32[160,128]{1,0:T(8,128)S(1)} %get-tuple-element.46), channel_id=1, source_target_pairs={{0,8},{4,20},{8,0},{12,28},{16,24},{20,4},{24,16},{28,12},{1,9},{5... | collective-permute-start | bytes 245768 | tf_op jit(solution)/shard_map/ppermute | solution.py:300
  28.8 5.3 %collective-permute-start.6 = (f32[160,128]{1,0:T(8,128)S(1)}, f32[160,128]{1,0:T(8,128)S(1)}, u32[]{:S(2)}, u32[]{:S(2)}) collective-permute-start(f32[160,128]{1,0:T(8,128)S(1)} %get-tuple-element.47), channel_id=1, source_target_pairs={{0,16},{4,12},{8,24},{12,4},{16,0},{20,28},{24,8},{28,20},{1,17},{... | collective-permute-start | bytes 245768 | tf_op jit(solution)/shard_map/ppermute | solution.py:300
  29.7 5.6 %collective-permute-start.8 = (f32[160,128]{1,0:T(8,128)S(1)}, f32[160,128]{1,0:T(8,128)S(1)}, u32[]{:S(2)}, u32[]{:S(2)}) collective-permute-start(f32[160,128]{1,0:T(8,128)S(1)} %merge_layers.1.refs_0_), channel_id=1, source_target_pairs={{0,24},{4,28},{8,16},{12,20},{16,8},{20,12},{24,0},{28,4},{1,25},{... | collective-permute-start | bytes 245768 | tf_op jit(solution)/shard_map/ppermute | solution.py:282
  32.4 4.5 %collective-permute-start.11 = (f32[160,128]{1,0:T(8,128)S(1)}, f32[160,128]{1,0:T(8,128)S(1)}, u32[]{:S(2)}, u32[]{:S(2)}) collective-permute-start(f32[160,128]{1,0:T(8,128)S(1)} %sum_away.1), channel_id=1, source_target_pairs={{0,1},{1,0},{2,3},{3,2},{4,5},{5,4},{6,7},{7,6},{8,9},{9,8},{10,11... | collective-permute-start | bytes 245768 | tf_op jit(solution)/shard_map/ppermute | solution.py:282
  36.9 5.4 %collective-permute-start.12 = (f32[160,128]{1,0:T(8,128)S(1)}, f32[160,128]{1,0:T(8,128)S(1)}, u32[]{:S(2)}, u32[]{:S(2)}) collective-permute-start(f32[160,128]{1,0:T(8,128)S(1)} %sum_home.1.after.refs_1_), channel_id=1, source_target_pairs={{0,2},{1,3},{2,0},{3,1},{4,6},{5,7},{6,4},{7,5},{8,10},{9,11},{10,... | collective-permute-start | bytes 245768 | tf_op jit(solution)/shard_map/ppermute | solution.py:282
  42.4 12.0 %copy-start.1 = (f32[2,400,400]{2,1,0:T(8,128)S(1)}, f32[2,400,400]{2,1,0:T(8,128)}, u32[]{:S(2)}) copy-start(f32[2,400,400]{2,1,0:T(8,128)} %ops.5) | copy-start | bytes 3840004
  42.4 5.5 %collective-permute-start.17 = (f32[160,128]{1,0:T(8,128)S(1)}, f32[160,128]{1,0:T(8,128)S(1)}, u32[]{:S(2)}, u32[]{:S(2)}) collective-permute-start(f32[160,128]{1,0:T(8,128)S(1)} %sum_layers.1.refs_0_), channel_id=1, source_target_pairs={{0,1},{1,0},{2,3},{3,2},{4,5},{5,4},{6,7},{7,6},{8,9},{9,8},{10,11... | collective-permute-start | bytes 245768 | tf_op jit(solution)/shard_map/ppermute | solution.py:282
  44.4 5.4 %collective-permute-start.15 = (f32[160,128]{1,0:T(8,128)S(1)}, f32[160,128]{1,0:T(8,128)S(1)}, u32[]{:S(2)}, u32[]{:S(2)}) collective-permute-start(f32[160,128]{1,0:T(8,128)S(1)} %sum_layers.1.refs_0_), channel_id=1, source_target_pairs={{0,24},{4,28},{8,16},{12,20},{16,8},{20,12},{24,0},{28,4},{1,25},{... | collective-permute-start | bytes 245768 | tf_op jit(solution)/shard_map/ppermute | solution.py:282
  45.2 5.3 %collective-permute-start.14 = (f32[160,128]{1,0:T(8,128)S(1)}, f32[160,128]{1,0:T(8,128)S(1)}, u32[]{:S(2)}, u32[]{:S(2)}) collective-permute-start(f32[160,128]{1,0:T(8,128)S(1)} %sum_layers.1.refs_0_), channel_id=1, source_target_pairs={{0,16},{4,12},{8,24},{12,4},{16,0},{20,28},{24,8},{28,20},{1,17},{... | collective-permute-start | bytes 245768 | tf_op jit(solution)/shard_map/ppermute | solution.py:300
  45.9 4.6 %collective-permute-start.13 = (f32[160,128]{1,0:T(8,128)S(1)}, f32[160,128]{1,0:T(8,128)S(1)}, u32[]{:S(2)}, u32[]{:S(2)}) collective-permute-start(f32[160,128]{1,0:T(8,128)S(1)} %sum_layers.1.refs_0_), channel_id=1, source_target_pairs={{0,8},{4,20},{8,0},{12,28},{16,24},{20,4},{24,16},{28,12},{1,9},{5... | collective-permute-start | bytes 245768 | tf_op jit(solution)/shard_map/ppermute | solution.py:300
  47.9 4.6 %collective-permute-start.19 = (f32[160,128]{1,0:T(8,128)S(1)}, f32[160,128]{1,0:T(8,128)S(1)}, u32[]{:S(2)}, u32[]{:S(2)}) collective-permute-start(f32[160,128]{1,0:T(8,128)S(1)} %collective-permute-done.17.refs_1_), channel_id=1, source_target_pairs={{0,16},{4,12},{8,24},{12,4},{16,0},{20,28},{24,8},{28,20},{1,17},{... | collective-permute-start | bytes 245768 | tf_op jit(solution)/shard_map/ppermute | solution.py:300
  49.0 4.4 %collective-permute-start.18 = (f32[160,128]{1,0:T(8,128)S(1)}, f32[160,128]{1,0:T(8,128)S(1)}, u32[]{:S(2)}, u32[]{:S(2)}) collective-permute-start(f32[160,128]{1,0:T(8,128)S(1)} %collective-permute-done.17.refs_1_), channel_id=1, source_target_pairs={{0,8},{4,20},{8,0},{12,28},{16,24},{20,4},{24,16},{28,12},{1,9},{5... | collective-permute-start | bytes 245768 | tf_op jit(solution)/shard_map/ppermute | solution.py:300
  49.8 4.4 %collective-permute-start.20 = (f32[160,128]{1,0:T(8,128)S(1)}, f32[160,128]{1,0:T(8,128)S(1)}, u32[]{:S(2)}, u32[]{:S(2)}) collective-permute-start(f32[160,128]{1,0:T(8,128)S(1)} %collective-permute-done.15.refs_3_), channel_id=1, source_target_pairs={{0,1},{1,0},{2,3},{3,2},{4,5},{5,4},{6,7},{7,6},{8,9},{9,8},{10,11... | collective-permute-start | bytes 245768 | tf_op jit(solution)/shard_map/ppermute | solution.py:282
  50.5 5.2 %collective-permute-start.16 = (f32[4,160,128]{2,1,0:T(8,128)S(1)}, f32[4,160,128]{2,1,0:T(8,128)S(1)}, u32[]{:S(2)}, u32[]{:S(2)}) collective-permute-start(f32[4,160,128]{2,1,0:T(8,128)S(1)} %join_near.1.after.near), channel_id=1, source_target_pairs={{0,4},{4,0},{8,12},{12,8},{16,20},{20,16},{24,28},{28,24},{1,5},{5... | collective-permute-start | bytes 983048 | tf_op jit(solution)/shard_map/ppermute | solution.py:282
  54.3 1.7 %collective-permute-start.21 = (f32[4,160,128]{2,1,0:T(8,128)S(1)}, f32[4,160,128]{2,1,0:T(8,128)S(1)}, u32[]{:S(2)}, u32[]{:S(2)}) collective-permute-start(f32[4,160,128]{2,1,0:T(8,128)S(1)} %join_far.1.far), channel_id=1, source_target_pairs={{0,4},{4,0},{8,12},{12,8},{16,20},{20,16},{24,28},{28,24},{1,5},{5... | collective-permute-start | bytes 983048 | tf_op jit(solution)/shard_map/ppermute | solution.py:282
